TPU v7x, 128 devices: a whole 4x4x4 slice. The times are simulated.
128 devices in a mesh: side: 2 (over core), dev: 64 (over y, x, z).
Axes of the slice: x: 4, y: 4, z: 4, core: 2. Of those that a mesh axis runs over, the one named last changes fastest.
Arguments:
- out_gates: bfloat16 [2048, 2048], P('dev'), may hold values from -6 to 6
- queries: bfloat16 [2048, 2048], P('dev'), may hold values from -6 to 6
- keys_new: bfloat16 [2048, 256], P('dev'), may hold values from -6 to 6
- values_new: bfloat16 [2048, 256], P('dev'), may hold values from -6 to 6
- lengths: int32 [2048], P('dev'), may hold values from 1 to 128, as said below
- page_table: int32 [2048, 8], P('dev'), may hold values from 0 to 143, as said below
- cache_pool: bfloat16 [9216, 16, 512], P('dev'), may hold values from -1 to 1
- query_gain: float32 [256], replicated, may hold values from 0.25 to 1.75
- key_gain: float32 [256], replicated, may hold values from 0.25 to 1.75
- out_weight: bfloat16 [2048, 2048], replicated, may hold values from -0.125 to 0.125
- residual: bfloat16 [2048, 2048], P('dev'), may hold values from -0.625 to 0.625
- post_gain: float32 [2048], replicated, may hold values from 0.25 to 1.75
- experts: int32 [2048, 10], P('dev'), may hold values from 0 to 255, all different within a row; in each aligned block of 32 rows (0 to 31, 32 to 63, ...) at most 2 rows name the same one
- route_weights: float32 [2048, 10], P('dev'), may hold values from 0.05 to 1
- gate_weight: bfloat16 [256, 2048, 256], P('dev'), may hold values from -0.125 to 0.125
- up_weight: bfloat16 [256, 2048, 256], P('dev'), may hold values from -0.125 to 0.125
- down_weight: bfloat16 [256, 256, 2048], P('dev'), may hold values from -0.375 to 0.375
- shared_gate: bfloat16 [2048, 256], replicated, may hold values from -0.125 to 0.125
- shared_up: bfloat16 [2048, 256], replicated, may hold values from -0.125 to 0.125
- shared_down: bfloat16 [256, 2048], replicated, may hold values from -0.375 to 0.375
- shared_mix: bfloat16 [2048], replicated, may hold values from -0.125 to 0.125
Outputs:
- layer_out: bfloat16 [2048, 2048], P('dev', 'side')
Inputs may be any that keep to these rules, and one draw needn't show every extreme that they name: Each row names 10 different experts; the rows of one device (aligned blocks of 32 rows) name one expert at most 2 times. A row's cache fills its first ceil(lengths / 16) page-table entries; in every device some row holds 128 tokens. `page_table`: indices are local to the row's device. The used entries of one device's rows name each of its 144 pages exactly once; unused entries name arbitrary pages.
All inputs are finite; a program needn't handle non-finite values.
Results may differ from a plain program's by a relative error of at most 0.024.
Values may be sent and summed in bfloat16 or wider, within the bound.
No kernel may reach another device: no remote copies, remote signals or barrier semaphores. Data moves between devices by JAX's collectives and lax.ppermute only.
A program may use at most 128 MiB of HBM per device.

v0:
```python
import jax
import jax.numpy as jnp
from jax import lax
from jax.sharding import PartitionSpec as P

eps = 1e-06


def from_behind(value, axis, steps):
    count = lax.axis_size(axis)
    first, last = (max(0, -steps), min(count, count - steps))
    return lax.ppermute(value, axis, [(source, source + steps) for source in range(first, last)])


def rms_scale(values, gain):
    wide = values.astype(jnp.float32)
    return wide * lax.rsqrt(jnp.mean(wide * wide, axis=-1, keepdims=True) + eps) * gain


def attend(
    gates_in, queries_in, keys_in, values_in, lengths_in, table_in, cache_pool, query_gain, key_gain
):
    rows = queries_in.shape[0]
    head_dim = keys_in.shape[1]
    heads = queries_in.shape[1] // head_dim
    scale = head_dim ** (-0.5)
    query_normed = rms_scale(queries_in.reshape(rows, heads, head_dim), query_gain).astype(
        jnp.bfloat16
    )
    key_normed = rms_scale(keys_in, key_gain).astype(jnp.bfloat16)
    pages = cache_pool[table_in]
    context = pages.shape[1] * pages.shape[2]
    pages = pages.reshape(rows, context, 2 * head_dim)
    cached_keys = pages[:, :, :head_dim]
    cached_values = pages[:, :, head_dim:]
    scores = (
        jnp.einsum("rhd,rtd->rht", query_normed, cached_keys, preferred_element_type=jnp.float32)
        * scale
    )
    own = (
        jnp.einsum("rhd,rd->rh", query_normed, key_normed, preferred_element_type=jnp.float32)
        * scale
    )
    valid = jnp.arange(context, dtype=jnp.int32)[None, None, :] < lengths_in[:, None, None]
    weights = jnp.where(valid, jnp.exp(scores), 0.0)
    own_weight = jnp.exp(own)
    total = jnp.sum(weights, axis=2) + own_weight
    probs = (weights / total[:, :, None]).astype(jnp.bfloat16)
    own_prob = (own_weight / total).astype(jnp.bfloat16)
    mixed = jnp.einsum("rht,rtd->rhd", probs, cached_values, preferred_element_type=jnp.float32)
    mixed = (
        mixed + own_prob.astype(jnp.float32)[:, :, None] * values_in.astype(jnp.float32)[:, None, :]
    )
    gated = mixed * jax.nn.sigmoid(gates_in.reshape(rows, heads, head_dim).astype(jnp.float32))
    return gated.reshape(rows, heads * head_dim).astype(jnp.bfloat16)


def slot_index(chosen, experts_all, local_experts, capacity):
    flat = chosen.reshape(-1)
    onehot = (flat[:, None] == jnp.arange(experts_all, dtype=jnp.int32)[None, :]).astype(jnp.int32)
    rank = jnp.sum((jnp.cumsum(onehot, axis=0) - 1) * onehot, axis=1)
    owner = flat // local_experts
    return owner * (capacity * local_experts) + rank * local_experts + flat % local_experts


def pack_rows(normed, slots, n_dev, capacity, local_experts):
    topk = slots.shape[0] // normed.shape[0]
    copies = jnp.repeat(normed, topk, axis=0)
    filled = (
        jnp.zeros((n_dev * capacity * local_experts, normed.shape[1]), jnp.bfloat16)
        .at[slots]
        .set(copies)
    )
    return filled.reshape(n_dev, capacity, local_experts, normed.shape[1])


def serve_rows(received, gate_weight, up_weight, down_weight):
    gate_val = jnp.einsum(
        "scud,udf->scuf", received, gate_weight, preferred_element_type=jnp.float32
    )
    up_val = jnp.einsum("scud,udf->scuf", received, up_weight, preferred_element_type=jnp.float32)
    inner = (jax.nn.silu(gate_val) * up_val).astype(jnp.bfloat16)
    return jnp.einsum(
        "scuf,ufd->scud", inner, down_weight, preferred_element_type=jnp.float32
    ).astype(jnp.bfloat16)


def shared_branch(normed, shared_gate, shared_up, shared_down, shared_mix):
    gate_val = jnp.dot(normed, shared_gate, preferred_element_type=jnp.float32)
    up_val = jnp.dot(normed, shared_up, preferred_element_type=jnp.float32)
    inner = (jax.nn.silu(gate_val) * up_val).astype(jnp.bfloat16)
    result = jnp.dot(inner, shared_down, preferred_element_type=jnp.float32)
    weight = jax.nn.sigmoid(jnp.dot(normed, shared_mix, preferred_element_type=jnp.float32))
    return result * weight[:, None]


def combine(hidden, returned, slots, weights_in, shared_out):
    rows, topk = weights_in.shape
    picked = returned[slots].reshape(rows, topk, returned.shape[1])
    share = weights_in / jnp.sum(weights_in, axis=1, keepdims=True)
    routed = jnp.einsum("rk,rkd->rd", share, picked.astype(jnp.float32))
    return (hidden.astype(jnp.float32) + routed + shared_out).astype(jnp.bfloat16)


def on_device(
    out_gates,
    queries,
    keys_new,
    values_new,
    lengths,
    page_table,
    cache_pool,
    query_gain,
    key_gain,
    out_weight,
    residual,
    post_gain,
    experts,
    route_weights,
    gate_weight,
    up_weight,
    down_weight,
    shared_gate,
    shared_up,
    shared_down,
    shared_mix,
):
    n_dev = lax.axis_size("dev")
    local_experts = gate_weight.shape[0]
    experts_all = local_experts * n_dev
    rows_dev, topk = experts.shape
    capacity = max(2, (3 * rows_dev * topk + 2 * experts_all - 1) // (2 * experts_all))
    width = residual.shape[1]
    side = lax.axis_index("side")
    row_args = (
        out_gates,
        queries,
        keys_new,
        values_new,
        lengths,
        page_table,
        residual,
        experts,
        route_weights,
    )

    def front(picked_rows):
        (
            gates_in,
            queries_in,
            keys_in,
            values_in,
            lengths_in,
            table_in,
            residual_in,
            chosen,
            weights_unused,
        ) = picked_rows
        attended = attend(
            gates_in,
            queries_in,
            keys_in,
            values_in,
            lengths_in,
            table_in,
            cache_pool,
            query_gain,
            key_gain,
        )
        projected = jnp.dot(attended, out_weight, preferred_element_type=jnp.float32)
        hidden = (residual_in.astype(jnp.float32) + projected).astype(jnp.bfloat16)
        normed = rms_scale(hidden, post_gain).astype(jnp.bfloat16)
        slots = slot_index(chosen, experts_all, local_experts, capacity)
        return (hidden, normed, slots, pack_rows(normed, slots, n_dev, capacity, local_experts))

    def home_front(unused):
        return front(row_args)

    def away_front(unused):
        return (
            jnp.zeros((rows_dev, width), jnp.bfloat16),
            jnp.zeros((rows_dev, width), jnp.bfloat16),
            jnp.zeros((rows_dev * topk,), jnp.int32),
            jnp.zeros((n_dev, capacity, local_experts, width), jnp.bfloat16),
        )

    hidden, normed, slots, packed = lax.cond(side == 0, home_front, away_front, None)
    moved = lax.all_to_all(packed, "dev", split_axis=0, concat_axis=0, tiled=True)
    received = from_behind(moved, "side", 1)

    def expert_work(unused):
        return (
            serve_rows(received, gate_weight, up_weight, down_weight),
            jnp.zeros((rows_dev, width), jnp.float32),
        )

    def home_work(unused):
        return (
            jnp.zeros_like(received),
            shared_branch(normed, shared_gate, shared_up, shared_down, shared_mix),
        )

    served, shared_out = lax.cond(side == 1, expert_work, home_work, None)
    crossed = from_behind(served, "side", -1)
    returned = lax.all_to_all(crossed, "dev", split_axis=0, concat_axis=0, tiled=True)
    joined = combine(hidden, returned.reshape(-1, width), slots, route_weights, shared_out)
    halves_out = lax.all_to_all(joined, "side", split_axis=1, concat_axis=0, tiled=True)
    return halves_out[:rows_dev]


def solution(mesh):
    placed = (
        P("dev", None),
        P("dev", None),
        P("dev", None),
        P("dev", None),
        P("dev"),
        P("dev", None),
        P("dev", None, None),
        P(),
        P(),
        P(),
        P("dev", None),
        P(),
        P("dev", None),
        P("dev", None),
        P("dev", None, None),
        P("dev", None, None),
        P("dev", None, None),
        P(),
        P(),
        P(),
        P(),
    )
    return jax.shard_map(
        on_device, mesh=mesh, in_specs=placed, out_specs=P("dev", "side"), check_vma=False
    )
```

profile of v0, /device:TPU:1, one launch (start us, length us, event | category | flops | bytes accessed | tf_op | source)
XLA Modules:
  0.0 136.5 jit_solution(3828621713904988717)
XLA Ops:
  0.0 1.8 %conditional.2 = (bf16[32,2048]{1,0:T(8,128)(2,1)S(1)}, s32[320]{0:T(512)S(1)}, bf16[64,2,4,2048]{3,2,1,0:T(4,128)(2,1)S(1)}, f32[32,2048]{1,0:T(8,128)}) conditional(s32[]{:T(128)} %convert_element_type.77, () %tuple.23, (bf16[32,2048]{1,0:T(8,128)(2,1)}, s32[32]{0:T(128)}, bf16[32,2048]{1,0:T(8,128)(2,1)}, f32[256]{0:T(256)}, s32[32,8]{0,1:T(8,128)}, ...), branch_computations={%region_0.0_spmd, %region_1.10_spmd} | conditional | flops 317103872 | bytes 42057204 | solution.py:187
  0.0 1.0 broadcast.231
  1.0 0.7 broadcast.232
  1.8 2.2 %copy.61 = bf16[64,2,4,2048]{3,1,2,0:T(2,128)(2,1)S(1)} copy(bf16[64,2,4,2048]{3,2,1,0:T(4,128)(2,1)S(1)} %get-tuple-element.80) | data formatting | bytes 4194304 | tf_op jit(solution)/shard_map/cond | solution.py:187
  4.0 0.0 copy-start.4
  4.0 0.0 copy-start.14
  4.0 30.5 %all_to_all.26 = bf16[64,2,4,2048]{3,1,2,0:T(2,128)(2,1)S(1)} all-to-all(bf16[64,2,4,2048]{3,1,2,0:T(2,128)(2,1)S(1)} %copy.61), channel_id=1, replica_groups=mesh['side'=2,'dev'=64] {'dev'}, dimensions={0} | all-to-all | bytes 4194304 | tf_op jit(solution)/shard_map/all_to_all | solution.py:188
  34.5 1.3 collective-permute-start
  35.8 31.4 %collective-permute-done = bf16[64,2,4,2048]{3,1,2,0:T(2,128)(2,1)} collective-permute-done((bf16[64,2,4,2048]{3,1,2,0:T(2,128)(2,1)S(1)}, bf16[64,2,4,2048]{3,1,2,0:T(2,128)(2,1)}, u32[]{:S(2)}, u32[]{:S(2)}) %collective-permute-start) | collective-permute-done | bytes 2097184 | tf_op jit(solution)/shard_map/ppermute | solution.py:12
  67.2 0.0 copy-done.4
  67.2 0.0 copy-done.14
  67.2 17.2 %conditional.3 = (bf16[64,2,4,2048]{3,2,1,0:T(4,128)(2,1)S(1)}, f32[32,2048]{1,0:T(8,128)S(1)}) conditional(s32[]{:T(128)} %convert_element_type.78, (bf16[32,2048]{1,0:T(8,128)(2,1)S(1)}, bf16[2048,256]{1,0:T(8,128)(2,1)S(1)}, bf16[2048,256]{1,0:T(8,128)(2,1)}, bf16[256,2048]{1,0:T(8,128)(2,1)}, bf16[2048]{0:T(1024)(128)(2,1)S(1)}) %tuple.44, ...), branch_computations={%region_11.12_spmd, %region_12.13_spmd} | conditional | flops 1612447744 | bytes 24379412 | solution.py:203
  67.2 5.4 %fusion.26 = f32[64,2,4,256]{3,0,1,2:T(8,128)S(1)} fusion(bf16[64,2,4,2048]{3,1,2,0:T(2,128)(2,1)} %get-tuple-element.172, bf16[4,2048,256]{2,1,0:T(8,128)(2,1)} %get-tuple-element.121), kind=kOutput, calls=%fused_computation.28 | convolution fusion | flops 536870912 | bytes 6815744 | tf_op jit(solution)/shard_map/cond/branch_1_fun/scud,udf->scuf/dot_general | solution.py:78
  72.6 8.5 %fusion.21 = bf16[64,2,4,2048]{3,0,1,2:T(8,128)(2,1)} fusion(bf16[4,256,2048]{2,1,0:T(8,128)(2,1)} %get-tuple-element.123, bf16[64,2,4,2048]{3,1,2,0:T(2,128)(2,1)} %get-tuple-element.172, bf16[4,2048,256]{2,1,0:T(8,128)(2,1)} %get-tuple-element.122, f32[64,2,4,256]{3,0,1,2:T(8,128)S(1)} %fusion.26), kind=kOutput, calls=%fused_computation.25 | convolution fusion | flops 1075576832 | bytes 13107200 | tf_op jit(solution)/shard_map/cond/branch_1_fun/scuf,ufd->scud/dot_general | solution.py:83
  81.2 3.2 %copy.56 = bf16[64,2,4,2048]{3,2,1,0:T(4,128)(2,1)S(1)} copy(bf16[64,2,4,2048]{3,0,1,2:T(8,128)(2,1)} %fusion.21) | data formatting | bytes 4194304 | tf_op jit(solution)/shard_map
  84.4 0.0 copy-start.5
  84.4 0.0 copy-start.10
  84.4 2.7 %collective-permute-start.1 = (bf16[64,2,4,2048]{3,2,1,0:T(4,128)(2,1)S(1)}, bf16[64,2,4,2048]{3,2,1,0:T(4,128)(2,1)}, u32[]{:S(2)}, u32[]{:S(2)}) collective-permute-start(bf16[64,2,4,2048]{3,2,1,0:T(4,128)(2,1)S(1)} %get-tuple-element.81), channel_id=1, source_target_pairs={{64,0},{65,1},{66,2},{67,3},{68,4},{69,5},{70,6},{71,7},{72,8},{73... | collective-permute-start | bytes 6291464 | tf_op jit(solution)/shard_map/ppermute | solution.py:12
  87.2 2.6 %collective-permute-done.1 = bf16[64,2,4,2048]{3,2,1,0:T(4,128)(2,1)} collective-permute-done((bf16[64,2,4,2048]{3,2,1,0:T(4,128)(2,1)S(1)}, bf16[64,2,4,2048]{3,2,1,0:T(4,128)(2,1)}, u32[]{:S(2)}, u32[]{:S(2)}) %collective-permute-start.1) | collective-permute-done | bytes 2097184 | tf_op jit(solution)/shard_map/ppermute | solution.py:12
  89.8 0.0 copy-done.5
  89.8 5.6 %all-to-all-start.1 = ((bf16[64,2,4,2048]{3,2,1,0:T(4,128)(2,1)}), bf16[64,2,4,2048]{3,2,1,0:T(4,128)(2,1)}, u32[]{:S(2)}, u32[]{:S(2)}) async-start(bf16[64,2,4,2048]{3,2,1,0:T(4,128)(2,1)} %collective-permute-done.1), calls=%async_computation.1 | async-start | bytes 4194304 | tf_op jit(solution)/shard_map/all_to_all | solution.py:205
  95.4 0.1 copy.69
  95.5 28.2 %all-to-all-done.1 = bf16[64,2,4,2048]{3,2,1,0:T(4,128)(2,1)} async-done(((bf16[64,2,4,2048]{3,2,1,0:T(4,128)(2,1)}), bf16[64,2,4,2048]{3,2,1,0:T(4,128)(2,1)}, u32[]{:S(2)}, u32[]{:S(2)}) %all-to-all-start.1) | async-done | bytes 2097184 | tf_op jit(solution)/shard_map/all_to_all | solution.py:205
  123.7 2.5 %reshape.223 = bf16[512,2048]{1,0:T(8,128)(2,1)S(1)} reshape(bf16[64,2,4,2048]{3,2,1,0:T(4,128)(2,1)} %all-to-all-done.1) | data formatting | bytes 4194304 | tf_op jit(solution)/shard_map/reshape | solution.py:206
  126.2 2.4 %gather_fusion.1 = bf16[320,2048]{1,0:T(8,128)(2,1)S(1)} fusion(bf16[512,2048]{1,0:T(8,128)(2,1)S(1)} %reshape.223, s32[1024]{0:T(1024)S(1)} %pad_clamp_fusion.1), kind=kCustom, calls=%fused_computation.1 | custom fusion | bytes 2622720 | tf_op jit(solution)/shard_map/gather | solution.py:99
  128.7 0.5 reshape.224
  129.2 0.4 fusion.107
  129.6 0.5 copy-done.1
  130.1 0.1 copy-done.6
  130.2 0.1 fusion.104
  130.3 5.5 %all_to_all.27 = bf16[32,2,1024]{2,0,1:T(8,128)(2,1)S(1)} all-to-all(bf16[32,2,1024]{2,0,1:T(8,128)(2,1)S(1)} %bitcast.106), channel_id=1, replica_groups=mesh['side'=2,'dev'=64] {'side'}, dimensions={1} | all-to-all | bytes 262144 | tf_op jit(solution)/shard_map/all_to_all | solution.py:207
  135.8 0.6 slice_bitcast_fusion.1
  (11 shorter events, 0.1 us)
Async XLA Ops:
  4.0 63.2 %copy-start.4 = (bf16[2048,256]{1,0:T(8,128)(2,1)S(1)}, bf16[2048,256]{1,0:T(8,128)(2,1)}, u32[]{:S(2)}) copy-start(bf16[2048,256]{1,0:T(8,128)(2,1)} %param.42) | copy-start | bytes 3145732
  4.0 63.2 %copy-start.14 = (bf16[2048]{0:T(1024)(128)(2,1)S(1)}, bf16[2048]{0:T(1024)(128)(2,1)}, u32[]{:S(2)}) copy-start(bf16[2048]{0:T(1024)(128)(2,1)} %param.45) | copy-start | bytes 12292
  34.5 32.7 %collective-permute-start = (bf16[64,2,4,2048]{3,1,2,0:T(2,128)(2,1)S(1)}, bf16[64,2,4,2048]{3,1,2,0:T(2,128)(2,1)}, u32[]{:S(2)}, u32[]{:S(2)}) collective-permute-start(bf16[64,2,4,2048]{3,1,2,0:T(2,128)(2,1)S(1)} %all_to_all.26), channel_id=1, source_target_pairs={{0,64},{1,65},{2,66},{3,67},{4,68},{5,69},{6,70},{7,71},{8,72},{9,... | collective-permute-start | bytes 6291464 | tf_op jit(solution)/shard_map/ppermute | solution.py:12
  84.4 5.4 %copy-start.5 = (f32[32,2048]{1,0:T(8,128)}, f32[32,2048]{1,0:T(8,128)S(1)}, u32[]{:S(2)}) copy-start(f32[32,2048]{1,0:T(8,128)S(1)} %get-tuple-element.83) | copy-start | bytes 786436
  84.4 10.9 %copy-start.10 = (f32[32,10]{0,1:T(8,128)S(1)}, f32[32,10]{0,1:T(8,128)}, u32[]{:S(2)}) copy-start(f32[32,10]{0,1:T(8,128)} %param.38) | copy-start | bytes 3844
  84.4 5.3 %collective-permute-start.1 = (bf16[64,2,4,2048]{3,2,1,0:T(4,128)(2,1)S(1)}, bf16[64,2,4,2048]{3,2,1,0:T(4,128)(2,1)}, u32[]{:S(2)}, u32[]{:S(2)}) collective-permute-start(bf16[64,2,4,2048]{3,2,1,0:T(4,128)(2,1)S(1)} %get-tuple-element.81), channel_id=1, source_target_pairs={{64,0},{65,1},{66,2},{67,3},{68,4},{69,5},{70,6},{71,7},{72,8},{73... | collective-permute-start | bytes 6291464 | tf_op jit(solution)/shard_map/ppermute | solution.py:12
  89.8 33.9 %all-to-all-start.1 = ((bf16[64,2,4,2048]{3,2,1,0:T(4,128)(2,1)}), bf16[64,2,4,2048]{3,2,1,0:T(4,128)(2,1)}, u32[]{:S(2)}, u32[]{:S(2)}) async-start(bf16[64,2,4,2048]{3,2,1,0:T(4,128)(2,1)} %collective-permute-done.1), calls=%async_computation.1 | async-start | bytes 4194304 | tf_op jit(solution)/shard_map/all_to_all | solution.py:205
  129.2 1.0 copy-start.1
  129.2 1.0 copy-start.6
where the time goes:
time: 137 us; the launch traced here: 136 us
  waiting for transfers between devices  62.2 us (45%)
  blocking collectives  36.1 us (26%)
  matrix products  14.4 us (11%)
  local copies, waits for them, and re-layouts  13.9 us (10%)
  starting transfers between devices  9.59 us (7%)
    ppermute x2, waiting for transfers between devices, from_behind(): lax.ppermute(value, axis, [(source, source + steps) for source in range(f...  34 us
    all_to_all x1, blocking collectives, on_device(): lax.all_to_all(packed, 'dev', split_axis=0, concat_axis=0, tiled=True)  30.5 us
    all_to_all x1, waiting for transfers between devices, on_device(): lax.all_to_all(crossed, 'dev', split_axis=0, concat_axis=0, tiled=True)  28.2 us
    dot_general x1, matrix products, serve_rows(): jnp.einsum('scuf,ufd->scud', inner, down_weight, preferred_element_type=j...  8.53 us
    all_to_all x1, starting transfers between devices, on_device(): lax.all_to_all(crossed, 'dev', split_axis=0, concat_axis=0, tiled=True)  5.57 us
    all_to_all x1, blocking collectives, on_device(): lax.all_to_all(joined, 'side', split_axis=1, concat_axis=0, tiled=True)  5.53 us
    dot_general x1, matrix products, serve_rows(): jnp.einsum('scud,udf->scuf', received, gate_weight, preferred_element_typ...  5.41 us
    another operation x6, local copies, waits for them, and re-layouts  5.01 us
  transfers between devices with their start and end apart: 3, of which 3 were waited for; matrix products, arithmetic and copies ran while one was open for 0% of the time, Pallas kernels for 0%

commit v1 on v0

v1 whole, which is shorter than its diff:
```python
import functools
import jax
import jax.numpy as jnp
from jax import lax
from jax.experimental import pallas as pl
from jax.experimental.pallas import tpu as pltpu
from jax.sharding import PartitionSpec as P

eps = 1e-06
f32 = jnp.float32
bf16 = jnp.bfloat16
i32 = jnp.int32
MIB = 1 << 20


def dot(left, right):
    return jnp.dot(left, right, preferred_element_type=f32)


def iota(shape, axis):
    return lax.broadcasted_iota(i32, shape, axis)


def rms_scale(wide, gain):
    return wide * lax.rsqrt(jnp.mean(wide * wide, axis=-1, keepdims=True) + eps) * gain


def group_order(groups, members, to_groups):
    size = groups * members
    by_group = iota((size, size), 0 if to_groups else 1)
    by_member = iota((size, size), 1 if to_groups else 0)
    wanted = (by_group % members) * groups + by_group // members
    return (wanted == by_member).astype(f32).astype(bf16)


def expert_hits(experts_ref, slot_expert):
    rows, topk = experts_ref.shape
    hits = jnp.zeros(slot_expert.shape, f32)
    for k in range(topk):
        hits = jnp.where(experts_ref[:, k : k + 1] == slot_expert, 1.0, hits)
    earlier = (iota((rows, rows), 1) < iota((rows, rows), 0)).astype(f32).astype(bf16)
    rank = dot(earlier, hits.astype(bf16))
    return hits, rank


def front_kernel(
    lengths_ref,
    table_ref,
    experts_ref,
    gates_ref,
    queries_ref,
    keys_ref,
    values_ref,
    query_gain_ref,
    key_gain_ref,
    post_gain_ref,
    residual_ref,
    pool_hbm,
    weight_hbm,
    packed_ref,
    hidden_ref,
    normed_ref,
    pool,
    weight,
    query,
    prob,
    attended,
    pool_sem,
    weight_sem,
    *,
    page,
    local,
):
    rows, width = queries_ref.shape
    head = keys_ref.shape[1]
    heads = width // head
    tokens = pool.shape[0]
    context = 256
    chunks = tokens // context
    side = lax.axis_index("side")

    pool_copies = []
    third = tokens // pool_sem.shape[0]
    for i in range(pool_sem.shape[0]):
        part = pl.ds(i * third, third)
        pool_copies.append(
            pltpu.make_async_copy(pool_hbm.at[part], pool.at[part], pool_sem.at[i])
        )
    weight_copies = []
    quarter = width // weight_sem.shape[0]
    for i in range(weight_sem.shape[0]):
        part = pl.ds(i * quarter, quarter)
        weight_copies.append(
            pltpu.make_async_copy(weight_hbm.at[part], weight.at[part], weight_sem.at[i])
        )
    for copy in pool_copies + weight_copies:
        copy.start()

    scale = head ** (-0.5)
    key_normed = rms_scale(keys_ref[...].astype(f32), key_gain_ref[...]).astype(bf16).astype(f32)
    own = []
    for h in range(heads):
        part = queries_ref[:, h * head : (h + 1) * head].astype(f32)
        normed = rms_scale(part, query_gain_ref[...]).astype(bf16)
        query[h * rows : (h + 1) * rows, :] = normed
        own.append(jnp.sum(normed.astype(f32) * key_normed, axis=-1, keepdims=True))
    own_weight = jnp.exp(jnp.concatenate(own, axis=0) * scale)

    same = iota((rows, rows), 0) == iota((rows, rows), 1)
    lengths = jnp.sum(
        jnp.where(same, jnp.broadcast_to(lengths_ref[...], (rows, rows)), 0), axis=1, keepdims=True
    )
    total = jnp.zeros((heads * rows, context), f32)
    for c in range(chunks):
        if (c * context) % third == 0:
            pool_copies[c * context // third].wait()
        at = pl.ds(c * context, context)
        token = iota((rows, context), 1) + c * context
        token_page = token // page
        token_in = token % page
        valid = jnp.zeros((rows, context), f32)
        for entry in range(table_ref.shape[1]):
            hit = (table_ref[:, entry : entry + 1] == token_page) & (
                token_in + entry * page < lengths
            )
            valid = jnp.where(hit, 1.0, valid)
        scores = lax.dot_general(
            query[...],
            pool[at, :head],
            (((1,), (1,)), ((), ())),
            preferred_element_type=f32,
        )
        weights = jnp.exp(scores * scale)
        weights = (weights.reshape(heads, rows, context) * valid[None]).reshape(
            heads * rows, context
        )
        total = total + weights
        prob[:, at] = weights.astype(bf16)
    mixed = dot(prob[...], pool[:, head:])
    inverse = 1.0 / (jnp.sum(total, axis=1, keepdims=True) + own_weight)
    new_values = values_ref[...].astype(f32)
    for h in range(heads):
        part = slice(h * rows, (h + 1) * rows)
        value = (mixed[part] + own_weight[part] * new_values) * inverse[part]
        gate = jax.nn.sigmoid(gates_ref[:, h * head : (h + 1) * head].astype(f32))
        attended[:, h * head : (h + 1) * head] = (value * gate).astype(bf16)

    projected = residual_ref[...].astype(f32)
    for i, copy in enumerate(weight_copies):
        copy.wait()
        at = slice(i * quarter, (i + 1) * quarter)
        projected = projected + dot(attended[:, at], weight[at, :])
    hidden = projected.astype(bf16)
    hidden_ref[...] = hidden
    normed = rms_scale(hidden.astype(f32), post_gain_ref[...]).astype(bf16)
    normed_ref[...] = normed

    slots, columns = packed_ref.shape
    parts = width // columns
    mine = local // 2
    slot = iota((rows, slots), 1)
    per = parts * mine
    destination = slot // per
    n_dev = slots // per // 2
    expert = (destination % n_dev) * local + (destination // n_dev) * mine + slot % mine
    hits, rank = expert_hits(experts_ref, expert)
    chosen = jnp.where(rank == side.astype(f32), hits, 0.0)
    slot_part = slot % per // mine
    spread = jnp.concatenate(
        [jnp.where(slot_part == p, chosen, 0.0) for p in range(parts)], axis=0
    )
    stacked = jnp.concatenate(
        [normed[:, p * columns : (p + 1) * columns] for p in range(parts)], axis=0
    )
    packed_ref[...] = dot(spread.T.astype(bf16), stacked).astype(bf16)


def expert_kernel(
    normed_ref,
    hidden_ref,
    mix_ref,
    received_hbm,
    gate_hbm,
    up_hbm,
    down_hbm,
    shared_gate_hbm,
    shared_up_hbm,
    shared_down_hbm,
    sent_ref,
    base_ref,
    received,
    gate,
    up,
    down,
    shared_gate,
    shared_up,
    shared_down,
    taken,
    result,
    sem,
):
    mine, width, inner_width = gate.shape
    slots, columns = received.shape
    parts = width // columns
    rows = slots // (parts * mine)
    half = width // 2
    side = lax.axis_index("side")
    experts_at = pl.ds(side * mine, mine)
    columns_at = pl.ds(pl.multiple_of(side * half, half), half)
    copies = [
        pltpu.make_async_copy(source, target, sem.at[i])
        for i, (source, target) in enumerate(
            (
                (received_hbm, received),
                (shared_gate_hbm, shared_gate),
                (shared_up_hbm, shared_up),
                (gate_hbm.at[experts_at], gate),
                (up_hbm.at[experts_at], up),
                (shared_down_hbm.at[:, columns_at], shared_down),
                (down_hbm.at[experts_at], down),
            )
        )
    ]
    for copy in copies:
        copy.start()
    groups = parts * mine
    block = 32
    inward = group_order(groups, block, True)
    outward = group_order(groups, block, False)

    copies[0].wait()
    for b in range(rows // block):
        ordered = dot(inward, received[b * groups * block : (b + 1) * groups * block, :]).astype(
            bf16
        )
        for p in range(parts):
            for j in range(mine):
                at = (p * mine + j) * block
                taken[j, b * block : (b + 1) * block, p * columns : (p + 1) * columns] = ordered[
                    at : at + block
                ]

    copies[1].wait()
    copies[2].wait()
    normed = normed_ref[...]
    shared_inner = (
        jax.nn.silu(dot(normed, shared_gate[...])) * dot(normed, shared_up[...])
    ).astype(bf16)
    mix = jax.nn.sigmoid(
        jnp.sum(normed.astype(f32) * mix_ref[...].astype(f32), axis=-1, keepdims=True)
    )
    copies[3].wait()
    copies[4].wait()
    inner = [
        (jax.nn.silu(dot(taken[j], gate[j])) * dot(taken[j], up[j])).astype(bf16)
        for j in range(mine)
    ]
    copies[5].wait()
    base_ref[...] = hidden_ref[:, columns_at].astype(f32) + mix * dot(
        shared_inner, shared_down[...]
    )
    copies[6].wait()
    for j in range(mine):
        result[j] = dot(inner[j], down[j]).astype(bf16)

    n_dev = rows // 2
    for t in range(2):
        for b in range(n_dev // block):
            gathered = jnp.concatenate(
                [
                    result[
                        j,
                        s * n_dev + b * block : s * n_dev + (b + 1) * block,
                        t * half + p * columns : t * half + (p + 1) * columns,
                    ]
                    for p in range(half // columns)
                    for s in range(2)
                    for j in range(mine)
                ],
                axis=0,
            )
            at = (t * n_dev + b * block) * groups
            sent_ref[at : at + groups * block, :] = dot(outward, gathered).astype(bf16)


def combine_kernel(
    experts_ref, weights_ref, base_ref, returned_hbm, out_ref, returned, sem, *, local
):
    copy = pltpu.make_async_copy(returned_hbm, returned, sem.at[0])
    copy.start()
    rows, topk = experts_ref.shape
    slots, columns = returned.shape
    parts = out_ref.shape[1] // columns
    mine = local // 2
    per = parts * 2 * mine
    slot = iota((rows, slots), 1)
    source = slot // per
    n_dev = slots // per // 2
    expert = (source % n_dev) * local + (source // n_dev) * mine + slot % mine
    weights = weights_ref[...]
    share = weights / jnp.sum(weights, axis=1, keepdims=True)
    spread = jnp.zeros((rows, slots), f32)
    for k in range(topk):
        spread = jnp.where(experts_ref[:, k : k + 1] == expert, share[:, k : k + 1], spread)
    hits, rank = expert_hits(experts_ref, expert)
    sender = slot % (2 * mine) // mine
    spread = jnp.where(rank == sender.astype(f32), spread, 0.0)
    slot_part = slot % per // (2 * mine)
    pieces = []
    for p in range(parts):
        piece = jnp.where(slot_part == p, spread, 0.0)
        high = piece.astype(bf16)
        pieces.append(high)
        pieces.append((piece - high.astype(f32)).astype(bf16))
    stacked = jnp.concatenate(pieces, axis=0)
    copy.wait()
    routed = dot(stacked, returned[...])
    for p in range(parts):
        at = 2 * p * rows
        value = routed[at : at + rows] + routed[at + rows : at + 2 * rows]
        out_ref[:, p * columns : (p + 1) * columns] = (
            base_ref[:, p * columns : (p + 1) * columns] + value
        ).astype(bf16)


VMEM = pl.BlockSpec(memory_space=pltpu.VMEM)
HBM = pl.BlockSpec(memory_space=pl.ANY)


def exchange(value):
    return lax.all_to_all(value, ("side", "dev"), split_axis=0, concat_axis=0, tiled=True)


def on_device(
    out_gates,
    queries,
    keys_new,
    values_new,
    lengths,
    page_table,
    cache_pool,
    query_gain,
    key_gain,
    out_weight,
    residual,
    post_gain,
    experts,
    route_weights,
    gate_weight,
    up_weight,
    down_weight,
    shared_gate,
    shared_up,
    shared_down,
    shared_mix,
):
    n_dev = lax.axis_size("dev")
    local, width, inner_width = gate_weight.shape
    rows = queries.shape[0]
    head = keys_new.shape[1]
    heads = width // head
    pages, page, both = cache_pool.shape
    tokens = pages * page
    mine = local // 2
    columns = width * mine // 8
    slots = 2 * n_dev * 8
    packed, hidden, normed = pl.pallas_call(
        functools.partial(front_kernel, page=page, local=local),
        out_shape=(
            jax.ShapeDtypeStruct((slots, columns), bf16),
            jax.ShapeDtypeStruct((rows, width), bf16),
            jax.ShapeDtypeStruct((rows, width), bf16),
        ),
        in_specs=[VMEM] * 11 + [HBM] * 2,
        out_specs=(VMEM, VMEM, VMEM),
        scratch_shapes=[
            pltpu.VMEM((tokens, both), bf16),
            pltpu.VMEM((width, width), bf16),
            pltpu.VMEM((heads * rows, head), bf16),
            pltpu.VMEM((heads * rows, tokens), bf16),
            pltpu.VMEM((rows, width), bf16),
            pltpu.SemaphoreType.DMA((3,)),
            pltpu.SemaphoreType.DMA((4,)),
        ],
        compiler_params=pltpu.CompilerParams(vmem_limit_bytes=40 * MIB),
    )(
        lengths[None, :],
        page_table,
        experts,
        out_gates,
        queries,
        keys_new,
        values_new,
        query_gain[None, :],
        key_gain[None, :],
        post_gain[None, :],
        residual,
        cache_pool.reshape(tokens, both),
        out_weight,
    )
    received = exchange(packed)
    half = width // 2
    sent, base = pl.pallas_call(
        expert_kernel,
        out_shape=(
            jax.ShapeDtypeStruct((slots, columns), bf16),
            jax.ShapeDtypeStruct((rows, half), f32),
        ),
        in_specs=[VMEM] * 3 + [HBM] * 7,
        out_specs=(VMEM, VMEM),
        scratch_shapes=[
            pltpu.VMEM((slots, columns), bf16),
            pltpu.VMEM((mine, width, inner_width), bf16),
            pltpu.VMEM((mine, width, inner_width), bf16),
            pltpu.VMEM((mine, inner_width, width), bf16),
            pltpu.VMEM(shared_gate.shape, bf16),
            pltpu.VMEM(shared_up.shape, bf16),
            pltpu.VMEM((shared_down.shape[0], half), bf16),
            pltpu.VMEM((mine, 2 * n_dev, width), bf16),
            pltpu.VMEM((mine, 2 * n_dev, width), bf16),
            pltpu.SemaphoreType.DMA((7,)),
        ],
        compiler_params=pltpu.CompilerParams(vmem_limit_bytes=40 * MIB),
    )(
        normed,
        hidden,
        shared_mix[None, :],
        received,
        gate_weight,
        up_weight,
        down_weight,
        shared_gate,
        shared_up,
        shared_down,
    )
    returned = exchange(sent)
    return pl.pallas_call(
        functools.partial(combine_kernel, local=local),
        out_shape=jax.ShapeDtypeStruct((rows, half), bf16),
        in_specs=[VMEM] * 3 + [HBM],
        out_specs=VMEM,
        scratch_shapes=[
            pltpu.VMEM((slots, columns), bf16),
            pltpu.SemaphoreType.DMA((1,)),
        ],
        compiler_params=pltpu.CompilerParams(vmem_limit_bytes=40 * MIB),
    )(experts, route_weights, base, returned)


def solution(mesh):
    placed = (
        P("dev", None),
        P("dev", None),
        P("dev", None),
        P("dev", None),
        P("dev"),
        P("dev", None),
        P("dev", None, None),
        P(),
        P(),
        P(),
        P("dev", None),
        P(),
        P("dev", None),
        P("dev", None),
        P("dev", None, None),
        P("dev", None, None),
        P("dev", None, None),
        P(),
        P(),
        P(),
        P(),
    )
    return jax.shard_map(
        on_device, mesh=mesh, in_specs=placed, out_specs=P("dev", "side"), check_vma=False
    )
```

time: 137 us -> 85.6 us (0.62)
  blocking collectives: 36.1 us -> 0 us
  waiting for transfers between devices: 62.2 us -> 33.9 us
  matrix products: 14.4 us -> 0 us
  Pallas kernels: 0 us -> 12.5 us
  starting transfers between devices: 9.59 us -> 17.2 us
  local copies, waits for them, and re-layouts: 13.9 us -> 21.1 us
    all_to_all x2 -> x0, blocking collectives: 36.1 us -> none  [the longest x1 30.5 us: on_device(): lax.all_to_all(packed, 'dev', split_axis=0, concat_axis=0, tiled=True)]
    ppermute x2 -> x0, waiting for transfers between devices: 34 us -> none  [from_behind(): lax.ppermute(value, axis, [(source, source + steps) for source in range(f...]
    unnamed x12 -> x39, local copies, waits for them, and re-layouts: 0.59 us -> 20.5 us
    dot_general x3 -> x0, matrix products: 14.4 us -> none  [the longest x1 8.53 us: serve_rows(): jnp.einsum('scuf,ufd->scud', inner, down_weight, preferred_element_type=j...]
    pallas_call x0 -> x3, Pallas kernels: none -> 12.5 us  [the longest x1 6.79 us: on_device(): pl.pallas_call(functools.partial(front_kernel, page=page, local=local), o...]
    all_to_all x1 -> x2, starting transfers between devices: 5.57 us -> 17.2 us  [exchange(): lax.all_to_all(value, ('side', 'dev'), split_axis=0, concat_axis=0, tiled...]
    all_to_all x1 -> x2, waiting for transfers between devices: 28.2 us -> 33.9 us  [exchange(): lax.all_to_all(value, ('side', 'dev'), split_axis=0, concat_axis=0, tiled...]
    another operation x6 -> x0, local copies, waits for them, and re-layouts: 5.01 us -> none
  transfers between devices with their start and end apart: 3 -> 2, of which waited for: 3 -> 2; matrix products, arithmetic and copies ran while one was open for 0% -> 2% of each run, Pallas kernels for 0% -> 0%
where the time goes in v1:
time: 85.6 us; the launch traced here: 84.8 us
  waiting for transfers between devices  33.9 us (40%)
  local copies, waits for them, and re-layouts  21.1 us (25%)
  starting transfers between devices  17.2 us (20%)
  Pallas kernels  12.5 us (15%)
    all_to_all x2, waiting for transfers between devices, exchange(): lax.all_to_all(value, ('side', 'dev'), split_axis=0, concat_axis=0, tiled...  33.9 us
    unnamed x39, local copies, waits for them, and re-layouts  20.5 us
    all_to_all x2, starting transfers between devices, exchange(): lax.all_to_all(value, ('side', 'dev'), split_axis=0, concat_axis=0, tiled...  17.2 us
    pallas_call x1, Pallas kernels, on_device(): pl.pallas_call(functools.partial(front_kernel, page=page, local=local), o...  6.79 us
    pallas_call x1, Pallas kernels, on_device(): pl.pallas_call(expert_kernel, out_shape=(jax.ShapeDtypeStruct((slots, col...  4.31 us
  transfers between devices with their start and end apart: 2, of which 2 were waited for; matrix products, arithmetic and copies ran while one was open for 2% of the time, Pallas kernels for 0%

profile of v1, /device:TPU:1, one launch (start us, length us, event | category | flops | bytes accessed | tf_op | source)
XLA Modules:
  0.0 84.8 jit_solution(3617247338405909991)
XLA Ops:
  0.0 0.8 copy.24.experts_ref
  0.8 0.8 copy.22.table_ref
  1.5 0.0 copy-start
  1.5 3.4 %copy-done = bf16[2048,2048]{1,0:T(8,128)(2,1)S(1)} copy-done((bf16[2048,2048]{1,0:T(8,128)(2,1)S(1)}, bf16[2048,2048]{1,0:T(8,128)(2,1)}, u32[]{:S(2)}) %copy-start) | copy-done | bytes 8388632
  4.9 0.0 copy-start.3
  4.9 1.7 %copy-done.3 = bf16[144,16,512]{2,1,0:T(8,128)(2,1)S(1)} copy-done((bf16[144,16,512]{2,1,0:T(8,128)(2,1)S(1)}, bf16[144,16,512]{2,1,0:T(8,128)(2,1)}, u32[]{:S(2)}) %copy-start.3) | copy-done | bytes 2359320
  6.6 0.0 copy-start.7
  6.6 0.9 %copy-done.7 = bf16[32,2048]{1,0:T(8,128)(2,1)S(1)} copy-done((bf16[32,2048]{1,0:T(8,128)(2,1)S(1)}, bf16[32,2048]{1,0:T(8,128)(2,1)}, u32[]{:S(2)}) %copy-start.7) | copy-done | bytes 131096
  7.5 0.9 %copy-done.8 = bf16[32,2048]{1,0:T(8,128)(2,1)S(1)} copy-done((bf16[32,2048]{1,0:T(8,128)(2,1)S(1)}, bf16[32,2048]{1,0:T(8,128)(2,1)}, u32[]{:S(2)}) %copy-start.8) | copy-done | bytes 131096
  8.4 0.9 %copy-done.9 = bf16[32,2048]{1,0:T(8,128)(2,1)S(1)} copy-done((bf16[32,2048]{1,0:T(8,128)(2,1)S(1)}, bf16[32,2048]{1,0:T(8,128)(2,1)}, u32[]{:S(2)}) %copy-start.9) | copy-done | bytes 131096
  9.3 0.7 copy-done.11
  10.0 0.7 copy-done.12
  10.7 0.7 copy-done.13
  11.4 0.7 copy-done.14
  12.1 0.7 copy-done.15
  12.8 0.7 copy-done.16
  13.5 6.8 %shard_map.199 = (bf16[1024,512]{1,0:T(8,128)(2,1)}, bf16[32,2048]{1,0:T(8,128)(2,1)S(1)}, bf16[32,2048]{1,0:T(8,128)(2,1)S(1)}) custom-call(s32[1,32]{1,0:T(1,128)S(1)} %bitcast.15, s32[32,8]{1,0:T(8,128)S(1)} %copy.22.table_ref, s32[32,10]{1,0:T(8,128)S(1)} %copy.24.experts_ref, bf16[32,2048]{1,0:T(8,128)(2,1)S(1)} %copy-done.7, ...), custom_call_target="tpu_custom_call" | custom-call | tf_op jit(solution)/shard_map/pallas_call | solution.py:367
  20.2 11.5 %all-to-all-start = ((bf16[128,8,512]{2,1,0:T(8,128)(2,1)}), bf16[128,8,512]{2,1,0:T(8,128)(2,1)S(1)}, u32[]{:S(2)}, u32[]{:S(2)}) async-start(bf16[128,8,512]{2,1,0:T(8,128)(2,1)} %bitcast.5), calls=%async_computation | async-start | bytes 2097152 | tf_op jit(solution)/shard_map/all_to_all | solution.py:331
  31.8 0.0 copy-done.17
  31.8 0.6 broadcast_in_dim.19.mix_ref
  32.4 17.0 %all-to-all-done = bf16[128,8,512]{2,1,0:T(8,128)(2,1)S(1)} async-done(((bf16[128,8,512]{2,1,0:T(8,128)(2,1)}), bf16[128,8,512]{2,1,0:T(8,128)(2,1)S(1)}, u32[]{:S(2)}, u32[]{:S(2)}) %all-to-all-start) | async-done | bytes 1048608 | tf_op jit(solution)/shard_map/all_to_all | solution.py:331
  49.4 0.0 copy-done.4
  49.4 0.0 copy-done.5
  49.4 2.2 %copy-done.1 = bf16[4,2048,256]{2,1,0:T(8,128)(2,1)S(1)} copy-done((bf16[4,2048,256]{2,1,0:T(8,128)(2,1)S(1)}, bf16[4,2048,256]{2,1,0:T(8,128)(2,1)}, u32[]{:S(2)}) %copy-start.1) | copy-done | bytes 4194328
  51.6 2.2 %copy-done.2 = bf16[4,2048,256]{2,1,0:T(8,128)(2,1)S(1)} copy-done((bf16[4,2048,256]{2,1,0:T(8,128)(2,1)S(1)}, bf16[4,2048,256]{2,1,0:T(8,128)(2,1)}, u32[]{:S(2)}) %copy-start.2) | copy-done | bytes 4194328
  53.8 1.2 %copy-done.6 = bf16[256,2048]{1,0:T(8,128)(2,1)S(1)} copy-done((bf16[256,2048]{1,0:T(8,128)(2,1)S(1)}, bf16[256,2048]{1,0:T(8,128)(2,1)}, u32[]{:S(2)}) %copy-start.6) | copy-done | bytes 1048600
  55.0 0.7 copy-done.10
  55.7 4.3 %shard_map.200 = (bf16[1024,512]{1,0:T(8,128)(2,1)}, f32[32,1024]{1,0:T(8,128)S(1)}) custom-call(bf16[32,2048]{1,0:T(8,128)(2,1)S(1)} %get-tuple-element.10.normed_ref, bf16[32,2048]{1,0:T(8,128)(2,1)S(1)} %get-tuple-element.11.hidden_ref, bf16[1,2048]{1,0:T(2,128)(2,1)S(1)} %copy-done.10, bf16[1024,512]{1,0:T(8,128)(2,1)S(1)} %bitcast.10, ...), custom_call_target="tpu_custom_call" | custom-call | tf_op jit(solution)/shard_map/pallas_call | solution.py:403
  60.0 5.7 %all-to-all-start.1 = ((bf16[128,8,512]{2,1,0:T(8,128)(2,1)}), bf16[128,8,512]{2,1,0:T(8,128)(2,1)S(1)}, u32[]{:S(2)}, u32[]{:S(2)}) async-start(bf16[128,8,512]{2,1,0:T(8,128)(2,1)} %bitcast.7), calls=%async_computation.1 | async-start | bytes 2097152 | tf_op jit(solution)/shard_map/all_to_all | solution.py:331
  65.8 0.8 copy.25.weights_ref
  66.5 16.9 %all-to-all-done.1 = bf16[128,8,512]{2,1,0:T(8,128)(2,1)S(1)} async-done(((bf16[128,8,512]{2,1,0:T(8,128)(2,1)}), bf16[128,8,512]{2,1,0:T(8,128)(2,1)S(1)}, u32[]{:S(2)}, u32[]{:S(2)}) %all-to-all-start.1) | async-done | bytes 1048608 | tf_op jit(solution)/shard_map/all_to_all | solution.py:331
  83.4 1.4 %shard_map.201 = bf16[32,1024]{1,0:T(8,128)(2,1)} custom-call(s32[32,10]{1,0:T(8,128)S(1)} %copy.24.experts_ref, f32[32,10]{1,0:T(8,128)S(1)} %copy.25.weights_ref, f32[32,1024]{1,0:T(8,128)S(1)} %get-tuple-element.13.base_ref, bf16[1024,512]{1,0:T(8,128)(2,1)S(1)} %bitcast.9), custom_call_target="tpu_custom_call" | custom-call | tf_op jit(solution)/shard_map/pallas_call | solution.py:437
  (15 shorter events, 0.0 us)
Async XLA Ops:
  1.5 3.4 %copy-start = (bf16[2048,2048]{1,0:T(8,128)(2,1)S(1)}, bf16[2048,2048]{1,0:T(8,128)(2,1)}, u32[]{:S(2)}) copy-start(bf16[2048,2048]{1,0:T(8,128)(2,1)} %weight_hbm.1) | copy-start | bytes 25165828
  4.9 1.7 %copy-start.3 = (bf16[144,16,512]{2,1,0:T(8,128)(2,1)S(1)}, bf16[144,16,512]{2,1,0:T(8,128)(2,1)}, u32[]{:S(2)}) copy-start(bf16[144,16,512]{2,1,0:T(8,128)(2,1)} %param.27) | copy-start | bytes 7077892
  6.6 0.9 %copy-start.7 = (bf16[32,2048]{1,0:T(8,128)(2,1)S(1)}, bf16[32,2048]{1,0:T(8,128)(2,1)}, u32[]{:S(2)}) copy-start(bf16[32,2048]{1,0:T(8,128)(2,1)} %gates_ref.1) | copy-start | bytes 393220
  7.5 0.9 %copy-start.8 = (bf16[32,2048]{1,0:T(8,128)(2,1)S(1)}, bf16[32,2048]{1,0:T(8,128)(2,1)}, u32[]{:S(2)}) copy-start(bf16[32,2048]{1,0:T(8,128)(2,1)} %queries_ref.1) | copy-start | bytes 393220
  8.4 0.9 %copy-start.9 = (bf16[32,2048]{1,0:T(8,128)(2,1)S(1)}, bf16[32,2048]{1,0:T(8,128)(2,1)}, u32[]{:S(2)}) copy-start(bf16[32,2048]{1,0:T(8,128)(2,1)} %residual_ref.1) | copy-start | bytes 393220
  9.3 0.7 copy-start.11
  10.0 0.7 copy-start.12
  10.7 0.7 copy-start.13
  11.4 0.7 copy-start.14
  12.1 0.7 copy-start.15
  12.8 0.7 copy-start.16
  13.4 18.3 %copy-start.17 = (bf16[2048]{0:T(1024)(128)(2,1)S(1)}, bf16[2048]{0:T(1024)(128)(2,1)}, u32[]{:S(2)}) copy-start(bf16[2048]{0:T(1024)(128)(2,1)} %param.41) | copy-start | bytes 12292
  13.4 36.0 %copy-start.4 = (bf16[2048,256]{1,0:T(8,128)(2,1)S(1)}, bf16[2048,256]{1,0:T(8,128)(2,1)}, u32[]{:S(2)}) copy-start(bf16[2048,256]{1,0:T(8,128)(2,1)} %shared_gate_hbm.1) | copy-start | bytes 3145732
  13.5 36.0 %copy-start.5 = (bf16[2048,256]{1,0:T(8,128)(2,1)S(1)}, bf16[2048,256]{1,0:T(8,128)(2,1)}, u32[]{:S(2)}) copy-start(bf16[2048,256]{1,0:T(8,128)(2,1)} %shared_up_hbm.1) | copy-start | bytes 3145732
  20.2 29.2 %all-to-all-start = ((bf16[128,8,512]{2,1,0:T(8,128)(2,1)}), bf16[128,8,512]{2,1,0:T(8,128)(2,1)S(1)}, u32[]{:S(2)}, u32[]{:S(2)}) async-start(bf16[128,8,512]{2,1,0:T(8,128)(2,1)} %bitcast.5), calls=%async_computation | async-start | bytes 2097152 | tf_op jit(solution)/shard_map/all_to_all | solution.py:331
  49.4 2.2 %copy-start.1 = (bf16[4,2048,256]{2,1,0:T(8,128)(2,1)S(1)}, bf16[4,2048,256]{2,1,0:T(8,128)(2,1)}, u32[]{:S(2)}) copy-start(bf16[4,2048,256]{2,1,0:T(8,128)(2,1)} %gate_hbm.1) | copy-start | bytes 12582916
  51.6 2.2 %copy-start.2 = (bf16[4,2048,256]{2,1,0:T(8,128)(2,1)S(1)}, bf16[4,2048,256]{2,1,0:T(8,128)(2,1)}, u32[]{:S(2)}) copy-start(bf16[4,2048,256]{2,1,0:T(8,128)(2,1)} %up_hbm.1) | copy-start | bytes 12582916
  53.8 1.2 %copy-start.6 = (bf16[256,2048]{1,0:T(8,128)(2,1)S(1)}, bf16[256,2048]{1,0:T(8,128)(2,1)}, u32[]{:S(2)}) copy-start(bf16[256,2048]{1,0:T(8,128)(2,1)} %shared_down_hbm.1) | copy-start | bytes 3145732
  55.0 0.7 copy-start.10
  60.0 23.4 %all-to-all-start.1 = ((bf16[128,8,512]{2,1,0:T(8,128)(2,1)}), bf16[128,8,512]{2,1,0:T(8,128)(2,1)S(1)}, u32[]{:S(2)}, u32[]{:S(2)}) async-start(bf16[128,8,512]{2,1,0:T(8,128)(2,1)} %bitcast.7), calls=%async_computation.1 | async-start | bytes 2097152 | tf_op jit(solution)/shard_map/all_to_all | solution.py:331

commit v2 on v1

v2 whole, which is shorter than its diff:
```python
import functools
import jax
import jax.numpy as jnp
from jax import lax
from jax.experimental import pallas as pl
from jax.experimental.pallas import tpu as pltpu
from jax.sharding import PartitionSpec as P

eps = 1e-06
f32 = jnp.float32
bf16 = jnp.bfloat16
i32 = jnp.int32
MIB = 1 << 20


def dot(left, right):
    return jnp.dot(left, right, preferred_element_type=f32)


def iota(shape, axis):
    return lax.broadcasted_iota(i32, shape, axis)


def rms_scale(wide, gain):
    return wide * lax.rsqrt(jnp.mean(wide * wide, axis=-1, keepdims=True) + eps) * gain


def group_order(groups, members, to_groups):
    size = groups * members
    by_group = iota((size, size), 0 if to_groups else 1)
    by_member = iota((size, size), 1 if to_groups else 0)
    wanted = (by_group % members) * groups + by_group // members
    return (wanted == by_member).astype(f32).astype(bf16)


def expert_hits(experts, slot_expert):
    rows, topk = experts.shape
    hits = jnp.zeros(slot_expert.shape, f32)
    for k in range(topk):
        hits = jnp.where(experts[:, k : k + 1] == slot_expert, 1.0, hits)
    earlier = (iota((rows, rows), 1) < iota((rows, rows), 0)).astype(f32).astype(bf16)
    rank = dot(earlier, hits.astype(bf16))
    return hits, rank


def start_all(pairs, sem):
    copies = [
        pltpu.make_async_copy(source, target, sem.at[i]) for i, (source, target) in enumerate(pairs)
    ]
    for copy in copies:
        copy.start()
    return copies


def pieces_of(source, target, count):
    size = source.shape[0] // count
    return [
        (source.at[pl.ds(i * size, size)], target.at[pl.ds(i * size, size)]) for i in range(count)
    ]


def front_kernel(*refs, page, local):
    sources, refs = refs[:13], refs[13:]
    packed_ref, hidden_ref, normed_ref = refs[:3]
    targets, refs = refs[3:16], refs[16:]
    query, prob, attended, sem = refs
    pool_hbm, weight_hbm = sources[-2:]
    (
        lengths_ref,
        table_in,
        experts_in,
        queries_ref,
        query_gain_ref,
        keys_ref,
        key_gain_ref,
        values_ref,
        gates_ref,
        residual_ref,
        post_gain_ref,
        pool,
        weight,
    ) = targets
    rows, width = queries_ref.shape
    head = keys_ref.shape[1]
    heads = width // head
    tokens = pool.shape[0]
    context = 256
    chunks = tokens // context
    pool_parts = 3
    weight_parts = 4
    third = tokens // pool_parts
    quarter = width // weight_parts
    side = lax.axis_index("side")
    pairs = list(zip(sources, targets))
    copies = start_all(
        pairs[:7]
        + pieces_of(pool_hbm, pool, pool_parts)
        + pairs[7:11]
        + pieces_of(weight_hbm, weight, weight_parts),
        sem,
    )
    pool_copies = copies[7 : 7 + pool_parts]
    late_copies = copies[7 + pool_parts : 11 + pool_parts]
    weight_copies = copies[11 + pool_parts :]
    for copy in copies[:7]:
        copy.wait()
    table = table_in[...].T

    scale = head ** (-0.5)
    key_normed = rms_scale(keys_ref[...].astype(f32), key_gain_ref[...]).astype(bf16).astype(f32)
    own = []
    for h in range(heads):
        part = queries_ref[:, h * head : (h + 1) * head].astype(f32)
        normed = rms_scale(part, query_gain_ref[...]).astype(bf16)
        query[h * rows : (h + 1) * rows, :] = normed
        own.append(jnp.sum(normed.astype(f32) * key_normed, axis=-1, keepdims=True))
    own_weight = jnp.exp(jnp.concatenate(own, axis=0) * scale)

    same = iota((rows, rows), 0) == iota((rows, rows), 1)
    lengths = jnp.sum(
        jnp.where(same, jnp.broadcast_to(lengths_ref[...], (rows, rows)), 0), axis=1, keepdims=True
    )
    total = jnp.zeros((heads * rows, context), f32)
    for c in range(chunks):
        if (c * context) % third == 0:
            pool_copies[c * context // third].wait()
        at = pl.ds(c * context, context)
        token = iota((rows, context), 1) + c * context
        token_page = token // page
        token_in = token % page
        valid = jnp.zeros((rows, context), f32)
        for entry in range(table.shape[1]):
            hit = (table[:, entry : entry + 1] == token_page) & (
                token_in + entry * page < lengths
            )
            valid = jnp.where(hit, 1.0, valid)
        scores = lax.dot_general(
            query[...],
            pool[at, :head],
            (((1,), (1,)), ((), ())),
            preferred_element_type=f32,
        )
        weights = jnp.exp(scores * scale)
        weights = (weights.reshape(heads, rows, context) * valid[None]).reshape(
            heads * rows, context
        )
        total = total + weights
        prob[:, at] = weights.astype(bf16)
    mixed = dot(prob[...], pool[:, head:])
    for copy in late_copies:
        copy.wait()
    inverse = 1.0 / (jnp.sum(total, axis=1, keepdims=True) + own_weight)
    new_values = values_ref[...].astype(f32)
    for h in range(heads):
        part = slice(h * rows, (h + 1) * rows)
        value = (mixed[part] + own_weight[part] * new_values) * inverse[part]
        gate = jax.nn.sigmoid(gates_ref[:, h * head : (h + 1) * head].astype(f32))
        attended[:, h * head : (h + 1) * head] = (value * gate).astype(bf16)

    projected = residual_ref[...].astype(f32)
    for i, copy in enumerate(weight_copies):
        copy.wait()
        at = slice(i * quarter, (i + 1) * quarter)
        projected = projected + dot(attended[:, at], weight[at, :])
    hidden = projected.astype(bf16)
    hidden_ref[...] = hidden
    normed = rms_scale(hidden.astype(f32), post_gain_ref[...]).astype(bf16)
    normed_ref[...] = normed

    slots, columns = packed_ref.shape
    parts = width // columns
    mine = local // 2
    slot = iota((rows, slots), 1)
    per = parts * mine
    destination = slot // per
    n_dev = slots // per // 2
    expert = (destination % n_dev) * local + (destination // n_dev) * mine + slot % mine
    hits, rank = expert_hits(experts_in[...].T, expert)
    chosen = jnp.where(rank == side.astype(f32), hits, 0.0)
    slot_part = slot % per // mine
    spread = jnp.concatenate(
        [jnp.where(slot_part == p, chosen, 0.0) for p in range(parts)], axis=0
    )
    stacked = jnp.concatenate(
        [normed[:, p * columns : (p + 1) * columns] for p in range(parts)], axis=0
    )
    packed_ref[...] = dot(spread.T.astype(bf16), stacked).astype(bf16)


def middle_kernel(
    normed_ref,
    hidden_ref,
    experts_hbm,
    weights_hbm,
    mix_hbm,
    shared_gate_hbm,
    shared_up_hbm,
    shared_down_hbm,
    gate_hbm,
    up_hbm,
    down_hbm,
    base_ref,
    spread_ref,
    gate_ref,
    up_ref,
    down_ref,
    experts_in,
    weights_in,
    mix,
    shared_gate,
    shared_up,
    shared_down,
    sem,
    *,
    n_dev,
):
    rows, width = normed_ref.shape
    half = width // 2
    local = gate_hbm.shape[0]
    mine = local // 2
    side = lax.axis_index("side")
    experts_at = pl.ds(side * mine, mine)
    columns_at = pl.ds(pl.multiple_of(side * half, half), half)
    copies = start_all(
        [
            (experts_hbm, experts_in),
            (weights_hbm, weights_in),
            (mix_hbm, mix),
            (shared_gate_hbm, shared_gate),
            (shared_up_hbm, shared_up),
            (shared_down_hbm.at[:, columns_at], shared_down),
            (gate_hbm.at[experts_at], gate_ref),
            (up_hbm.at[experts_at], up_ref),
            (down_hbm.at[experts_at], down_ref),
        ],
        sem,
    )
    for copy in copies[:2]:
        copy.wait()
    experts = experts_in[...].T
    weights = weights_in[...].T
    slots = spread_ref.shape[1]
    per = slots // (2 * n_dev)
    parts = per // local
    slot = iota((rows, slots), 1)
    source = slot // per
    expert = (source % n_dev) * local + (source // n_dev) * mine + slot % mine
    share = weights / jnp.sum(weights, axis=1, keepdims=True)
    spread = jnp.zeros((rows, slots), f32)
    for k in range(experts.shape[1]):
        spread = jnp.where(experts[:, k : k + 1] == expert, share[:, k : k + 1], spread)
    hits, rank = expert_hits(experts, expert)
    sender = slot % (2 * mine) // mine
    spread = jnp.where(rank == sender.astype(f32), spread, 0.0)
    slot_part = slot % per // (2 * mine)
    for p in range(parts):
        piece = jnp.where(slot_part == p, spread, 0.0)
        high = piece.astype(bf16)
        at = 2 * p * rows
        spread_ref[at : at + rows, :] = high
        spread_ref[at + rows : at + 2 * rows, :] = (piece - high.astype(f32)).astype(bf16)

    for copy in copies[2:6]:
        copy.wait()
    normed = normed_ref[...]
    shared_inner = (
        jax.nn.silu(dot(normed, shared_gate[...])) * dot(normed, shared_up[...])
    ).astype(bf16)
    lanes = mix.shape[1]
    logit = jnp.zeros((rows, lanes), f32)
    for i in range(width // lanes):
        logit = logit + normed[:, i * lanes : (i + 1) * lanes].astype(f32) * mix[
            i : i + 1, :
        ].astype(f32)
    scale = jax.nn.sigmoid(jnp.sum(logit, axis=-1, keepdims=True))
    base_ref[...] = hidden_ref[:, columns_at].astype(f32) + scale * dot(
        shared_inner, shared_down[...]
    )
    for copy in copies[6:]:
        copy.wait()


def expert_kernel(received, gate, up, down, sent_ref, taken, result):
    mine, width, inner_width = gate.shape
    slots, columns = received.shape
    parts = width // columns
    rows = slots // (parts * mine)
    half = width // 2
    groups = parts * mine
    block = 32
    inward = group_order(groups, block, True)
    outward = group_order(groups, block, False)

    for b in range(rows // block):
        ordered = dot(inward, received[b * groups * block : (b + 1) * groups * block, :]).astype(
            bf16
        )
        for p in range(parts):
            for j in range(mine):
                at = (p * mine + j) * block
                taken[j, b * block : (b + 1) * block, p * columns : (p + 1) * columns] = ordered[
                    at : at + block
                ]
    for j in range(mine):
        inner = (jax.nn.silu(dot(taken[j], gate[j])) * dot(taken[j], up[j])).astype(bf16)
        result[j] = dot(inner, down[j]).astype(bf16)

    n_dev = rows // 2
    for t in range(2):
        for b in range(n_dev // block):
            gathered = jnp.concatenate(
                [
                    result[
                        j,
                        s * n_dev + b * block : s * n_dev + (b + 1) * block,
                        t * half + p * columns : t * half + (p + 1) * columns,
                    ]
                    for p in range(half // columns)
                    for s in range(2)
                    for j in range(mine)
                ],
                axis=0,
            )
            at = (t * n_dev + b * block) * groups
            sent_ref[at : at + groups * block, :] = dot(outward, gathered).astype(bf16)


def combine_kernel(spread_ref, base_ref, returned, out_ref):
    rows, half = base_ref.shape
    columns = returned.shape[1]
    routed = dot(spread_ref[...], returned[...])
    for p in range(half // columns):
        at = 2 * p * rows
        value = routed[at : at + rows] + routed[at + rows : at + 2 * rows]
        out_ref[:, p * columns : (p + 1) * columns] = (
            base_ref[:, p * columns : (p + 1) * columns] + value
        ).astype(bf16)


VMEM = pl.BlockSpec(memory_space=pltpu.VMEM)
HBM = pl.BlockSpec(memory_space=pltpu.HBM)


def exchange(value):
    return lax.all_to_all(value, ("side", "dev"), split_axis=0, concat_axis=0, tiled=True)


def on_device(
    out_gates,
    queries,
    keys_new,
    values_new,
    lengths,
    page_table,
    cache_pool,
    query_gain,
    key_gain,
    out_weight,
    residual,
    post_gain,
    experts,
    route_weights,
    gate_weight,
    up_weight,
    down_weight,
    shared_gate,
    shared_up,
    shared_down,
    shared_mix,
):
    n_dev = lax.axis_size("dev")
    local, width, inner_width = gate_weight.shape
    rows = queries.shape[0]
    head = keys_new.shape[1]
    heads = width // head
    pages, page, both = cache_pool.shape
    tokens = pages * page
    mine = local // 2
    columns = width * mine // 8
    slots = 2 * n_dev * 8
    sources = (
        lengths[None, :],
        page_table.T,
        experts.T,
        queries,
        query_gain[None, :],
        keys_new,
        key_gain[None, :],
        values_new,
        out_gates,
        residual,
        post_gain[None, :],
        cache_pool.reshape(tokens, both),
        out_weight,
    )
    packed, hidden, normed = pl.pallas_call(
        functools.partial(front_kernel, page=page, local=local),
        out_shape=(
            jax.ShapeDtypeStruct((slots, columns), bf16),
            jax.ShapeDtypeStruct((rows, width), bf16),
            jax.ShapeDtypeStruct((rows, width), bf16),
        ),
        in_specs=[HBM] * len(sources),
        out_specs=(VMEM, VMEM, VMEM),
        scratch_shapes=[pltpu.VMEM(source.shape, source.dtype) for source in sources]
        + [
            pltpu.VMEM((heads * rows, head), bf16),
            pltpu.VMEM((heads * rows, tokens), bf16),
            pltpu.VMEM((rows, width), bf16),
            pltpu.SemaphoreType.DMA((18,)),
        ],
        compiler_params=pltpu.CompilerParams(vmem_limit_bytes=63 * MIB),
    )(*sources)
    received = exchange(packed)
    half = width // 2
    inner_width = gate_weight.shape[2]
    base, spread, gate, up, down = pl.pallas_call(
        functools.partial(middle_kernel, n_dev=n_dev),
        out_shape=(
            jax.ShapeDtypeStruct((rows, half), f32),
            jax.ShapeDtypeStruct((4 * rows, slots), bf16),
            jax.ShapeDtypeStruct((mine, width, inner_width), bf16),
            jax.ShapeDtypeStruct((mine, width, inner_width), bf16),
            jax.ShapeDtypeStruct((mine, inner_width, width), bf16),
        ),
        in_specs=[VMEM] * 2 + [HBM] * 9,
        out_specs=(VMEM,) * 5,
        scratch_shapes=[
            pltpu.VMEM(experts.T.shape, i32),
            pltpu.VMEM(route_weights.T.shape, f32),
            pltpu.VMEM((width // 128, 128), bf16),
            pltpu.VMEM(shared_gate.shape, bf16),
            pltpu.VMEM(shared_up.shape, bf16),
            pltpu.VMEM((shared_down.shape[0], half), bf16),
            pltpu.SemaphoreType.DMA((9,)),
        ],
        compiler_params=pltpu.CompilerParams(vmem_limit_bytes=44 * MIB),
        cost_estimate=pl.CostEstimate(
            flops=2 * rows * width * 3 * inner_width, bytes_accessed=10 * MIB, transcendentals=0
        ),
    )(
        normed,
        hidden,
        experts.T,
        route_weights.T,
        shared_mix.reshape(width // 128, 128),
        shared_gate,
        shared_up,
        shared_down,
        gate_weight,
        up_weight,
        down_weight,
    )
    sent = pl.pallas_call(
        expert_kernel,
        out_shape=jax.ShapeDtypeStruct((slots, columns), bf16),
        in_specs=[VMEM] * 4,
        out_specs=VMEM,
        scratch_shapes=[
            pltpu.VMEM((mine, 2 * n_dev, width), bf16),
            pltpu.VMEM((mine, 2 * n_dev, width), bf16),
        ],
        compiler_params=pltpu.CompilerParams(vmem_limit_bytes=32 * MIB),
    )(received, gate, up, down)
    returned = exchange(sent)
    return pl.pallas_call(
        combine_kernel,
        out_shape=jax.ShapeDtypeStruct((rows, half), bf16),
        in_specs=[VMEM] * 3,
        out_specs=VMEM,
        compiler_params=pltpu.CompilerParams(vmem_limit_bytes=8 * MIB),
    )(spread, base, returned)


def solution(mesh):
    placed = (
        P("dev", None),
        P("dev", None),
        P("dev", None),
        P("dev", None),
        P("dev"),
        P("dev", None),
        P("dev", None, None),
        P(),
        P(),
        P(),
        P("dev", None),
        P(),
        P("dev", None),
        P("dev", None),
        P("dev", None, None),
        P("dev", None, None),
        P("dev", None, None),
        P(),
        P(),
        P(),
        P(),
    )
    return jax.shard_map(
        on_device, mesh=mesh, in_specs=placed, out_specs=P("dev", "side"), check_vma=False
    )
```

time: 85.6 us -> 66.3 us (0.77)
  waiting for transfers between devices: 33.9 us -> 5.66 us
  blocking collectives: 0 us -> 23.2 us
  local copies, waits for them, and re-layouts: 21.1 us -> 12 us
  starting transfers between devices: 17.2 us -> 11.5 us
  Pallas kernels: 12.5 us -> 13.5 us
    all_to_all x2 -> x1, waiting for transfers between devices: 33.9 us -> 5.66 us  [exchange(): lax.all_to_all(value, ('side', 'dev'), split_axis=0, concat_axis=0, tiled...]
    all_to_all x0 -> x1, blocking collectives: none -> 23.2 us  [exchange(): lax.all_to_all(value, ('side', 'dev'), split_axis=0, concat_axis=0, tiled...]
    unnamed x39 -> x24, local copies, waits for them, and re-layouts: 20.5 us -> 12 us
    all_to_all x2 -> x1, starting transfers between devices: 17.2 us -> 11.5 us  [exchange(): lax.all_to_all(value, ('side', 'dev'), split_axis=0, concat_axis=0, tiled...]
    pallas_call x2 -> x3, Pallas kernels: 5.67 us -> 5.97 us  [the longest x1 3.13 us: on_device(): pl.pallas_call(functools.partial(middle_kernel, n_dev=n_dev), out_shape=(...]
  transfers between devices with their start and end apart: 2 -> 1, of which waited for: 2 -> 1; matrix products, arithmetic and copies ran while one was open for 2% -> 0% of each run, Pallas kernels for 0% -> 5%
where the time goes in v2:
time: 66.3 us; the launch traced here: 65.9 us
  blocking collectives  23.2 us (35%)
  Pallas kernels  13.5 us (20%)
  local copies, waits for them, and re-layouts  12 us (18%)
  starting transfers between devices  11.5 us (17%)
  waiting for transfers between devices  5.66 us (9%)
    all_to_all x1, blocking collectives, exchange(): lax.all_to_all(value, ('side', 'dev'), split_axis=0, concat_axis=0, tiled...  23.2 us
    unnamed x24, local copies, waits for them, and re-layouts  12 us
    all_to_all x1, starting transfers between devices, exchange(): lax.all_to_all(value, ('side', 'dev'), split_axis=0, concat_axis=0, tiled...  11.5 us
    pallas_call x1, Pallas kernels, on_device(): pl.pallas_call(functools.partial(front_kernel, page=page, local=local), o...  7.5 us
    all_to_all x1, waiting for transfers between devices, exchange(): lax.all_to_all(value, ('side', 'dev'), split_axis=0, concat_axis=0, tiled...  5.66 us
    pallas_call x1, Pallas kernels, on_device(): pl.pallas_call(functools.partial(middle_kernel, n_dev=n_dev), out_shape=(...  3.13 us
    pallas_call x1, Pallas kernels, on_device(): pl.pallas_call(expert_kernel, out_shape=jax.ShapeDtypeStruct((slots, colu...  1.89 us
  transfers between devices with their start and end apart: 1, of which 1 were waited for; matrix products, arithmetic and copies ran while one was open for 0% of the time, Pallas kernels for 5%

profile of v2, /device:TPU:1, one launch (start us, length us, event | category | flops | bytes accessed | tf_op | source)
XLA Modules:
  0.0 65.9 jit_solution(7403668079880053311)
XLA Ops:
  0.0 0.0 copy-start.9
  0.0 0.0 copy-start.10
  0.0 7.5 %shard_map.199 = (bf16[1024,512]{1,0:T(8,128)(2,1)}, bf16[32,2048]{1,0:T(8,128)(2,1)}, bf16[32,2048]{1,0:T(8,128)(2,1)}) custom-call(s32[1,32]{1,0:T(1,128)} %bitcast.26, s32[8,32]{1,0:T(8,128)} %bitcast.23, s32[10,32]{1,0:T(8,128)} %bitcast.16, bf16[32,2048]{1,0:T(8,128)(2,1)} %refs_3_.1, f32[1,256]{1,0:T(1,128)} %bitcast.24, bf16[32,256]{1,0:T(8,128)(2,1)} %refs_5_.1, ...), custom_call_target="tpu_custom_call" | custom-call | tf_op jit(solution)/shard_map/pallas_call | solution.py:396
  7.5 11.5 %all-to-all-start = ((bf16[128,8,512]{2,1,0:T(8,128)(2,1)}), bf16[128,8,512]{2,1,0:T(8,128)(2,1)S(1)}, u32[]{:S(2)}, u32[]{:S(2)}) async-start(bf16[128,8,512]{2,1,0:T(8,128)(2,1)} %bitcast.21), calls=%async_computation | async-start | bytes 2097152 | tf_op jit(solution)/shard_map/all_to_all | solution.py:345
  19.0 0.0 copy-done.9
  19.0 0.0 copy-done.10
  19.0 0.0 copy-start.4
  19.1 1.2 %copy-done.4 = bf16[2048,256]{1,0:T(8,128)(2,1)S(1)} copy-done((bf16[2048,256]{1,0:T(8,128)(2,1)S(1)}, bf16[2048,256]{1,0:T(8,128)(2,1)}, u32[]{:S(2)}) %copy-start.4) | copy-done | bytes 1048600
  20.3 0.0 copy-start.5
  20.3 1.2 %copy-done.5 = bf16[2048,256]{1,0:T(8,128)(2,1)S(1)} copy-done((bf16[2048,256]{1,0:T(8,128)(2,1)S(1)}, bf16[2048,256]{1,0:T(8,128)(2,1)}, u32[]{:S(2)}) %copy-start.5) | copy-done | bytes 1048600
  21.5 0.0 copy-start.6
  21.5 1.2 %copy-done.6 = bf16[256,2048]{1,0:T(8,128)(2,1)S(1)} copy-done((bf16[256,2048]{1,0:T(8,128)(2,1)S(1)}, bf16[256,2048]{1,0:T(8,128)(2,1)}, u32[]{:S(2)}) %copy-start.6) | copy-done | bytes 1048600
  22.7 0.0 copy-start.7
  22.7 0.9 %copy-done.7 = bf16[32,2048]{1,0:T(8,128)(2,1)S(1)} copy-done((bf16[32,2048]{1,0:T(8,128)(2,1)S(1)}, bf16[32,2048]{1,0:T(8,128)(2,1)}, u32[]{:S(2)}) %copy-start.7) | copy-done | bytes 131096
  23.6 0.0 copy-start.8
  23.6 0.9 %copy-done.8 = bf16[32,2048]{1,0:T(8,128)(2,1)S(1)} copy-done((bf16[32,2048]{1,0:T(8,128)(2,1)S(1)}, bf16[32,2048]{1,0:T(8,128)(2,1)}, u32[]{:S(2)}) %copy-start.8) | copy-done | bytes 131096
  24.5 0.0 copy-start.11
  24.5 0.7 %copy-done.11 = bf16[2048]{0:T(1024)(128)(2,1)S(1)} copy-done((bf16[2048]{0:T(1024)(128)(2,1)S(1)}, bf16[2048]{0:T(1024)(128)(2,1)}, u32[]{:S(2)}) %copy-start.11) | copy-done | bytes 4120
  25.2 3.1 %shard_map.200 = (f32[32,1024]{1,0:T(8,128)S(1)}, bf16[128,1024]{1,0:T(8,128)(2,1)S(1)}, bf16[2,2048,256]{2,1,0:T(8,128)(2,1)S(1)}, bf16[2,2048,256]{2,1,0:T(8,128)(2,1)S(1)}, bf16[2,256,2048]{2,1,0:T(8,128)(2,1)S(1)}) custom-call(bf16[32,2048]{1,0:T(8,128)(2,1)S(1)} %copy-done.8, bf16[32,2048]{1,0:T(8,128)(2,1)S(1)} %copy-done.7, s32[10,32]{1,0:T(8,128)S(1)} %bitcast.17, ...), custom_call_target="tpu_custom_call" | custom-call | flops 100663296 | bytes 10485760 | tf_op jit(solution)/shard_map/pallas_call | solution.py:417
  28.4 0.0 copy-start
  28.4 1.3 %copy-done = bf16[2,2048,256]{2,1,0:T(8,128)(2,1)} copy-done((bf16[2,2048,256]{2,1,0:T(8,128)(2,1)}, bf16[2,2048,256]{2,1,0:T(8,128)(2,1)S(1)}, u32[]{:S(2)}) %copy-start) | copy-done | bytes 2097176
  29.7 0.0 copy-start.2
  29.7 1.3 %copy-done.2 = bf16[2,256,2048]{2,1,0:T(8,128)(2,1)} copy-done((bf16[2,256,2048]{2,1,0:T(8,128)(2,1)}, bf16[2,256,2048]{2,1,0:T(8,128)(2,1)S(1)}, u32[]{:S(2)}) %copy-start.2) | copy-done | bytes 2097176
  31.0 5.7 %all-to-all-done = bf16[128,8,512]{2,1,0:T(8,128)(2,1)S(1)} async-done(((bf16[128,8,512]{2,1,0:T(8,128)(2,1)}), bf16[128,8,512]{2,1,0:T(8,128)(2,1)S(1)}, u32[]{:S(2)}, u32[]{:S(2)}) %all-to-all-start) | async-done | bytes 1048608 | tf_op jit(solution)/shard_map/all_to_all | solution.py:345
  36.7 0.0 copy-start.1
  36.7 1.6 %copy-done.1 = bf16[2,2048,256]{2,1,0:T(8,128)(2,1)S(1)} copy-done((bf16[2,2048,256]{2,1,0:T(8,128)(2,1)S(1)}, bf16[2,2048,256]{2,1,0:T(8,128)(2,1)}, u32[]{:S(2)}) %copy-start.1) | copy-done | bytes 2097176
  38.3 0.0 copy-start.3
  38.3 1.6 %copy-done.3 = bf16[2,256,2048]{2,1,0:T(8,128)(2,1)S(1)} copy-done((bf16[2,256,2048]{2,1,0:T(8,128)(2,1)S(1)}, bf16[2,256,2048]{2,1,0:T(8,128)(2,1)}, u32[]{:S(2)}) %copy-start.3) | copy-done | bytes 2097176
  39.9 1.9 %shard_map.201 = bf16[1024,512]{1,0:T(8,128)(2,1)S(1)} custom-call(bf16[1024,512]{1,0:T(8,128)(2,1)S(1)} %bitcast.14, bf16[2,2048,256]{2,1,0:T(8,128)(2,1)S(1)} %get-tuple-element.18.gate, bf16[2,2048,256]{2,1,0:T(8,128)(2,1)S(1)} %copy-done.1, bf16[2,256,2048]{2,1,0:T(8,128)(2,1)S(1)} %copy-done.3), custom_call_target="tpu_custom_call" | custom-call | tf_op jit(solution)/shard_map/pallas_call | solution.py:454
  41.8 23.2 %all_to_all.22 = bf16[128,8,512]{2,1,0:T(8,128)(2,1)S(1)} all-to-all(bf16[128,8,512]{2,1,0:T(8,128)(2,1)S(1)} %bitcast.15), channel_id=1, replica_groups=mesh['side'=2,'dev'=64] {'side','dev'}, dimensions={0} | all-to-all | bytes 2097152 | tf_op jit(solution)/shard_map/all_to_all | solution.py:345
  64.9 0.9 %shard_map.202 = bf16[32,1024]{1,0:T(8,128)(2,1)} custom-call(bf16[128,1024]{1,0:T(8,128)(2,1)S(1)} %get-tuple-element.15.spread_ref, f32[32,1024]{1,0:T(8,128)S(1)} %get-tuple-element.16.base_ref, bf16[1024,512]{1,0:T(8,128)(2,1)S(1)} %bitcast.13), custom_call_target="tpu_custom_call" | custom-call | tf_op jit(solution)/shard_map/pallas_call | solution.py:466
Async XLA Ops:
  0.0 19.0 %copy-start.9 = (s32[32,10]{0,1:T(8,128)S(1)}, s32[32,10]{0,1:T(8,128)}, u32[]{:S(2)}) copy-start(s32[32,10]{0,1:T(8,128)} %param.33) | copy-start | bytes 3844
  0.0 19.0 %copy-start.10 = (f32[32,10]{0,1:T(8,128)S(1)}, f32[32,10]{0,1:T(8,128)}, u32[]{:S(2)}) copy-start(f32[32,10]{0,1:T(8,128)} %param.34) | copy-start | bytes 3844
  7.5 29.2 %all-to-all-start = ((bf16[128,8,512]{2,1,0:T(8,128)(2,1)}), bf16[128,8,512]{2,1,0:T(8,128)(2,1)S(1)}, u32[]{:S(2)}, u32[]{:S(2)}) async-start(bf16[128,8,512]{2,1,0:T(8,128)(2,1)} %bitcast.21), calls=%async_computation | async-start | bytes 2097152 | tf_op jit(solution)/shard_map/all_to_all | solution.py:345
  19.0 1.2 %copy-start.4 = (bf16[2048,256]{1,0:T(8,128)(2,1)S(1)}, bf16[2048,256]{1,0:T(8,128)(2,1)}, u32[]{:S(2)}) copy-start(bf16[2048,256]{1,0:T(8,128)(2,1)} %shared_gate_hbm.1) | copy-start | bytes 3145732
  20.3 1.2 %copy-start.5 = (bf16[2048,256]{1,0:T(8,128)(2,1)S(1)}, bf16[2048,256]{1,0:T(8,128)(2,1)}, u32[]{:S(2)}) copy-start(bf16[2048,256]{1,0:T(8,128)(2,1)} %shared_up_hbm.1) | copy-start | bytes 3145732
  21.5 1.2 %copy-start.6 = (bf16[256,2048]{1,0:T(8,128)(2,1)S(1)}, bf16[256,2048]{1,0:T(8,128)(2,1)}, u32[]{:S(2)}) copy-start(bf16[256,2048]{1,0:T(8,128)(2,1)} %shared_down_hbm.1) | copy-start | bytes 3145732
  22.7 0.9 %copy-start.7 = (bf16[32,2048]{1,0:T(8,128)(2,1)S(1)}, bf16[32,2048]{1,0:T(8,128)(2,1)}, u32[]{:S(2)}) copy-start(bf16[32,2048]{1,0:T(8,128)(2,1)} %get-tuple-element.14.hidden_ref) | copy-start | bytes 393220
  23.6 0.9 %copy-start.8 = (bf16[32,2048]{1,0:T(8,128)(2,1)S(1)}, bf16[32,2048]{1,0:T(8,128)(2,1)}, u32[]{:S(2)}) copy-start(bf16[32,2048]{1,0:T(8,128)(2,1)} %get-tuple-element.13.normed_ref) | copy-start | bytes 393220
  24.5 0.7 %copy-start.11 = (bf16[2048]{0:T(1024)(128)(2,1)S(1)}, bf16[2048]{0:T(1024)(128)(2,1)}, u32[]{:S(2)}) copy-start(bf16[2048]{0:T(1024)(128)(2,1)} %param.41) | copy-start | bytes 12292
  28.4 1.3 %copy-start = (bf16[2,2048,256]{2,1,0:T(8,128)(2,1)}, bf16[2,2048,256]{2,1,0:T(8,128)(2,1)S(1)}, u32[]{:S(2)}) copy-start(bf16[2,2048,256]{2,1,0:T(8,128)(2,1)S(1)} %get-tuple-element.19.up) | copy-start | bytes 6291460
  29.7 1.3 %copy-start.2 = (bf16[2,256,2048]{2,1,0:T(8,128)(2,1)}, bf16[2,256,2048]{2,1,0:T(8,128)(2,1)S(1)}, u32[]{:S(2)}) copy-start(bf16[2,256,2048]{2,1,0:T(8,128)(2,1)S(1)} %get-tuple-element.20.down) | copy-start | bytes 6291460
  36.7 1.6 %copy-start.1 = (bf16[2,2048,256]{2,1,0:T(8,128)(2,1)S(1)}, bf16[2,2048,256]{2,1,0:T(8,128)(2,1)}, u32[]{:S(2)}) copy-start(bf16[2,2048,256]{2,1,0:T(8,128)(2,1)} %copy-done) | copy-start | bytes 6291460
  38.3 1.6 %copy-start.3 = (bf16[2,256,2048]{2,1,0:T(8,128)(2,1)S(1)}, bf16[2,256,2048]{2,1,0:T(8,128)(2,1)}, u32[]{:S(2)}) copy-start(bf16[2,256,2048]{2,1,0:T(8,128)(2,1)} %copy-done.2) | copy-start | bytes 6291460

commit v3 on v2

--- a/solution.py
+++ b/solution.py
@@ -60,11 +60,11 @@
 
 
 def front_kernel(*refs, page, local):
-    sources, refs = refs[:13], refs[13:]
-    packed_ref, hidden_ref, normed_ref = refs[:3]
-    targets, refs = refs[3:16], refs[16:]
-    query, prob, attended, sem = refs
-    pool_hbm, weight_hbm = sources[-2:]
+    sources, refs = refs[:12], refs[12:]
+    packed_ref, hidden_ref, attended, refs = *refs[:3], refs[3:]
+    targets, refs = refs[:12], refs[12:]
+    query, prob, valid, chosen, sem = refs
+    residual_hbm, pool_hbm, weight_hbm = sources[-3:]
     (
         lengths_ref,
         table_in,
@@ -76,35 +76,71 @@
         values_ref,
         gates_ref,
         residual_ref,
-        post_gain_ref,
         pool,
         weight,
     ) = targets
     rows, width = queries_ref.shape
+    half = width // 2
     head = keys_ref.shape[1]
     heads = width // head
     tokens = pool.shape[0]
     context = 256
     chunks = tokens // context
-    pool_parts = 3
     weight_parts = 4
-    third = tokens // pool_parts
     quarter = width // weight_parts
     side = lax.axis_index("side")
+    columns_at = pl.ds(pl.multiple_of(side * half, half), half)
     pairs = list(zip(sources, targets))
     copies = start_all(
         pairs[:7]
-        + pieces_of(pool_hbm, pool, pool_parts)
-        + pairs[7:11]
-        + pieces_of(weight_hbm, weight, weight_parts),
+        + pieces_of(pool_hbm, pool, chunks)
+        + pairs[7:9]
+        + [(residual_hbm.at[:, columns_at], residual_ref)]
+        + [
+            (source.at[:, columns_at], target)
+            for source, target in pieces_of(weight_hbm, weight, weight_parts)
+        ],
         sem,
     )
-    pool_copies = copies[7 : 7 + pool_parts]
-    late_copies = copies[7 + pool_parts : 11 + pool_parts]
-    weight_copies = copies[11 + pool_parts :]
+    pool_copies = copies[7 : 7 + chunks]
+    late_copies = copies[7 + chunks : 10 + chunks]
+    weight_copies = copies[10 + chunks :]
     for copy in copies[:7]:
         copy.wait()
+
+    slots, columns = packed_ref.shape
+    parts = half // columns
+    mine = local // 2
+    slot = iota((rows, slots), 1)
+    per = parts * 2 * mine
+    destination = slot // per
+    n_dev = slots // per // 2
+    expert = (destination % n_dev) * local + (destination // n_dev) * mine + slot % mine
+    hits, rank = expert_hits(experts_in[...].T, expert)
+    slot_rank = slot % (2 * mine) // mine
+    picked = jnp.where(rank == slot_rank.astype(f32), hits, 0.0)
+    slot_part = slot % per // (2 * mine)
+    picked = jnp.concatenate(
+        [jnp.where(slot_part == p, picked, 0.0) for p in range(parts)], axis=0
+    )
+    chosen[...] = picked.T.astype(bf16)
+
     table = table_in[...].T
+    same = iota((rows, rows), 0) == iota((rows, rows), 1)
+    lengths = jnp.sum(
+        jnp.where(same, jnp.broadcast_to(lengths_ref[...], (rows, rows)), 0), axis=1, keepdims=True
+    )
+    for c in range(chunks):
+        token = iota((rows, context), 1) + c * context
+        token_page = token // page
+        token_in = token % page
+        mask = jnp.zeros((rows, context), f32)
+        for entry in range(table.shape[1]):
+            hit = (table[:, entry : entry + 1] == token_page) & (
+                token_in + entry * page < lengths
+            )
+            mask = jnp.where(hit, 1.0, mask)
+        valid[:, c * context : (c + 1) * context] = mask
 
     scale = head ** (-0.5)
     key_normed = rms_scale(keys_ref[...].astype(f32), key_gain_ref[...]).astype(bf16).astype(f32)
@@ -116,24 +152,10 @@
         own.append(jnp.sum(normed.astype(f32) * key_normed, axis=-1, keepdims=True))
     own_weight = jnp.exp(jnp.concatenate(own, axis=0) * scale)
 
-    same = iota((rows, rows), 0) == iota((rows, rows), 1)
-    lengths = jnp.sum(
-        jnp.where(same, jnp.broadcast_to(lengths_ref[...], (rows, rows)), 0), axis=1, keepdims=True
-    )
     total = jnp.zeros((heads * rows, context), f32)
     for c in range(chunks):
-        if (c * context) % third == 0:
-            pool_copies[c * context // third].wait()
-        at = pl.ds(c * context, context)
-        token = iota((rows, context), 1) + c * context
-        token_page = token // page
-        token_in = token % page
-        valid = jnp.zeros((rows, context), f32)
-        for entry in range(table.shape[1]):
-            hit = (table[:, entry : entry + 1] == token_page) & (
-                token_in + entry * page < lengths
-            )
-            valid = jnp.where(hit, 1.0, valid)
+        pool_copies[c].wait()
+        at = slice(c * context, (c + 1) * context)
         scores = lax.dot_general(
             query[...],
             pool[at, :head],
@@ -141,7 +163,7 @@
             preferred_element_type=f32,
         )
         weights = jnp.exp(scores * scale)
-        weights = (weights.reshape(heads, rows, context) * valid[None]).reshape(
+        weights = (weights.reshape(heads, rows, context) * valid[:, at][None]).reshape(
             heads * rows, context
         )
         total = total + weights
@@ -164,68 +186,58 @@
         projected = projected + dot(attended[:, at], weight[at, :])
     hidden = projected.astype(bf16)
     hidden_ref[...] = hidden
-    normed = rms_scale(hidden.astype(f32), post_gain_ref[...]).astype(bf16)
-    normed_ref[...] = normed
-
-    slots, columns = packed_ref.shape
-    parts = width // columns
-    mine = local // 2
-    slot = iota((rows, slots), 1)
-    per = parts * mine
-    destination = slot // per
-    n_dev = slots // per // 2
-    expert = (destination % n_dev) * local + (destination // n_dev) * mine + slot % mine
-    hits, rank = expert_hits(experts_in[...].T, expert)
-    chosen = jnp.where(rank == side.astype(f32), hits, 0.0)
-    slot_part = slot % per // mine
-    spread = jnp.concatenate(
-        [jnp.where(slot_part == p, chosen, 0.0) for p in range(parts)], axis=0
-    )
     stacked = jnp.concatenate(
-        [normed[:, p * columns : (p + 1) * columns] for p in range(parts)], axis=0
-    )
-    packed_ref[...] = dot(spread.T.astype(bf16), stacked).astype(bf16)
-
-
-def middle_kernel(
-    normed_ref,
-    hidden_ref,
-    experts_hbm,
-    weights_hbm,
-    mix_hbm,
-    shared_gate_hbm,
-    shared_up_hbm,
-    shared_down_hbm,
-    gate_hbm,
-    up_hbm,
-    down_hbm,
-    base_ref,
-    spread_ref,
-    gate_ref,
-    up_ref,
-    down_ref,
-    experts_in,
-    weights_in,
-    mix,
-    shared_gate,
-    shared_up,
-    shared_down,
-    sem,
-    *,
-    n_dev,
-):
-    rows, width = normed_ref.shape
+        [hidden[:, p * columns : (p + 1) * columns] for p in range(parts)], axis=0
+    )
+    packed_ref[...] = dot(chosen[...], stacked).astype(bf16)
+
+
+def middle_kernel(*refs, n_dev):
+    (
+        attended,
+        hidden_ref,
+        experts_hbm,
+        weights_hbm,
+        mix_hbm,
+        residual_hbm,
+        post_gain_hbm,
+        out_weight_hbm,
+        shared_gate_hbm,
+        shared_up_hbm,
+        shared_down_hbm,
+        gate_hbm,
+        up_hbm,
+        down_hbm,
+    ) = refs[:14]
+    base_ref, spread_ref, post_gain, gate_ref, up_ref, down_ref = refs[14:20]
+    (
+        experts_in,
+        weights_in,
+        mix,
+        residual,
+        out_weight,
+        shared_gate,
+        shared_up,
+        shared_down,
+        hidden,
+        sem,
+    ) = refs[20:]
+    rows, width = hidden.shape
     half = width // 2
     local = gate_hbm.shape[0]
     mine = local // 2
     side = lax.axis_index("side")
     experts_at = pl.ds(side * mine, mine)
     columns_at = pl.ds(pl.multiple_of(side * half, half), half)
+    others_at = pl.ds(pl.multiple_of((1 - side) * half, half), half)
     copies = start_all(
         [
             (experts_hbm, experts_in),
             (weights_hbm, weights_in),
             (mix_hbm, mix),
+            (residual_hbm.at[:, others_at], residual),
+            (post_gain_hbm, post_gain),
+            (out_weight_hbm.at[:, others_at], out_weight),
             (shared_gate_hbm, shared_gate),
             (shared_up_hbm, shared_up),
             (shared_down_hbm.at[:, columns_at], shared_down),
@@ -250,8 +262,8 @@
     for k in range(experts.shape[1]):
         spread = jnp.where(experts[:, k : k + 1] == expert, share[:, k : k + 1], spread)
     hits, rank = expert_hits(experts, expert)
-    sender = slot % (2 * mine) // mine
-    spread = jnp.where(rank == sender.astype(f32), spread, 0.0)
+    slot_rank = slot % (2 * mine) // mine
+    spread = jnp.where(rank == slot_rank.astype(f32), spread, 0.0)
     slot_part = slot % per // (2 * mine)
     for p in range(parts):
         piece = jnp.where(slot_part == p, spread, 0.0)
@@ -260,9 +272,14 @@
         spread_ref[at : at + rows, :] = high
         spread_ref[at + rows : at + 2 * rows, :] = (piece - high.astype(f32)).astype(bf16)
 
-    for copy in copies[2:6]:
+    for copy in copies[2:9]:
         copy.wait()
-    normed = normed_ref[...]
+    mine_hidden = hidden_ref[...]
+    hidden[:, columns_at] = mine_hidden
+    hidden[:, others_at] = (
+        residual[...].astype(f32) + dot(attended[...], out_weight[...])
+    ).astype(bf16)
+    normed = rms_scale(hidden[...].astype(f32), post_gain[...]).astype(bf16)
     shared_inner = (
         jax.nn.silu(dot(normed, shared_gate[...])) * dot(normed, shared_up[...])
     ).astype(bf16)
@@ -273,50 +290,51 @@
             i : i + 1, :
         ].astype(f32)
     scale = jax.nn.sigmoid(jnp.sum(logit, axis=-1, keepdims=True))
-    base_ref[...] = hidden_ref[:, columns_at].astype(f32) + scale * dot(
-        shared_inner, shared_down[...]
-    )
-    for copy in copies[6:]:
+    base_ref[...] = mine_hidden.astype(f32) + scale * dot(shared_inner, shared_down[...])
+    for copy in copies[9:]:
         copy.wait()
 
 
-def expert_kernel(received, gate, up, down, sent_ref, taken, result):
+def expert_kernel(received, post_gain, gate, up, down, sent_ref, taken, result):
     mine, width, inner_width = gate.shape
     slots, columns = received.shape
-    parts = width // columns
-    rows = slots // (parts * mine)
     half = width // 2
-    groups = parts * mine
+    parts = half // columns
+    groups = parts * 2 * mine
+    n_dev = slots // groups // 2
     block = 32
     inward = group_order(groups, block, True)
     outward = group_order(groups, block, False)
 
-    for b in range(rows // block):
-        ordered = dot(inward, received[b * groups * block : (b + 1) * groups * block, :]).astype(
-            bf16
-        )
-        for p in range(parts):
-            for j in range(mine):
-                at = (p * mine + j) * block
-                taken[j, b * block : (b + 1) * block, p * columns : (p + 1) * columns] = ordered[
-                    at : at + block
-                ]
+    for s in range(2):
+        for b in range(n_dev // block):
+            at = (s * n_dev + b * block) * groups
+            ordered = dot(inward, received[at : at + groups * block, :]).astype(bf16)
+            for p in range(parts):
+                for r in range(2):
+                    for j in range(mine):
+                        at = ((p * 2 + r) * mine + j) * block
+                        row = r * n_dev + b * block
+                        column = s * half + p * columns
+                        taken[j, row : row + block, column : column + columns] = ordered[
+                            at : at + block
+                        ]
     for j in range(mine):
-        inner = (jax.nn.silu(dot(taken[j], gate[j])) * dot(taken[j], up[j])).astype(bf16)
+        normed = rms_scale(taken[j].astype(f32), post_gain[...]).astype(bf16)
+        inner = (jax.nn.silu(dot(normed, gate[j])) * dot(normed, up[j])).astype(bf16)
         result[j] = dot(inner, down[j]).astype(bf16)
 
-    n_dev = rows // 2
     for t in range(2):
         for b in range(n_dev // block):
             gathered = jnp.concatenate(
                 [
                     result[
                         j,
-                        s * n_dev + b * block : s * n_dev + (b + 1) * block,
+                        r * n_dev + b * block : r * n_dev + (b + 1) * block,
                         t * half + p * columns : t * half + (p + 1) * columns,
                     ]
-                    for p in range(half // columns)
-                    for s in range(2)
+                    for p in range(parts)
+                    for r in range(2)
                     for j in range(mine)
                 ],
                 axis=0,
@@ -378,6 +396,8 @@
     mine = local // 2
     columns = width * mine // 8
     slots = 2 * n_dev * 8
+    half = width // 2
+    inner_width = gate_weight.shape[2]
     sources = (
         lengths[None, :],
         page_table.T,
@@ -389,61 +409,71 @@
         values_new,
         out_gates,
         residual,
-        post_gain[None, :],
         cache_pool.reshape(tokens, both),
         out_weight,
     )
-    packed, hidden, normed = pl.pallas_call(
+    held = [pltpu.VMEM(source.shape, source.dtype) for source in sources]
+    held[9] = pltpu.VMEM((rows, half), bf16)
+    held[11] = pltpu.VMEM((width, half), bf16)
+    packed, hidden, attended = pl.pallas_call(
         functools.partial(front_kernel, page=page, local=local),
         out_shape=(
             jax.ShapeDtypeStruct((slots, columns), bf16),
-            jax.ShapeDtypeStruct((rows, width), bf16),
+            jax.ShapeDtypeStruct((rows, half), bf16),
             jax.ShapeDtypeStruct((rows, width), bf16),
         ),
         in_specs=[HBM] * len(sources),
         out_specs=(VMEM, VMEM, VMEM),
-        scratch_shapes=[pltpu.VMEM(source.shape, source.dtype) for source in sources]
+        scratch_shapes=held
         + [
             pltpu.VMEM((heads * rows, head), bf16),
             pltpu.VMEM((heads * rows, tokens), bf16),
-            pltpu.VMEM((rows, width), bf16),
-            pltpu.SemaphoreType.DMA((18,)),
+            pltpu.VMEM((rows, tokens), f32),
+            pltpu.VMEM((slots, half // columns * rows), bf16),
+            pltpu.SemaphoreType.DMA((14 + tokens // 256,)),
         ],
         compiler_params=pltpu.CompilerParams(vmem_limit_bytes=63 * MIB),
     )(*sources)
     received = exchange(packed)
-    half = width // 2
-    inner_width = gate_weight.shape[2]
-    base, spread, gate, up, down = pl.pallas_call(
+    base, spread, gain, gate, up, down = pl.pallas_call(
         functools.partial(middle_kernel, n_dev=n_dev),
         out_shape=(
             jax.ShapeDtypeStruct((rows, half), f32),
             jax.ShapeDtypeStruct((4 * rows, slots), bf16),
+            jax.ShapeDtypeStruct((1, width), f32),
             jax.ShapeDtypeStruct((mine, width, inner_width), bf16),
             jax.ShapeDtypeStruct((mine, width, inner_width), bf16),
             jax.ShapeDtypeStruct((mine, inner_width, width), bf16),
         ),
-        in_specs=[VMEM] * 2 + [HBM] * 9,
-        out_specs=(VMEM,) * 5,
+        in_specs=[VMEM] * 2 + [HBM] * 12,
+        out_specs=(VMEM,) * 6,
         scratch_shapes=[
             pltpu.VMEM(experts.T.shape, i32),
             pltpu.VMEM(route_weights.T.shape, f32),
             pltpu.VMEM((width // 128, 128), bf16),
+            pltpu.VMEM((rows, half), bf16),
+            pltpu.VMEM((width, half), bf16),
             pltpu.VMEM(shared_gate.shape, bf16),
             pltpu.VMEM(shared_up.shape, bf16),
             pltpu.VMEM((shared_down.shape[0], half), bf16),
-            pltpu.SemaphoreType.DMA((9,)),
+            pltpu.VMEM((rows, width), bf16),
+            pltpu.SemaphoreType.DMA((12,)),
         ],
-        compiler_params=pltpu.CompilerParams(vmem_limit_bytes=44 * MIB),
+        compiler_params=pltpu.CompilerParams(vmem_limit_bytes=40 * MIB),
         cost_estimate=pl.CostEstimate(
-            flops=2 * rows * width * 3 * inner_width, bytes_accessed=10 * MIB, transcendentals=0
+            flops=2 * rows * width * (half + 3 * inner_width),
+            bytes_accessed=14 * MIB,
+            transcendentals=0,
         ),
     )(
-        normed,
+        attended,
         hidden,
         experts.T,
         route_weights.T,
         shared_mix.reshape(width // 128, 128),
+        residual,
+        post_gain[None, :],
+        out_weight,
         shared_gate,
         shared_up,
         shared_down,
@@ -454,14 +484,14 @@
     sent = pl.pallas_call(
         expert_kernel,
         out_shape=jax.ShapeDtypeStruct((slots, columns), bf16),
-        in_specs=[VMEM] * 4,
+        in_specs=[VMEM] * 5,
         out_specs=VMEM,
         scratch_shapes=[
             pltpu.VMEM((mine, 2 * n_dev, width), bf16),
             pltpu.VMEM((mine, 2 * n_dev, width), bf16),
         ],
-        compiler_params=pltpu.CompilerParams(vmem_limit_bytes=32 * MIB),
-    )(received, gate, up, down)
+        compiler_params=pltpu.CompilerParams(vmem_limit_bytes=24 * MIB),
+    )(received, gain, gate, up, down)
     returned = exchange(sent)
     return pl.pallas_call(
         combine_kernel,

time: 66.3 us -> 71.3 us (1.075)
  waiting for transfers between devices: 5.66 us -> 0.82 us
  local copies, waits for them, and re-layouts: 12 us -> 16.8 us
  blocking collectives: 23.2 us -> 26.4 us
  Pallas kernels: 13.5 us -> 15.1 us
    all_to_all x1, waiting for transfers between devices: 5.66 us -> 0.82 us  [exchange(): lax.all_to_all(value, ('side', 'dev'), split_axis=0, concat_axis=0, tiled...]
    unnamed x24 -> x38, local copies, waits for them, and re-layouts: 12 us -> 16.8 us
    all_to_all x1, blocking collectives: 23.2 us -> 26.4 us  [exchange(): lax.all_to_all(value, ('side', 'dev'), split_axis=0, concat_axis=0, tiled...]
    pallas_call x1, Pallas kernels: 3.13 us -> 3.9 us  [on_device(): pl.pallas_call(functools.partial(middle_kernel, n_dev=n_dev), out_shape=(...]
  transfers between devices with their start and end apart: 1 -> 1, of which waited for: 1 -> 1; matrix products, arithmetic and copies ran while one was open for 0% -> 0% of each run, Pallas kernels for 5% -> 6%
where the time goes in v3:
time: 71.3 us; the launch traced here: 70.7 us
  blocking collectives  26.4 us (37%)
  local copies, waits for them, and re-layouts  16.8 us (24%)
  Pallas kernels  15.1 us (21%)
  starting transfers between devices  11.5 us (16%)
  waiting for transfers between devices  0.82 us (1%)
    all_to_all x1, blocking collectives, exchange(): lax.all_to_all(value, ('side', 'dev'), split_axis=0, concat_axis=0, tiled...  26.4 us
    unnamed x38, local copies, waits for them, and re-layouts  16.8 us
    all_to_all x1, starting transfers between devices, exchange(): lax.all_to_all(value, ('side', 'dev'), split_axis=0, concat_axis=0, tiled...  11.5 us
    pallas_call x1, Pallas kernels, on_device(): pl.pallas_call(functools.partial(front_kernel, page=page, local=local), o...  8.19 us
    pallas_call x1, Pallas kernels, on_device(): pl.pallas_call(functools.partial(middle_kernel, n_dev=n_dev), out_shape=(...  3.9 us
    pallas_call x1, Pallas kernels, on_device(): pl.pallas_call(expert_kernel, out_shape=jax.ShapeDtypeStruct((slots, colu...  2.11 us
  transfers between devices with their start and end apart: 1, of which 1 were waited for; matrix products, arithmetic and copies ran while one was open for 0% of the time, Pallas kernels for 6%

profile of v3, /device:TPU:1, one launch (start us, length us, event | category | flops | bytes accessed | tf_op | source)
XLA Modules:
  0.0 70.7 jit_solution(11347354230551298807)
XLA Ops:
  0.0 0.0 copy-start.8
  0.0 0.0 copy-start.13
  0.0 0.0 copy-start.14
  0.0 8.2 %shard_map.199 = (bf16[1024,512]{1,0:T(8,128)(2,1)}, bf16[32,1024]{1,0:T(8,128)(2,1)}, bf16[32,2048]{1,0:T(8,128)(2,1)}) custom-call(s32[1,32]{1,0:T(1,128)} %bitcast.26, s32[8,32]{1,0:T(8,128)} %bitcast.23, s32[10,32]{1,0:T(8,128)} %bitcast.16, bf16[32,2048]{1,0:T(8,128)(2,1)} %refs_3_.1, f32[1,256]{1,0:T(1,128)} %bitcast.24, bf16[32,256]{1,0:T(8,128)(2,1)} %refs_5_.2, ...), custom_call_target="tpu_custom_call" | custom-call | tf_op jit(solution)/shard_map/pallas_call | solution.py:418
  8.2 11.5 %all-to-all-start = ((bf16[128,8,512]{2,1,0:T(8,128)(2,1)}), bf16[128,8,512]{2,1,0:T(8,128)(2,1)S(1)}, u32[]{:S(2)}, u32[]{:S(2)}) async-start(bf16[128,8,512]{2,1,0:T(8,128)(2,1)} %bitcast.22), calls=%async_computation | async-start | bytes 2097152 | tf_op jit(solution)/shard_map/all_to_all | solution.py:363
  19.7 0.0 copy-done.8
  19.7 0.0 copy-done.13
  19.7 0.0 copy-done.14
  19.7 0.0 copy-start
  19.8 2.2 %copy-done = bf16[4,2048,256]{2,1,0:T(8,128)(2,1)S(1)} copy-done((bf16[4,2048,256]{2,1,0:T(8,128)(2,1)S(1)}, bf16[4,2048,256]{2,1,0:T(8,128)(2,1)}, u32[]{:S(2)}) %copy-start) | copy-done | bytes 4194328
  21.9 0.0 copy-start.5
  21.9 1.2 %copy-done.5 = bf16[2048,256]{1,0:T(8,128)(2,1)S(1)} copy-done((bf16[2048,256]{1,0:T(8,128)(2,1)S(1)}, bf16[2048,256]{1,0:T(8,128)(2,1)}, u32[]{:S(2)}) %copy-start.5) | copy-done | bytes 1048600
  23.2 1.2 %copy-done.6 = bf16[2048,256]{1,0:T(8,128)(2,1)S(1)} copy-done((bf16[2048,256]{1,0:T(8,128)(2,1)S(1)}, bf16[2048,256]{1,0:T(8,128)(2,1)}, u32[]{:S(2)}) %copy-start.6) | copy-done | bytes 1048600
  24.4 1.2 %copy-done.7 = bf16[256,2048]{1,0:T(8,128)(2,1)S(1)} copy-done((bf16[256,2048]{1,0:T(8,128)(2,1)S(1)}, bf16[256,2048]{1,0:T(8,128)(2,1)}, u32[]{:S(2)}) %copy-start.7) | copy-done | bytes 1048600
  25.6 0.9 %copy-done.9 = bf16[32,2048]{1,0:T(8,128)(2,1)S(1)} copy-done((bf16[32,2048]{1,0:T(8,128)(2,1)S(1)}, bf16[32,2048]{1,0:T(8,128)(2,1)}, u32[]{:S(2)}) %copy-start.9) | copy-done | bytes 131096
  26.5 0.8 %copy-done.12 = bf16[32,1024]{1,0:T(8,128)(2,1)S(1)} copy-done((bf16[32,1024]{1,0:T(8,128)(2,1)S(1)}, bf16[32,1024]{1,0:T(8,128)(2,1)}, u32[]{:S(2)}) %copy-start.12) | copy-done | bytes 65560
  27.4 0.7 copy-done.15
  28.1 0.7 copy-done.18
  28.7 3.9 %shard_map.200 = (f32[32,1024]{1,0:T(8,128)S(1)}, bf16[128,1024]{1,0:T(8,128)(2,1)S(1)}, f32[1,2048]{1,0:T(1,128)S(1)}, bf16[2,2048,256]{2,1,0:T(8,128)(2,1)S(1)...) custom-call(bf16[32,2048]{1,0:T(8,128)(2,1)S(1)} %copy-done.9, bf16[32,1024]{1,0:T(8,128)(2,1)S(1)} %copy-done.12, ...), custom_call_target="tpu_custom_call" | custom-call | flops 234881024 | bytes 14680064 | tf_op jit(solution)/shard_map/pallas_call | solution.py:438
  32.6 0.0 copy-start.1
  32.7 1.3 %copy-done.1 = bf16[2,2048,256]{2,1,0:T(8,128)(2,1)} copy-done((bf16[2,2048,256]{2,1,0:T(8,128)(2,1)}, bf16[2,2048,256]{2,1,0:T(8,128)(2,1)S(1)}, u32[]{:S(2)}) %copy-start.1) | copy-done | bytes 2097176
  34.0 1.3 %copy-done.3 = bf16[2,256,2048]{2,1,0:T(8,128)(2,1)} copy-done((bf16[2,256,2048]{2,1,0:T(8,128)(2,1)}, bf16[2,256,2048]{2,1,0:T(8,128)(2,1)S(1)}, u32[]{:S(2)}) %copy-start.3) | copy-done | bytes 2097176
  35.3 0.7 copy-done.10
  36.0 0.6 copy-done.16
  36.5 0.8 %all-to-all-done = bf16[128,8,512]{2,1,0:T(8,128)(2,1)S(1)} async-done(((bf16[128,8,512]{2,1,0:T(8,128)(2,1)}), bf16[128,8,512]{2,1,0:T(8,128)(2,1)S(1)}, u32[]{:S(2)}, u32[]{:S(2)}) %all-to-all-start) | async-done | bytes 1048608 | tf_op jit(solution)/shard_map/all_to_all | solution.py:363
  37.4 1.6 %copy-done.2 = bf16[2,2048,256]{2,1,0:T(8,128)(2,1)S(1)} copy-done((bf16[2,2048,256]{2,1,0:T(8,128)(2,1)S(1)}, bf16[2,2048,256]{2,1,0:T(8,128)(2,1)}, u32[]{:S(2)}) %copy-start.2) | copy-done | bytes 2097176
  39.0 1.6 %copy-done.4 = bf16[2,256,2048]{2,1,0:T(8,128)(2,1)S(1)} copy-done((bf16[2,256,2048]{2,1,0:T(8,128)(2,1)S(1)}, bf16[2,256,2048]{2,1,0:T(8,128)(2,1)}, u32[]{:S(2)}) %copy-start.4) | copy-done | bytes 2097176
  40.6 0.7 copy-done.17
  41.3 2.1 %shard_map.201 = bf16[1024,512]{1,0:T(8,128)(2,1)S(1)} custom-call(bf16[1024,512]{1,0:T(8,128)(2,1)S(1)} %bitcast.13, f32[1,2048]{1,0:T(1,128)S(1)} %copy-done.17, bf16[2,2048,256]{2,1,0:T(8,128)(2,1)S(1)} %get-tuple-element.20.gate, bf16[2,2048,256]{2,1,0:T(8,128)(2,1)S(1)} %copy-done.2, bf16[2,256,2048]{2,1,0:T(8,128)(2,1)S(1)} %copy-done.4), custom_call_target="tpu_custom_call" | custom-call | tf_op jit(solution)/shard_map/pallas_call | solution.py:484
  43.4 26.4 %all_to_all.22 = bf16[128,8,512]{2,1,0:T(8,128)(2,1)S(1)} all-to-all(bf16[128,8,512]{2,1,0:T(8,128)(2,1)S(1)} %bitcast.14), channel_id=1, replica_groups=mesh['side'=2,'dev'=64] {'side','dev'}, dimensions={0} | all-to-all | bytes 2097152 | tf_op jit(solution)/shard_map/all_to_all | solution.py:363
  69.8 0.0 copy-done.11
  69.8 1.0 %shard_map.202 = bf16[32,1024]{1,0:T(8,128)(2,1)} custom-call(bf16[128,1024]{1,0:T(8,128)(2,1)S(1)} %get-tuple-element.16.spread_ref, f32[32,1024]{1,0:T(8,128)S(1)} %copy-done.11, bf16[1024,512]{1,0:T(8,128)(2,1)S(1)} %bitcast.15), custom_call_target="tpu_custom_call" | custom-call | tf_op jit(solution)/shard_map/pallas_call | solution.py:496
  (13 shorter events, 0.0 us)
Async XLA Ops:
  0.0 19.7 %copy-start.8 = (bf16[32,2048]{1,0:T(8,128)(2,1)S(1)}, bf16[32,2048]{1,0:T(8,128)(2,1)}, u32[]{:S(2)}) copy-start(bf16[32,2048]{1,0:T(8,128)(2,1)} %refs_5_.3) | copy-start | bytes 393220
  0.0 19.7 %copy-start.13 = (s32[32,10]{0,1:T(8,128)S(1)}, s32[32,10]{0,1:T(8,128)}, u32[]{:S(2)}) copy-start(s32[32,10]{0,1:T(8,128)} %param.33) | copy-start | bytes 3844
  0.0 19.7 %copy-start.14 = (f32[32,10]{0,1:T(8,128)S(1)}, f32[32,10]{0,1:T(8,128)}, u32[]{:S(2)}) copy-start(f32[32,10]{0,1:T(8,128)} %param.34) | copy-start | bytes 3844
  8.2 29.2 %all-to-all-start = ((bf16[128,8,512]{2,1,0:T(8,128)(2,1)}), bf16[128,8,512]{2,1,0:T(8,128)(2,1)S(1)}, u32[]{:S(2)}, u32[]{:S(2)}) async-start(bf16[128,8,512]{2,1,0:T(8,128)(2,1)} %bitcast.22), calls=%async_computation | async-start | bytes 2097152 | tf_op jit(solution)/shard_map/all_to_all | solution.py:363
  19.7 2.2 %copy-start = (bf16[4,2048,256]{2,1,0:T(8,128)(2,1)S(1)}, bf16[4,2048,256]{2,1,0:T(8,128)(2,1)}, u32[]{:S(2)}) copy-start(bf16[4,2048,256]{2,1,0:T(8,128)(2,1)} %refs_11_.3) | copy-start | bytes 12582916
  21.9 1.2 %copy-start.5 = (bf16[2048,256]{1,0:T(8,128)(2,1)S(1)}, bf16[2048,256]{1,0:T(8,128)(2,1)}, u32[]{:S(2)}) copy-start(bf16[2048,256]{1,0:T(8,128)(2,1)} %refs_8_.3) | copy-start | bytes 3145732
  23.2 1.2 %copy-start.6 = (bf16[2048,256]{1,0:T(8,128)(2,1)S(1)}, bf16[2048,256]{1,0:T(8,128)(2,1)}, u32[]{:S(2)}) copy-start(bf16[2048,256]{1,0:T(8,128)(2,1)} %refs_9_.3) | copy-start | bytes 3145732
  24.4 1.2 %copy-start.7 = (bf16[256,2048]{1,0:T(8,128)(2,1)S(1)}, bf16[256,2048]{1,0:T(8,128)(2,1)}, u32[]{:S(2)}) copy-start(bf16[256,2048]{1,0:T(8,128)(2,1)} %refs_10_.1) | copy-start | bytes 3145732
  25.6 0.9 %copy-start.9 = (bf16[32,2048]{1,0:T(8,128)(2,1)S(1)}, bf16[32,2048]{1,0:T(8,128)(2,1)}, u32[]{:S(2)}) copy-start(bf16[32,2048]{1,0:T(8,128)(2,1)} %get-tuple-element.14.refs_0_) | copy-start | bytes 393220
  26.5 0.8 %copy-start.12 = (bf16[32,1024]{1,0:T(8,128)(2,1)S(1)}, bf16[32,1024]{1,0:T(8,128)(2,1)}, u32[]{:S(2)}) copy-start(bf16[32,1024]{1,0:T(8,128)(2,1)} %get-tuple-element.15.refs_1_) | copy-start | bytes 196612
  27.4 0.7 copy-start.15
  28.1 0.7 copy-start.18
  32.6 1.3 %copy-start.1 = (bf16[2,2048,256]{2,1,0:T(8,128)(2,1)}, bf16[2,2048,256]{2,1,0:T(8,128)(2,1)S(1)}, u32[]{:S(2)}) copy-start(bf16[2,2048,256]{2,1,0:T(8,128)(2,1)S(1)} %get-tuple-element.21.up) | copy-start | bytes 6291460
  34.0 1.3 %copy-start.3 = (bf16[2,256,2048]{2,1,0:T(8,128)(2,1)}, bf16[2,256,2048]{2,1,0:T(8,128)(2,1)S(1)}, u32[]{:S(2)}) copy-start(bf16[2,256,2048]{2,1,0:T(8,128)(2,1)S(1)} %get-tuple-element.22.down) | copy-start | bytes 6291460
  35.3 0.7 copy-start.10
  36.0 0.6 copy-start.16
  37.4 1.6 %copy-start.2 = (bf16[2,2048,256]{2,1,0:T(8,128)(2,1)S(1)}, bf16[2,2048,256]{2,1,0:T(8,128)(2,1)}, u32[]{:S(2)}) copy-start(bf16[2,2048,256]{2,1,0:T(8,128)(2,1)} %copy-done.1) | copy-start | bytes 6291460
  39.0 1.6 %copy-start.4 = (bf16[2,256,2048]{2,1,0:T(8,128)(2,1)S(1)}, bf16[2,256,2048]{2,1,0:T(8,128)(2,1)}, u32[]{:S(2)}) copy-start(bf16[2,256,2048]{2,1,0:T(8,128)(2,1)} %copy-done.3) | copy-start | bytes 6291460
  40.6 0.7 copy-start.17
  41.2 28.5 %copy-start.11 = (f32[32,1024]{1,0:T(8,128)S(1)}, f32[32,1024]{1,0:T(8,128)}, u32[]{:S(2)}) copy-start(f32[32,1024]{1,0:T(8,128)} %copy-done.10) | copy-start | bytes 393220

commit v4 on v3

--- a/solution.py
+++ b/solution.py
@@ -35,7 +35,7 @@
 
 def expert_hits(experts, slot_expert):
     rows, topk = experts.shape
-    hits = jnp.zeros(slot_expert.shape, f32)
+    hits = jnp.zeros((rows, slot_expert.shape[1]), f32)
     for k in range(topk):
         hits = jnp.where(experts[:, k : k + 1] == slot_expert, 1.0, hits)
     earlier = (iota((rows, rows), 1) < iota((rows, rows), 0)).astype(f32).astype(bf16)
@@ -93,54 +93,39 @@
     pairs = list(zip(sources, targets))
     copies = start_all(
         pairs[:7]
-        + pieces_of(pool_hbm, pool, chunks)
+        + [pairs[10]]
         + pairs[7:9]
-        + [(residual_hbm.at[:, columns_at], residual_ref)]
+        + [
+            (residual_hbm.at[:, columns_at], residual_ref),
+        ]
         + [
             (source.at[:, columns_at], target)
             for source, target in pieces_of(weight_hbm, weight, weight_parts)
         ],
         sem,
     )
-    pool_copies = copies[7 : 7 + chunks]
-    late_copies = copies[7 + chunks : 10 + chunks]
-    weight_copies = copies[10 + chunks :]
     for copy in copies[:7]:
         copy.wait()
-
-    slots, columns = packed_ref.shape
-    parts = half // columns
-    mine = local // 2
-    slot = iota((rows, slots), 1)
-    per = parts * 2 * mine
-    destination = slot // per
-    n_dev = slots // per // 2
-    expert = (destination % n_dev) * local + (destination // n_dev) * mine + slot % mine
-    hits, rank = expert_hits(experts_in[...].T, expert)
-    slot_rank = slot % (2 * mine) // mine
-    picked = jnp.where(rank == slot_rank.astype(f32), hits, 0.0)
-    slot_part = slot % per // (2 * mine)
-    picked = jnp.concatenate(
-        [jnp.where(slot_part == p, picked, 0.0) for p in range(parts)], axis=0
-    )
-    chosen[...] = picked.T.astype(bf16)
 
     table = table_in[...].T
     same = iota((rows, rows), 0) == iota((rows, rows), 1)
     lengths = jnp.sum(
         jnp.where(same, jnp.broadcast_to(lengths_ref[...], (rows, rows)), 0), axis=1, keepdims=True
     )
-    for c in range(chunks):
-        token = iota((rows, context), 1) + c * context
-        token_page = token // page
-        token_in = token % page
-        mask = jnp.zeros((rows, context), f32)
-        for entry in range(table.shape[1]):
-            hit = (table[:, entry : entry + 1] == token_page) & (
-                token_in + entry * page < lengths
-            )
-            mask = jnp.where(hit, 1.0, mask)
-        valid[:, c * context : (c + 1) * context] = mask
+    pages = tokens // page
+    number = iota((1, pages), 1)
+    limit = jnp.zeros((rows, pages), i32)
+    for entry in range(table.shape[1]):
+        held = jnp.clip(lengths - entry * page, 0, page)
+        limit = jnp.where(table[:, entry : entry + 1] == number, jnp.maximum(limit, held), limit)
+    per_chunk = context // page
+    limit = limit.astype(f32).astype(bf16)
+    limit = jnp.concatenate(
+        [limit[:, c * per_chunk : (c + 1) * per_chunk] for c in range(chunks)], axis=0
+    )
+    expand = iota((per_chunk, context), 1) // page == iota((per_chunk, context), 0)
+    limit = dot(limit, expand.astype(f32).astype(bf16))
+    valid[...] = (iota((1, context), 1) % page < limit.astype(i32)).astype(f32)
 
     scale = head ** (-0.5)
     key_normed = rms_scale(keys_ref[...].astype(f32), key_gain_ref[...]).astype(bf16).astype(f32)
@@ -148,13 +133,14 @@
     for h in range(heads):
         part = queries_ref[:, h * head : (h + 1) * head].astype(f32)
         normed = rms_scale(part, query_gain_ref[...]).astype(bf16)
-        query[h * rows : (h + 1) * rows, :] = normed
+        query[h * rows : (h + 1) * rows, :] = normed * jnp.asarray(scale, bf16)
         own.append(jnp.sum(normed.astype(f32) * key_normed, axis=-1, keepdims=True))
     own_weight = jnp.exp(jnp.concatenate(own, axis=0) * scale)
 
+    for copy in copies[7:11]:
+        copy.wait()
     total = jnp.zeros((heads * rows, context), f32)
     for c in range(chunks):
-        pool_copies[c].wait()
         at = slice(c * context, (c + 1) * context)
         scores = lax.dot_general(
             query[...],
@@ -162,15 +148,31 @@
             (((1,), (1,)), ((), ())),
             preferred_element_type=f32,
         )
-        weights = jnp.exp(scores * scale)
-        weights = (weights.reshape(heads, rows, context) * valid[:, at][None]).reshape(
+        mask = valid[c * rows : (c + 1) * rows, :]
+        weights = (jnp.exp(scores).reshape(heads, rows, context) * mask[None]).reshape(
             heads * rows, context
         )
         total = total + weights
         prob[:, at] = weights.astype(bf16)
+
+    slots, columns = packed_ref.shape
+    parts = half // columns
+    mine = local // 2
+    slot = iota((1, slots), 1)
+    per = parts * 2 * mine
+    destination = slot // per
+    n_dev = slots // per // 2
+    expert = (destination % n_dev) * local + (destination // n_dev) * mine + slot % mine
+    hits, rank = expert_hits(experts_in[...].T, expert)
+    slot_rank = (slot % (2 * mine) // mine).astype(f32)
+    picked = jnp.where(rank == slot_rank, hits, 0.0)
+    slot_part = slot % per // (2 * mine)
+    picked = jnp.concatenate(
+        [jnp.where(slot_part == p, picked, 0.0) for p in range(parts)], axis=0
+    )
+    chosen[...] = picked.T.astype(bf16)
+
     mixed = dot(prob[...], pool[:, head:])
-    for copy in late_copies:
-        copy.wait()
     inverse = 1.0 / (jnp.sum(total, axis=1, keepdims=True) + own_weight)
     new_values = values_ref[...].astype(f32)
     for h in range(heads):
@@ -180,7 +182,7 @@
         attended[:, h * head : (h + 1) * head] = (value * gate).astype(bf16)
 
     projected = residual_ref[...].astype(f32)
-    for i, copy in enumerate(weight_copies):
+    for i, copy in enumerate(copies[11:]):
         copy.wait()
         at = slice(i * quarter, (i + 1) * quarter)
         projected = projected + dot(attended[:, at], weight[at, :])
@@ -207,9 +209,8 @@
         shared_down_hbm,
         gate_hbm,
         up_hbm,
-        down_hbm,
-    ) = refs[:14]
-    base_ref, spread_ref, post_gain, gate_ref, up_ref, down_ref = refs[14:20]
+    ) = refs[:13]
+    base_ref, spread_ref, post_gain, first_ref = refs[13:17]
     (
         experts_in,
         weights_in,
@@ -221,13 +222,12 @@
         shared_down,
         hidden,
         sem,
-    ) = refs[20:]
+    ) = refs[17:]
     rows, width = hidden.shape
     half = width // 2
     local = gate_hbm.shape[0]
     mine = local // 2
     side = lax.axis_index("side")
-    experts_at = pl.ds(side * mine, mine)
     columns_at = pl.ds(pl.multiple_of(side * half, half), half)
     others_at = pl.ds(pl.multiple_of((1 - side) * half, half), half)
     copies = start_all(
@@ -241,9 +241,8 @@
             (shared_gate_hbm, shared_gate),
             (shared_up_hbm, shared_up),
             (shared_down_hbm.at[:, columns_at], shared_down),
-            (gate_hbm.at[experts_at], gate_ref),
-            (up_hbm.at[experts_at], up_ref),
-            (down_hbm.at[experts_at], down_ref),
+            (gate_hbm.at[side * mine], first_ref.at[0]),
+            (up_hbm.at[side * mine], first_ref.at[1]),
         ],
         sem,
     )
@@ -254,7 +253,7 @@
     slots = spread_ref.shape[1]
     per = slots // (2 * n_dev)
     parts = per // local
-    slot = iota((rows, slots), 1)
+    slot = iota((1, slots), 1)
     source = slot // per
     expert = (source % n_dev) * local + (source // n_dev) * mine + slot % mine
     share = weights / jnp.sum(weights, axis=1, keepdims=True)
@@ -295,8 +294,36 @@
         copy.wait()
 
 
-def expert_kernel(received, post_gain, gate, up, down, sent_ref, taken, result):
-    mine, width, inner_width = gate.shape
+def expert_kernel(
+    received,
+    post_gain,
+    first,
+    gate_hbm,
+    up_hbm,
+    down_hbm,
+    sent_ref,
+    gate,
+    up,
+    down,
+    taken,
+    result,
+    sem,
+):
+    mine, inner_width, width = down.shape
+    at = lax.axis_index("side") * mine
+    copies = start_all(
+        [
+            pair
+            for j in range(mine)
+            for pair in (
+                ((gate_hbm.at[at + j], gate.at[j - 1]), (up_hbm.at[at + j], up.at[j - 1]))
+                if j
+                else ()
+            )
+        ]
+        + [(down_hbm.at[at + j], down.at[j]) for j in range(mine)],
+        sem,
+    )
     slots, columns = received.shape
     half = width // 2
     parts = half // columns
@@ -319,10 +346,17 @@
                         taken[j, row : row + block, column : column + columns] = ordered[
                             at : at + block
                         ]
+    inner = []
     for j in range(mine):
         normed = rms_scale(taken[j].astype(f32), post_gain[...]).astype(bf16)
-        inner = (jax.nn.silu(dot(normed, gate[j])) * dot(normed, up[j])).astype(bf16)
-        result[j] = dot(inner, down[j]).astype(bf16)
+        if j:
+            copies[2 * j - 2].wait()
+            copies[2 * j - 1].wait()
+        gate_j, up_j = (gate[j - 1], up[j - 1]) if j else (first[0], first[1])
+        inner.append((jax.nn.silu(dot(normed, gate_j)) * dot(normed, up_j)).astype(bf16))
+    for j in range(mine):
+        copies[2 * mine - 2 + j].wait()
+        result[j] = dot(inner[j], down[j]).astype(bf16)
 
     for t in range(2):
         for b in range(n_dev // block):
@@ -357,6 +391,10 @@
 
 VMEM = pl.BlockSpec(memory_space=pltpu.VMEM)
 HBM = pl.BlockSpec(memory_space=pltpu.HBM)
+
+
+def in_hbm(value):
+    return pltpu.with_memory_space_constraint(value, pltpu.HBM)
 
 
 def exchange(value):
@@ -418,7 +456,7 @@
     packed, hidden, attended = pl.pallas_call(
         functools.partial(front_kernel, page=page, local=local),
         out_shape=(
-            jax.ShapeDtypeStruct((slots, columns), bf16),
+            pltpu.VMEM((slots, columns), bf16),
             jax.ShapeDtypeStruct((rows, half), bf16),
             jax.ShapeDtypeStruct((rows, width), bf16),
         ),
@@ -428,25 +466,23 @@
         + [
             pltpu.VMEM((heads * rows, head), bf16),
             pltpu.VMEM((heads * rows, tokens), bf16),
-            pltpu.VMEM((rows, tokens), f32),
+            pltpu.VMEM((rows * tokens // 256, 256), f32),
             pltpu.VMEM((slots, half // columns * rows), bf16),
-            pltpu.SemaphoreType.DMA((14 + tokens // 256,)),
+            pltpu.SemaphoreType.DMA((15,)),
         ],
-        compiler_params=pltpu.CompilerParams(vmem_limit_bytes=63 * MIB),
-    )(*sources)
+        compiler_params=pltpu.CompilerParams(vmem_limit_bytes=32 * MIB),
+    )(*map(in_hbm, sources))
     received = exchange(packed)
-    base, spread, gain, gate, up, down = pl.pallas_call(
+    base, spread, gain, first = pl.pallas_call(
         functools.partial(middle_kernel, n_dev=n_dev),
         out_shape=(
             jax.ShapeDtypeStruct((rows, half), f32),
             jax.ShapeDtypeStruct((4 * rows, slots), bf16),
             jax.ShapeDtypeStruct((1, width), f32),
-            jax.ShapeDtypeStruct((mine, width, inner_width), bf16),
-            jax.ShapeDtypeStruct((mine, width, inner_width), bf16),
-            jax.ShapeDtypeStruct((mine, inner_width, width), bf16),
+            jax.ShapeDtypeStruct((2, width, inner_width), bf16),
         ),
-        in_specs=[VMEM] * 2 + [HBM] * 12,
-        out_specs=(VMEM,) * 6,
+        in_specs=[VMEM] * 2 + [HBM] * 11,
+        out_specs=(VMEM,) * 4,
         scratch_shapes=[
             pltpu.VMEM(experts.T.shape, i32),
             pltpu.VMEM(route_weights.T.shape, f32),
@@ -457,41 +493,49 @@
             pltpu.VMEM(shared_up.shape, bf16),
             pltpu.VMEM((shared_down.shape[0], half), bf16),
             pltpu.VMEM((rows, width), bf16),
-            pltpu.SemaphoreType.DMA((12,)),
+            pltpu.SemaphoreType.DMA((11,)),
         ],
-        compiler_params=pltpu.CompilerParams(vmem_limit_bytes=40 * MIB),
+        compiler_params=pltpu.CompilerParams(vmem_limit_bytes=24 * MIB),
         cost_estimate=pl.CostEstimate(
             flops=2 * rows * width * (half + 3 * inner_width),
-            bytes_accessed=14 * MIB,
+            bytes_accessed=10 * MIB,
             transcendentals=0,
         ),
     )(
         attended,
         hidden,
-        experts.T,
-        route_weights.T,
-        shared_mix.reshape(width // 128, 128),
-        residual,
-        post_gain[None, :],
-        out_weight,
-        shared_gate,
-        shared_up,
-        shared_down,
-        gate_weight,
-        up_weight,
-        down_weight,
+        *map(
+            in_hbm,
+            (
+                experts.T,
+                route_weights.T,
+                shared_mix.reshape(width // 128, 128),
+                residual,
+                post_gain[None, :],
+                out_weight,
+                shared_gate,
+                shared_up,
+                shared_down,
+                gate_weight,
+                up_weight,
+            ),
+        ),
     )
     sent = pl.pallas_call(
         expert_kernel,
-        out_shape=jax.ShapeDtypeStruct((slots, columns), bf16),
-        in_specs=[VMEM] * 5,
+        out_shape=pltpu.VMEM((slots, columns), bf16),
+        in_specs=[VMEM] * 3 + [HBM] * 3,
         out_specs=VMEM,
         scratch_shapes=[
+            pltpu.VMEM((mine - 1, width, inner_width), bf16),
+            pltpu.VMEM((mine - 1, width, inner_width), bf16),
+            pltpu.VMEM((mine, inner_width, width), bf16),
             pltpu.VMEM((mine, 2 * n_dev, width), bf16),
             pltpu.VMEM((mine, 2 * n_dev, width), bf16),
+            pltpu.SemaphoreType.DMA((3 * mine - 2,)),
         ],
         compiler_params=pltpu.CompilerParams(vmem_limit_bytes=24 * MIB),
-    )(received, gain, gate, up, down)
+    )(received, gain, first, in_hbm(gate_weight), in_hbm(up_weight), in_hbm(down_weight))
     returned = exchange(sent)
     return pl.pallas_call(
         combine_kernel,

time: 71.3 us -> 64.1 us (0.90)
  local copies, waits for them, and re-layouts: 16.8 us -> 2.11 us
  waiting for transfers between devices: 0.82 us -> 11.5 us
  blocking collectives: 26.4 us -> 23.2 us
    unnamed x38 -> x8, local copies, waits for them, and re-layouts: 16.8 us -> 2.11 us
    all_to_all x1, waiting for transfers between devices: 0.82 us -> 11.5 us  [exchange(): lax.all_to_all(value, ('side', 'dev'), split_axis=0, concat_axis=0, tiled...]
    all_to_all x1, blocking collectives: 26.4 us -> 23.2 us  [exchange(): lax.all_to_all(value, ('side', 'dev'), split_axis=0, concat_axis=0, tiled...]
    pallas_call x1, Pallas kernels: 8.19 us -> 6.07 us  [on_device(): pl.pallas_call(functools.partial(front_kernel, page=page, local=local), o...]
    pallas_call x1, Pallas kernels: 2.11 us -> 3.81 us  [on_device(): pl.pallas_call(expert_kernel, out_shape=pltpu.VMEM((slots, columns), bf16...]
    pallas_call x1, Pallas kernels: 3.9 us -> 4.67 us  [on_device(): pl.pallas_call(functools.partial(middle_kernel, n_dev=n_dev), out_shape=(...]
  transfers between devices with their start and end apart: 1 -> 1, of which waited for: 1 -> 1; matrix products, arithmetic and copies ran while one was open for 0% -> 0% of each run, Pallas kernels for 6% -> 7%
where the time goes in v4:
time: 64.1 us; the launch traced here: 63.8 us
  blocking collectives  23.2 us (36%)
  Pallas kernels  15.5 us (24%)
  starting transfers between devices  11.5 us (18%)
  waiting for transfers between devices  11.5 us (18%)
  local copies, waits for them, and re-layouts  2.11 us (3%)
    all_to_all x1, blocking collectives, exchange(): lax.all_to_all(value, ('side', 'dev'), split_axis=0, concat_axis=0, tiled...  23.2 us
    all_to_all x1, starting transfers between devices, exchange(): lax.all_to_all(value, ('side', 'dev'), split_axis=0, concat_axis=0, tiled...  11.5 us
    all_to_all x1, waiting for transfers between devices, exchange(): lax.all_to_all(value, ('side', 'dev'), split_axis=0, concat_axis=0, tiled...  11.5 us
    pallas_call x1, Pallas kernels, on_device(): pl.pallas_call(functools.partial(front_kernel, page=page, local=local), o...  6.07 us
    pallas_call x1, Pallas kernels, on_device(): pl.pallas_call(functools.partial(middle_kernel, n_dev=n_dev), out_shape=(...  4.67 us
    pallas_call x1, Pallas kernels, on_device(): pl.pallas_call(expert_kernel, out_shape=pltpu.VMEM((slots, columns), bf16...  3.81 us
    unnamed x8, local copies, waits for them, and re-layouts  2.11 us
  transfers between devices with their start and end apart: 1, of which 1 were waited for; matrix products, arithmetic and copies ran while one was open for 0% of the time, Pallas kernels for 7%

profile of v4, /device:TPU:1, one launch (start us, length us, event | category | flops | bytes accessed | tf_op | source)
XLA Modules:
  0.0 63.8 jit_solution(16504687733080192981)
XLA Ops:
  0.0 6.1 %shard_map.199 = (bf16[1024,512]{1,0:T(8,128)(2,1)}, bf16[32,1024]{1,0:T(8,128)(2,1)S(1)}, bf16[32,2048]{1,0:T(8,128)(2,1)S(1)}) custom-call(s32[1,32]{1,0:T(1,128)} %bitcast.25, s32[8,32]{1,0:T(8,128)} %bitcast.21, s32[10,32]{1,0:T(8,128)} %bitcast.17, bf16[32,2048]{1,0:T(8,128)(2,1)} %refs_3_.1, f32[1,256]{1,0:T(1,128)} %bitcast.23, ...), custom_call_target="tpu_custom_call" | custom-call | tf_op jit(solution)/shard_map/pallas_call | solution.py:456
  6.1 0.0 copy-start.2
  6.1 0.6 copy-done.2
  6.7 11.5 %all-to-all-start = ((bf16[128,8,512]{2,1,0:T(8,128)(2,1)}), bf16[128,8,512]{2,1,0:T(8,128)(2,1)S(1)}, u32[]{:S(2)}, u32[]{:S(2)}) async-start(bf16[128,8,512]{2,1,0:T(8,128)(2,1)} %bitcast.9), calls=%async_computation | async-start | bytes 2097152 | tf_op jit(solution)/shard_map/all_to_all | solution.py:401
  18.2 0.0 copy-start.3
  18.2 0.8 %copy-done.3 = bf16[32,1024]{1,0:T(8,128)(2,1)S(1)} copy-done((bf16[32,1024]{1,0:T(8,128)(2,1)S(1)}, bf16[32,1024]{1,0:T(8,128)(2,1)}, u32[]{:S(2)}) %copy-start.3) | copy-done | bytes 65560
  19.1 4.7 %shard_map.200 = (f32[32,1024]{1,0:T(8,128)S(1)}, bf16[128,1024]{1,0:T(8,128)(2,1)S(1)}, f32[1,2048]{1,0:T(1,128)S(1)}, bf16[2,2048,256]{2,1,0:T(8,128)(2,1)S(1)}) custom-call(bf16[32,2048]{1,0:T(8,128)(2,1)S(1)} %get-tuple-element.12.refs_0_, bf16[32,1024]{1,0:T(8,128)(2,1)S(1)} %copy-done.3, s32[10,32]{1,0:T(8,128)} %bitcast.18, f32[10,32]{1,0:T(8,128)} %bitcast.19, ...), custom_call_target="tpu_custom_call" | custom-call | flops 234881024 | bytes 10485760 | tf_op jit(solution)/shard_map/pallas_call | solution.py:476
  23.7 0.0 copy-start
  23.8 0.6 %copy-done = f32[32,1024]{1,0:T(8,128)} copy-done((f32[32,1024]{1,0:T(8,128)}, f32[32,1024]{1,0:T(8,128)S(1)}, u32[]{:S(2)}) %copy-start) | copy-done | bytes 131096
  24.4 11.5 %all-to-all-done = bf16[128,8,512]{2,1,0:T(8,128)(2,1)S(1)} async-done(((bf16[128,8,512]{2,1,0:T(8,128)(2,1)}), bf16[128,8,512]{2,1,0:T(8,128)(2,1)S(1)}, u32[]{:S(2)}, u32[]{:S(2)}) %all-to-all-start) | async-done | bytes 1048608 | tf_op jit(solution)/shard_map/all_to_all | solution.py:401
  35.9 0.0 copy-start.1
  35.9 3.8 %shard_map.201 = bf16[1024,512]{1,0:T(8,128)(2,1)S(1)} custom-call(bf16[1024,512]{1,0:T(8,128)(2,1)S(1)} %bitcast.14, f32[1,2048]{1,0:T(1,128)S(1)} %get-tuple-element.17.post_gain, bf16[2,2048,256]{2,1,0:T(8,128)(2,1)S(1)} %get-tuple-element.18.first, bf16[4,2048,256]{2,1,0:T(8,128)(2,1)} %gate_hbm.1, bf16[4,2048,256]{2,1,0:T(8,128)(2,1)} %up_hbm.1, ...), custom_call_target="tpu_custom_call" | custom-call | tf_op jit(solution)/shard_map/pallas_call | solution.py:524
  39.7 23.2 %all_to_all.22 = bf16[128,8,512]{2,1,0:T(8,128)(2,1)S(1)} all-to-all(bf16[128,8,512]{2,1,0:T(8,128)(2,1)S(1)} %bitcast.15), channel_id=1, replica_groups=mesh['side'=2,'dev'=64] {'side','dev'}, dimensions={0} | all-to-all | bytes 2097152 | tf_op jit(solution)/shard_map/all_to_all | solution.py:401
  62.9 0.0 copy-done.1
  62.9 0.9 %shard_map.202 = bf16[32,1024]{1,0:T(8,128)(2,1)} custom-call(bf16[128,1024]{1,0:T(8,128)(2,1)S(1)} %get-tuple-element.14.spread_ref, f32[32,1024]{1,0:T(8,128)S(1)} %copy-done.1, bf16[1024,512]{1,0:T(8,128)(2,1)S(1)} %bitcast.13), custom_call_target="tpu_custom_call" | custom-call | tf_op jit(solution)/shard_map/pallas_call | solution.py:540
Async XLA Ops:
  6.1 0.6 copy-start.2
  6.7 29.2 %all-to-all-start = ((bf16[128,8,512]{2,1,0:T(8,128)(2,1)}), bf16[128,8,512]{2,1,0:T(8,128)(2,1)S(1)}, u32[]{:S(2)}, u32[]{:S(2)}) async-start(bf16[128,8,512]{2,1,0:T(8,128)(2,1)} %bitcast.9), calls=%async_computation | async-start | bytes 2097152 | tf_op jit(solution)/shard_map/all_to_all | solution.py:401
  18.2 0.8 %copy-start.3 = (bf16[32,1024]{1,0:T(8,128)(2,1)S(1)}, bf16[32,1024]{1,0:T(8,128)(2,1)}, u32[]{:S(2)}) copy-start(bf16[32,1024]{1,0:T(8,128)(2,1)} %copy-done.2) | copy-start | bytes 196612
  23.7 0.7 %copy-start = (f32[32,1024]{1,0:T(8,128)}, f32[32,1024]{1,0:T(8,128)S(1)}, u32[]{:S(2)}) copy-start(f32[32,1024]{1,0:T(8,128)S(1)} %get-tuple-element.15.base_ref) | copy-start | bytes 393220
  35.9 27.0 %copy-start.1 = (f32[32,1024]{1,0:T(8,128)S(1)}, f32[32,1024]{1,0:T(8,128)}, u32[]{:S(2)}) copy-start(f32[32,1024]{1,0:T(8,128)} %copy-done) | copy-start | bytes 393220

commit v5 on v4

--- a/solution.py
+++ b/solution.py
@@ -60,10 +60,11 @@
 
 
 def front_kernel(*refs, page, local):
-    sources, refs = refs[:12], refs[12:]
-    packed_ref, hidden_ref, attended, refs = *refs[:3], refs[3:]
+    sources, expert_sources, refs = refs[:12], refs[12:15], refs[15:]
+    packed_ref, hidden_ref, attended = refs[:3]
+    expert_targets, refs = refs[3:6], refs[6:]
     targets, refs = refs[:12], refs[12:]
-    query, prob, valid, chosen, sem = refs
+    query, prob, valid, chosen, sem, expert_sem = refs
     residual_hbm, pool_hbm, weight_hbm = sources[-3:]
     (
         lengths_ref,
@@ -139,6 +140,13 @@
 
     for copy in copies[7:11]:
         copy.wait()
+    expert_copies = start_all(
+        [
+            (source.at[pl.ds(side * (local // 2), local // 2)], target)
+            for source, target in zip(expert_sources, expert_targets)
+        ],
+        expert_sem,
+    )
     total = jnp.zeros((heads * rows, context), f32)
     for c in range(chunks):
         at = slice(c * context, (c + 1) * context)
@@ -192,9 +200,11 @@
         [hidden[:, p * columns : (p + 1) * columns] for p in range(parts)], axis=0
     )
     packed_ref[...] = dot(chosen[...], stacked).astype(bf16)
-
-
-def middle_kernel(*refs, n_dev):
+    for copy in expert_copies:
+        copy.wait()
+
+
+def middle_kernel(*refs, n_dev, local):
     (
         attended,
         hidden_ref,
@@ -207,25 +217,24 @@
         shared_gate_hbm,
         shared_up_hbm,
         shared_down_hbm,
-        gate_hbm,
-        up_hbm,
-    ) = refs[:13]
-    base_ref, spread_ref, post_gain, first_ref = refs[13:17]
+        sent_hbm,
+    ) = refs[:12]
+    base_ref, spread_ref = refs[12:14]
     (
         experts_in,
         weights_in,
         mix,
         residual,
+        post_gain,
         out_weight,
         shared_gate,
         shared_up,
         shared_down,
         hidden,
         sem,
-    ) = refs[17:]
+    ) = refs[14:]
     rows, width = hidden.shape
     half = width // 2
-    local = gate_hbm.shape[0]
     mine = local // 2
     side = lax.axis_index("side")
     columns_at = pl.ds(pl.multiple_of(side * half, half), half)
@@ -241,8 +250,6 @@
             (shared_gate_hbm, shared_gate),
             (shared_up_hbm, shared_up),
             (shared_down_hbm.at[:, columns_at], shared_down),
-            (gate_hbm.at[side * mine], first_ref.at[0]),
-            (up_hbm.at[side * mine], first_ref.at[1]),
         ],
         sem,
     )
@@ -271,7 +278,7 @@
         spread_ref[at : at + rows, :] = high
         spread_ref[at + rows : at + 2 * rows, :] = (piece - high.astype(f32)).astype(bf16)
 
-    for copy in copies[2:9]:
+    for copy in copies[2:]:
         copy.wait()
     mine_hidden = hidden_ref[...]
     hidden[:, columns_at] = mine_hidden
@@ -290,40 +297,10 @@
         ].astype(f32)
     scale = jax.nn.sigmoid(jnp.sum(logit, axis=-1, keepdims=True))
     base_ref[...] = mine_hidden.astype(f32) + scale * dot(shared_inner, shared_down[...])
-    for copy in copies[9:]:
-        copy.wait()
-
-
-def expert_kernel(
-    received,
-    post_gain,
-    first,
-    gate_hbm,
-    up_hbm,
-    down_hbm,
-    sent_ref,
-    gate,
-    up,
-    down,
-    taken,
-    result,
-    sem,
-):
+
+
+def expert_kernel(received, post_gain, gate, up, down, sent_hbm, taken, result, sent, sem):
     mine, inner_width, width = down.shape
-    at = lax.axis_index("side") * mine
-    copies = start_all(
-        [
-            pair
-            for j in range(mine)
-            for pair in (
-                ((gate_hbm.at[at + j], gate.at[j - 1]), (up_hbm.at[at + j], up.at[j - 1]))
-                if j
-                else ()
-            )
-        ]
-        + [(down_hbm.at[at + j], down.at[j]) for j in range(mine)],
-        sem,
-    )
     slots, columns = received.shape
     half = width // 2
     parts = half // columns
@@ -346,18 +323,12 @@
                         taken[j, row : row + block, column : column + columns] = ordered[
                             at : at + block
                         ]
-    inner = []
     for j in range(mine):
         normed = rms_scale(taken[j].astype(f32), post_gain[...]).astype(bf16)
-        if j:
-            copies[2 * j - 2].wait()
-            copies[2 * j - 1].wait()
-        gate_j, up_j = (gate[j - 1], up[j - 1]) if j else (first[0], first[1])
-        inner.append((jax.nn.silu(dot(normed, gate_j)) * dot(normed, up_j)).astype(bf16))
-    for j in range(mine):
-        copies[2 * mine - 2 + j].wait()
-        result[j] = dot(inner[j], down[j]).astype(bf16)
-
+        inner = jax.nn.silu(dot(normed, gate[j])) * dot(normed, up[j])
+        result[j] = dot(inner.astype(bf16), down[j]).astype(bf16)
+
+    copies = []
     for t in range(2):
         for b in range(n_dev // block):
             gathered = jnp.concatenate(
@@ -374,7 +345,13 @@
                 axis=0,
             )
             at = (t * n_dev + b * block) * groups
-            sent_ref[at : at + groups * block, :] = dot(outward, gathered).astype(bf16)
+            at = pl.ds(at, groups * block)
+            sent[at, :] = dot(outward, gathered).astype(bf16)
+            copy = pltpu.make_async_copy(sent.at[at], sent_hbm.at[at], sem.at[len(copies)])
+            copy.start()
+            copies.append(copy)
+    for copy in copies:
+        copy.wait()
 
 
 def combine_kernel(spread_ref, base_ref, returned, out_ref):
@@ -453,15 +430,18 @@
     held = [pltpu.VMEM(source.shape, source.dtype) for source in sources]
     held[9] = pltpu.VMEM((rows, half), bf16)
     held[11] = pltpu.VMEM((width, half), bf16)
-    packed, hidden, attended = pl.pallas_call(
+    packed, hidden, attended, gate, up, down = pl.pallas_call(
         functools.partial(front_kernel, page=page, local=local),
         out_shape=(
-            pltpu.VMEM((slots, columns), bf16),
+            jax.ShapeDtypeStruct((slots, columns), bf16),
             jax.ShapeDtypeStruct((rows, half), bf16),
             jax.ShapeDtypeStruct((rows, width), bf16),
+            jax.ShapeDtypeStruct((mine, width, inner_width), bf16),
+            jax.ShapeDtypeStruct((mine, width, inner_width), bf16),
+            jax.ShapeDtypeStruct((mine, inner_width, width), bf16),
         ),
-        in_specs=[HBM] * len(sources),
-        out_specs=(VMEM, VMEM, VMEM),
+        in_specs=[HBM] * (len(sources) + 3),
+        out_specs=(VMEM,) * 6,
         scratch_shapes=held
         + [
             pltpu.VMEM((heads * rows, head), bf16),
@@ -469,36 +449,50 @@
             pltpu.VMEM((rows * tokens // 256, 256), f32),
             pltpu.VMEM((slots, half // columns * rows), bf16),
             pltpu.SemaphoreType.DMA((15,)),
+            pltpu.SemaphoreType.DMA((3,)),
         ],
-        compiler_params=pltpu.CompilerParams(vmem_limit_bytes=32 * MIB),
-    )(*map(in_hbm, sources))
+        compiler_params=pltpu.CompilerParams(vmem_limit_bytes=24 * MIB),
+    )(*map(in_hbm, sources + (gate_weight, up_weight, down_weight)))
     received = exchange(packed)
-    base, spread, gain, first = pl.pallas_call(
-        functools.partial(middle_kernel, n_dev=n_dev),
+    sent = pl.pallas_call(
+        expert_kernel,
+        out_shape=jax.ShapeDtypeStruct((slots, columns), bf16),
+        in_specs=[VMEM] * 5,
+        out_specs=HBM,
+        scratch_shapes=[
+            pltpu.VMEM((mine, 2 * n_dev, width), bf16),
+            pltpu.VMEM((mine, 2 * n_dev, width), bf16),
+            pltpu.VMEM((slots, columns), bf16),
+            pltpu.SemaphoreType.DMA((2 * n_dev // 32,)),
+        ],
+        compiler_params=pltpu.CompilerParams(vmem_limit_bytes=24 * MIB),
+    )(received, post_gain[None, :], gate, up, down)
+    returned = exchange(sent)
+    base, spread = pl.pallas_call(
+        functools.partial(middle_kernel, n_dev=n_dev, local=local),
         out_shape=(
             jax.ShapeDtypeStruct((rows, half), f32),
             jax.ShapeDtypeStruct((4 * rows, slots), bf16),
-            jax.ShapeDtypeStruct((1, width), f32),
-            jax.ShapeDtypeStruct((2, width, inner_width), bf16),
         ),
-        in_specs=[VMEM] * 2 + [HBM] * 11,
-        out_specs=(VMEM,) * 4,
+        in_specs=[VMEM] * 2 + [HBM] * 10,
+        out_specs=(VMEM,) * 2,
         scratch_shapes=[
             pltpu.VMEM(experts.T.shape, i32),
             pltpu.VMEM(route_weights.T.shape, f32),
             pltpu.VMEM((width // 128, 128), bf16),
             pltpu.VMEM((rows, half), bf16),
+            pltpu.VMEM((1, width), f32),
             pltpu.VMEM((width, half), bf16),
             pltpu.VMEM(shared_gate.shape, bf16),
             pltpu.VMEM(shared_up.shape, bf16),
             pltpu.VMEM((shared_down.shape[0], half), bf16),
             pltpu.VMEM((rows, width), bf16),
-            pltpu.SemaphoreType.DMA((11,)),
+            pltpu.SemaphoreType.DMA((9,)),
         ],
         compiler_params=pltpu.CompilerParams(vmem_limit_bytes=24 * MIB),
         cost_estimate=pl.CostEstimate(
             flops=2 * rows * width * (half + 3 * inner_width),
-            bytes_accessed=10 * MIB,
+            bytes_accessed=8 * MIB,
             transcendentals=0,
         ),
     )(
@@ -516,27 +510,10 @@
                 shared_gate,
                 shared_up,
                 shared_down,
-                gate_weight,
-                up_weight,
+                sent,
             ),
         ),
     )
-    sent = pl.pallas_call(
-        expert_kernel,
-        out_shape=pltpu.VMEM((slots, columns), bf16),
-        in_specs=[VMEM] * 3 + [HBM] * 3,
-        out_specs=VMEM,
-        scratch_shapes=[
-            pltpu.VMEM((mine - 1, width, inner_width), bf16),
-            pltpu.VMEM((mine - 1, width, inner_width), bf16),
-            pltpu.VMEM((mine, inner_width, width), bf16),
-            pltpu.VMEM((mine, 2 * n_dev, width), bf16),
-            pltpu.VMEM((mine, 2 * n_dev, width), bf16),
-            pltpu.SemaphoreType.DMA((3 * mine - 2,)),
-        ],
-        compiler_params=pltpu.CompilerParams(vmem_limit_bytes=24 * MIB),
-    )(received, gain, first, in_hbm(gate_weight), in_hbm(up_weight), in_hbm(down_weight))
-    returned = exchange(sent)
     return pl.pallas_call(
         combine_kernel,
         out_shape=jax.ShapeDtypeStruct((rows, half), bf16),

time: 64.1 us -> 61.8 us (0.964)
  blocking collectives: 23.2 us -> 29 us
  starting transfers between devices: 11.5 us -> 5.71 us
  local copies, waits for them, and re-layouts: 2.11 us -> 0.01 us
  Pallas kernels: 15.5 us -> 13.9 us
  waiting for transfers between devices: 11.5 us -> 13 us
    all_to_all x1, blocking collectives: 23.2 us -> 29 us  [exchange(): lax.all_to_all(value, ('side', 'dev'), split_axis=0, concat_axis=0, tiled...]
    all_to_all x1, starting transfers between devices: 11.5 us -> 5.71 us  [exchange(): lax.all_to_all(value, ('side', 'dev'), split_axis=0, concat_axis=0, tiled...]
    unnamed x8 -> x2, local copies, waits for them, and re-layouts: 2.11 us -> 0.01 us
    all_to_all x1, waiting for transfers between devices: 11.5 us -> 13 us  [exchange(): lax.all_to_all(value, ('side', 'dev'), split_axis=0, concat_axis=0, tiled...]
    pallas_call x2, Pallas kernels: 8.48 us -> 7.56 us  [the longest x1 4.66 us: on_device(): pl.pallas_call(functools.partial(middle_kernel, n_dev=n_dev, local=local)...]
    pallas_call x1, Pallas kernels: 6.07 us -> 5.37 us  [on_device(): pl.pallas_call(functools.partial(front_kernel, page=page, local=local), o...]
  transfers between devices with their start and end apart: 1 -> 1, of which waited for: 1 -> 1; matrix products, arithmetic and copies ran while one was open for 0% -> 0% of each run, Pallas kernels for 7% -> 8%
where the time goes in v5:
time: 61.8 us; the launch traced here: 61.6 us
  blocking collectives  29 us (47%)
  Pallas kernels  13.9 us (22%)
  waiting for transfers between devices  13 us (21%)
  starting transfers between devices  5.71 us (9%)
    all_to_all x1, blocking collectives, exchange(): lax.all_to_all(value, ('side', 'dev'), split_axis=0, concat_axis=0, tiled...  29 us
    all_to_all x1, waiting for transfers between devices, exchange(): lax.all_to_all(value, ('side', 'dev'), split_axis=0, concat_axis=0, tiled...  13 us
    all_to_all x1, starting transfers between devices, exchange(): lax.all_to_all(value, ('side', 'dev'), split_axis=0, concat_axis=0, tiled...  5.71 us
    pallas_call x1, Pallas kernels, on_device(): pl.pallas_call(functools.partial(front_kernel, page=page, local=local), o...  5.37 us
    pallas_call x1, Pallas kernels, on_device(): pl.pallas_call(functools.partial(middle_kernel, n_dev=n_dev, local=local)...  4.66 us
    pallas_call x1, Pallas kernels, on_device(): pl.pallas_call(expert_kernel, out_shape=jax.ShapeDtypeStruct((slots, colu...  2.9 us
  transfers between devices with their start and end apart: 1, of which 1 were waited for; matrix products, arithmetic and copies ran while one was open for 0% of the time, Pallas kernels for 8%

profile of v5, /device:TPU:1, one launch (start us, length us, event | category | flops | bytes accessed | tf_op | source)
XLA Modules:
  0.0 61.6 jit_solution(3428614997777037107)
XLA Ops:
  0.0 0.0 copy-start
  0.0 5.4 %shard_map.199 = (bf16[1024,512]{1,0:T(8,128)(2,1)S(1)}, bf16[32,1024]{1,0:T(8,128)(2,1)S(1)}, bf16[32,2048]{1,0:T(8,128)(2,1)S(1)}, bf16[2,2048,256]{2,1,0:T(8,...) custom-call(s32[1,32]{1,0:T(1,128)} %bitcast.26, s32[8,32]{1,0:T(8,128)} %bitcast.23, ...), custom_call_target="tpu_custom_call" | custom-call | tf_op jit(solution)/shard_map/pallas_call | solution.py:433
  5.4 29.0 %all_to_all.22 = bf16[128,8,512]{2,1,0:T(8,128)(2,1)S(1)} all-to-all(bf16[128,8,512]{2,1,0:T(8,128)(2,1)S(1)} %bitcast.15), channel_id=1, replica_groups=mesh['side'=2,'dev'=64] {'side','dev'}, dimensions={0} | all-to-all | bytes 2097152 | tf_op jit(solution)/shard_map/all_to_all | solution.py:378
  34.3 0.0 copy-done
  34.3 2.9 %shard_map.200.refs_11_ = bf16[1024,512]{1,0:T(8,128)(2,1)} custom-call(bf16[1024,512]{1,0:T(8,128)(2,1)S(1)} %bitcast.13, f32[1,2048]{1,0:T(1,128)S(1)} %bitcast.17, bf16[2,2048,256]{2,1,0:T(8,128)(2,1)S(1)} %get-tuple-element.16.gate, bf16[2,2048,256]{2,1,0:T(8,128)(2,1)S(1)} %get-tuple-element.17.up, bf16[2,256,2048]{2,1,0:T(8,128)(2,1)S(1)} %get-tuple-element.18.down), custom_call_target="tpu_custom_call" | custom-call | tf_op jit(solution)/shard_map/pallas_call | solution.py:457
  37.2 5.7 %all-to-all-start.1 = ((bf16[128,8,512]{2,1,0:T(8,128)(2,1)}), bf16[128,8,512]{2,1,0:T(8,128)(2,1)S(1)}, u32[]{:S(2)}, u32[]{:S(2)}) async-start(bf16[128,8,512]{2,1,0:T(8,128)(2,1)} %bitcast.11), calls=%async_computation.1 | async-start | bytes 2097152 | tf_op jit(solution)/shard_map/all_to_all | solution.py:378
  43.0 4.7 %shard_map.201 = (f32[32,1024]{1,0:T(8,128)S(1)}, bf16[128,1024]{1,0:T(8,128)(2,1)S(1)}) custom-call(bf16[32,2048]{1,0:T(8,128)(2,1)S(1)} %get-tuple-element.13.refs_0_, bf16[32,1024]{1,0:T(8,128)(2,1)S(1)} %get-tuple-element.14.refs_1_, s32[10,32]{1,0:T(8,128)} %bitcast.20, f32[10,32]{1,0:T(8,128)} %bitcast.21, bf16[16,128]{1,0:T(8,128)(2,1)} %bitcast.22, ...), custom_call_target="tpu_custom_call" | custom-call | flops 234881024 | bytes 8388608 | tf_op jit(solution)/shard_map/pallas_call | solution.py:471
  47.6 13.0 %all-to-all-done.1 = bf16[128,8,512]{2,1,0:T(8,128)(2,1)S(1)} async-done(((bf16[128,8,512]{2,1,0:T(8,128)(2,1)}), bf16[128,8,512]{2,1,0:T(8,128)(2,1)S(1)}, u32[]{:S(2)}, u32[]{:S(2)}) %all-to-all-start.1) | async-done | bytes 1048608 | tf_op jit(solution)/shard_map/all_to_all | solution.py:378
  60.6 0.9 %shard_map.202 = bf16[32,1024]{1,0:T(8,128)(2,1)} custom-call(bf16[128,1024]{1,0:T(8,128)(2,1)S(1)} %get-tuple-element.19.spread_ref, f32[32,1024]{1,0:T(8,128)S(1)} %get-tuple-element.20.base_ref, bf16[1024,512]{1,0:T(8,128)(2,1)S(1)} %bitcast.14), custom_call_target="tpu_custom_call" | custom-call | tf_op jit(solution)/shard_map/pallas_call | solution.py:517
Async XLA Ops:
  0.0 34.3 %copy-start = (f32[2048]{0:T(1024)S(1)}, f32[2048]{0:T(1024)}, u32[]{:S(2)}) copy-start(f32[2048]{0:T(1024)} %param.32) | copy-start | bytes 24580
  37.2 23.4 %all-to-all-start.1 = ((bf16[128,8,512]{2,1,0:T(8,128)(2,1)}), bf16[128,8,512]{2,1,0:T(8,128)(2,1)S(1)}, u32[]{:S(2)}, u32[]{:S(2)}) async-start(bf16[128,8,512]{2,1,0:T(8,128)(2,1)} %bitcast.11), calls=%async_computation.1 | async-start | bytes 2097152 | tf_op jit(solution)/shard_map/all_to_all | solution.py:378

commit v6 on v5

--- a/solution.py
+++ b/solution.py
@@ -52,19 +52,12 @@
     return copies
 
 
-def pieces_of(source, target, count):
-    size = source.shape[0] // count
-    return [
-        (source.at[pl.ds(i * size, size)], target.at[pl.ds(i * size, size)]) for i in range(count)
-    ]
-
-
 def front_kernel(*refs, page, local):
     sources, expert_sources, refs = refs[:12], refs[12:15], refs[15:]
     packed_ref, hidden_ref, attended = refs[:3]
     expert_targets, refs = refs[3:6], refs[6:]
     targets, refs = refs[:12], refs[12:]
-    query, prob, valid, chosen, sem, expert_sem = refs
+    query, prob, valid, own_weight, chosen, sem, expert_sem = refs
     residual_hbm, pool_hbm, weight_hbm = sources[-3:]
     (
         lengths_ref,
@@ -87,9 +80,11 @@
     tokens = pool.shape[0]
     context = 256
     chunks = tokens // context
-    weight_parts = 4
-    quarter = width // weight_parts
     side = lax.axis_index("side")
+    always = side >= 0
+    slots, columns = packed_ref.shape
+    parts = half // columns
+    mine = local // 2
     columns_at = pl.ds(pl.multiple_of(side * half, half), half)
     pairs = list(zip(sources, targets))
     copies = start_all(
@@ -98,108 +93,111 @@
         + pairs[7:9]
         + [
             (residual_hbm.at[:, columns_at], residual_ref),
-        ]
-        + [
-            (source.at[:, columns_at], target)
-            for source, target in pieces_of(weight_hbm, weight, weight_parts)
+            (weight_hbm.at[:, columns_at], weight),
         ],
         sem,
     )
     for copy in copies[:7]:
         copy.wait()
 
-    table = table_in[...].T
-    same = iota((rows, rows), 0) == iota((rows, rows), 1)
-    lengths = jnp.sum(
-        jnp.where(same, jnp.broadcast_to(lengths_ref[...], (rows, rows)), 0), axis=1, keepdims=True
-    )
-    pages = tokens // page
-    number = iota((1, pages), 1)
-    limit = jnp.zeros((rows, pages), i32)
-    for entry in range(table.shape[1]):
-        held = jnp.clip(lengths - entry * page, 0, page)
-        limit = jnp.where(table[:, entry : entry + 1] == number, jnp.maximum(limit, held), limit)
-    per_chunk = context // page
-    limit = limit.astype(f32).astype(bf16)
-    limit = jnp.concatenate(
-        [limit[:, c * per_chunk : (c + 1) * per_chunk] for c in range(chunks)], axis=0
-    )
-    expand = iota((per_chunk, context), 1) // page == iota((per_chunk, context), 0)
-    limit = dot(limit, expand.astype(f32).astype(bf16))
-    valid[...] = (iota((1, context), 1) % page < limit.astype(i32)).astype(f32)
-
-    scale = head ** (-0.5)
-    key_normed = rms_scale(keys_ref[...].astype(f32), key_gain_ref[...]).astype(bf16).astype(f32)
-    own = []
-    for h in range(heads):
-        part = queries_ref[:, h * head : (h + 1) * head].astype(f32)
-        normed = rms_scale(part, query_gain_ref[...]).astype(bf16)
-        query[h * rows : (h + 1) * rows, :] = normed * jnp.asarray(scale, bf16)
-        own.append(jnp.sum(normed.astype(f32) * key_normed, axis=-1, keepdims=True))
-    own_weight = jnp.exp(jnp.concatenate(own, axis=0) * scale)
+    @pl.when(always)
+    def _():
+        table = table_in[...].T
+        same = iota((rows, rows), 0) == iota((rows, rows), 1)
+        lengths = jnp.sum(
+            jnp.where(same, jnp.broadcast_to(lengths_ref[...], (rows, rows)), 0), axis=1, keepdims=True
+        )
+        pages = tokens // page
+        number = iota((1, pages), 1)
+        limit = jnp.zeros((rows, pages), i32)
+        for entry in range(table.shape[1]):
+            held = jnp.clip(lengths - entry * page, 0, page)
+            limit = jnp.where(table[:, entry : entry + 1] == number, jnp.maximum(limit, held), limit)
+        per_chunk = context // page
+        limit = limit.astype(f32).astype(bf16)
+        limit = jnp.concatenate(
+            [limit[:, c * per_chunk : (c + 1) * per_chunk] for c in range(chunks)], axis=0
+        )
+        expand = iota((per_chunk, context), 1) // page == iota((per_chunk, context), 0)
+        limit = dot(limit, expand.astype(f32).astype(bf16))
+        valid[...] = (iota((1, context), 1) % page < limit.astype(i32)).astype(f32)
+
+        slot = iota((1, slots), 1)
+        per = parts * 2 * mine
+        destination = slot // per
+        n_dev = slots // per // 2
+        expert = (destination % n_dev) * local + (destination // n_dev) * mine + slot % mine
+        hits, rank = expert_hits(experts_in[...].T, expert)
+        slot_rank = (slot % (2 * mine) // mine).astype(f32)
+        picked = jnp.where(rank == slot_rank, hits, 0.0)
+        slot_part = slot % per // (2 * mine)
+        picked = jnp.concatenate(
+            [jnp.where(slot_part == p, picked, 0.0) for p in range(parts)], axis=0
+        )
+        chosen[...] = picked.T.astype(bf16)
+
+        scale = head ** (-0.5)
+        key_normed = rms_scale(keys_ref[...].astype(f32), key_gain_ref[...]).astype(bf16).astype(f32)
+        own = []
+        for h in range(heads):
+            part = queries_ref[:, h * head : (h + 1) * head].astype(f32)
+            normed = rms_scale(part, query_gain_ref[...]).astype(bf16)
+            query[h * rows : (h + 1) * rows, :] = normed * jnp.asarray(scale, bf16)
+            own.append(jnp.sum(normed.astype(f32) * key_normed, axis=-1, keepdims=True))
+        own_weight[...] = jnp.exp(jnp.concatenate(own, axis=0) * scale)
 
     for copy in copies[7:11]:
         copy.wait()
     expert_copies = start_all(
         [
-            (source.at[pl.ds(side * (local // 2), local // 2)], target)
+            (source.at[pl.ds(side * mine, target.shape[0])], target)
             for source, target in zip(expert_sources, expert_targets)
         ],
         expert_sem,
     )
-    total = jnp.zeros((heads * rows, context), f32)
-    for c in range(chunks):
-        at = slice(c * context, (c + 1) * context)
-        scores = lax.dot_general(
-            query[...],
-            pool[at, :head],
-            (((1,), (1,)), ((), ())),
-            preferred_element_type=f32,
+
+    @pl.when(always)
+    def _():
+        total = jnp.zeros((heads * rows, context), f32)
+        for c in range(chunks):
+            at = slice(c * context, (c + 1) * context)
+            scores = lax.dot_general(
+                query[...],
+                pool[at, :head],
+                (((1,), (1,)), ((), ())),
+                preferred_element_type=f32,
+            )
+            mask = valid[c * rows : (c + 1) * rows, :]
+            weights = (jnp.exp(scores).reshape(heads, rows, context) * mask[None]).reshape(
+                heads * rows, context
+            )
+            total = total + weights
+            prob[:, at] = weights.astype(bf16)
+
+        middle = heads * rows // 2
+        mixed = jnp.concatenate(
+            [dot(prob[:middle], pool[:, head:]), dot(prob[middle:], pool[:, head:])], axis=0
         )
-        mask = valid[c * rows : (c + 1) * rows, :]
-        weights = (jnp.exp(scores).reshape(heads, rows, context) * mask[None]).reshape(
-            heads * rows, context
+        inverse = 1.0 / (jnp.sum(total, axis=1, keepdims=True) + own_weight[...])
+        new_values = values_ref[...].astype(f32)
+        for h in range(heads):
+            part = slice(h * rows, (h + 1) * rows)
+            value = (mixed[part] + own_weight[part, :] * new_values) * inverse[part]
+            gate = jax.nn.sigmoid(gates_ref[:, h * head : (h + 1) * head].astype(f32))
+            attended[:, h * head : (h + 1) * head] = (value * gate).astype(bf16)
+
+    copies[11].wait()
+
+    @pl.when(always)
+    def _():
+        projected = residual_ref[...].astype(f32) + dot(attended[...], weight[...])
+        hidden = projected.astype(bf16)
+        hidden_ref[...] = hidden
+        stacked = jnp.concatenate(
+            [hidden[:, p * columns : (p + 1) * columns] for p in range(parts)], axis=0
         )
-        total = total + weights
-        prob[:, at] = weights.astype(bf16)
-
-    slots, columns = packed_ref.shape
-    parts = half // columns
-    mine = local // 2
-    slot = iota((1, slots), 1)
-    per = parts * 2 * mine
-    destination = slot // per
-    n_dev = slots // per // 2
-    expert = (destination % n_dev) * local + (destination // n_dev) * mine + slot % mine
-    hits, rank = expert_hits(experts_in[...].T, expert)
-    slot_rank = (slot % (2 * mine) // mine).astype(f32)
-    picked = jnp.where(rank == slot_rank, hits, 0.0)
-    slot_part = slot % per // (2 * mine)
-    picked = jnp.concatenate(
-        [jnp.where(slot_part == p, picked, 0.0) for p in range(parts)], axis=0
-    )
-    chosen[...] = picked.T.astype(bf16)
-
-    mixed = dot(prob[...], pool[:, head:])
-    inverse = 1.0 / (jnp.sum(total, axis=1, keepdims=True) + own_weight)
-    new_values = values_ref[...].astype(f32)
-    for h in range(heads):
-        part = slice(h * rows, (h + 1) * rows)
-        value = (mixed[part] + own_weight[part] * new_values) * inverse[part]
-        gate = jax.nn.sigmoid(gates_ref[:, h * head : (h + 1) * head].astype(f32))
-        attended[:, h * head : (h + 1) * head] = (value * gate).astype(bf16)
-
-    projected = residual_ref[...].astype(f32)
-    for i, copy in enumerate(copies[11:]):
-        copy.wait()
-        at = slice(i * quarter, (i + 1) * quarter)
-        projected = projected + dot(attended[:, at], weight[at, :])
-    hidden = projected.astype(bf16)
-    hidden_ref[...] = hidden
-    stacked = jnp.concatenate(
-        [hidden[:, p * columns : (p + 1) * columns] for p in range(parts)], axis=0
-    )
-    packed_ref[...] = dot(chosen[...], stacked).astype(bf16)
+        packed_ref[...] = dot(chosen[...], stacked).astype(bf16)
+
     for copy in expert_copies:
         copy.wait()
 
@@ -299,8 +297,27 @@
     base_ref[...] = mine_hidden.astype(f32) + scale * dot(shared_inner, shared_down[...])
 
 
-def expert_kernel(received, post_gain, gate, up, down, sent_hbm, taken, result, sent, sem):
-    mine, inner_width, width = down.shape
+def expert_kernel(
+    received,
+    post_gain,
+    gate,
+    up,
+    down,
+    down_hbm,
+    sent_hbm,
+    last_down,
+    taken,
+    inner,
+    result,
+    sent,
+    sem,
+):
+    mine, width, inner_width = gate.shape
+    side = lax.axis_index("side")
+    last = pltpu.make_async_copy(
+        down_hbm.at[side * mine + mine - 1], last_down, sem.at[sem.shape[0] - 1]
+    )
+    last.start()
     slots, columns = received.shape
     half = width // 2
     parts = half // columns
@@ -310,23 +327,29 @@
     inward = group_order(groups, block, True)
     outward = group_order(groups, block, False)
 
-    for s in range(2):
-        for b in range(n_dev // block):
-            at = (s * n_dev + b * block) * groups
-            ordered = dot(inward, received[at : at + groups * block, :]).astype(bf16)
-            for p in range(parts):
-                for r in range(2):
-                    for j in range(mine):
-                        at = ((p * 2 + r) * mine + j) * block
-                        row = r * n_dev + b * block
-                        column = s * half + p * columns
-                        taken[j, row : row + block, column : column + columns] = ordered[
-                            at : at + block
-                        ]
-    for j in range(mine):
-        normed = rms_scale(taken[j].astype(f32), post_gain[...]).astype(bf16)
-        inner = jax.nn.silu(dot(normed, gate[j])) * dot(normed, up[j])
-        result[j] = dot(inner.astype(bf16), down[j]).astype(bf16)
+    @pl.when(side >= 0)
+    def _():
+        for s in range(2):
+            for b in range(n_dev // block):
+                at = (s * n_dev + b * block) * groups
+                ordered = dot(inward, received[at : at + groups * block, :]).astype(bf16)
+                for p in range(parts):
+                    for r in range(2):
+                        for j in range(mine):
+                            at = ((p * 2 + r) * mine + j) * block
+                            row = r * n_dev + b * block
+                            column = s * half + p * columns
+                            taken[j, row : row + block, column : column + columns] = ordered[
+                                at : at + block
+                            ]
+        for j in range(mine):
+            normed = rms_scale(taken[j].astype(f32), post_gain[...]).astype(bf16)
+            inner[j] = (jax.nn.silu(dot(normed, gate[j])) * dot(normed, up[j])).astype(bf16)
+        for j in range(mine - 1):
+            result[j] = dot(inner[j], down[j]).astype(bf16)
+
+    last.wait()
+    result[mine - 1] = dot(inner[mine - 1], last_down[...]).astype(bf16)
 
     copies = []
     for t in range(2):
@@ -438,7 +461,7 @@
             jax.ShapeDtypeStruct((rows, width), bf16),
             jax.ShapeDtypeStruct((mine, width, inner_width), bf16),
             jax.ShapeDtypeStruct((mine, width, inner_width), bf16),
-            jax.ShapeDtypeStruct((mine, inner_width, width), bf16),
+            jax.ShapeDtypeStruct((mine - 1, inner_width, width), bf16),
         ),
         in_specs=[HBM] * (len(sources) + 3),
         out_specs=(VMEM,) * 6,
@@ -447,8 +470,9 @@
             pltpu.VMEM((heads * rows, head), bf16),
             pltpu.VMEM((heads * rows, tokens), bf16),
             pltpu.VMEM((rows * tokens // 256, 256), f32),
+            pltpu.VMEM((heads * rows, 1), f32),
             pltpu.VMEM((slots, half // columns * rows), bf16),
-            pltpu.SemaphoreType.DMA((15,)),
+            pltpu.SemaphoreType.DMA((12,)),
             pltpu.SemaphoreType.DMA((3,)),
         ],
         compiler_params=pltpu.CompilerParams(vmem_limit_bytes=24 * MIB),
@@ -457,16 +481,18 @@
     sent = pl.pallas_call(
         expert_kernel,
         out_shape=jax.ShapeDtypeStruct((slots, columns), bf16),
-        in_specs=[VMEM] * 5,
+        in_specs=[VMEM] * 5 + [HBM],
         out_specs=HBM,
         scratch_shapes=[
+            pltpu.VMEM((inner_width, width), bf16),
             pltpu.VMEM((mine, 2 * n_dev, width), bf16),
+            pltpu.VMEM((mine, 2 * n_dev, inner_width), bf16),
             pltpu.VMEM((mine, 2 * n_dev, width), bf16),
             pltpu.VMEM((slots, columns), bf16),
-            pltpu.SemaphoreType.DMA((2 * n_dev // 32,)),
+            pltpu.SemaphoreType.DMA((2 * n_dev // 32 + 1,)),
         ],
         compiler_params=pltpu.CompilerParams(vmem_limit_bytes=24 * MIB),
-    )(received, post_gain[None, :], gate, up, down)
+    )(received, post_gain[None, :], gate, up, down, in_hbm(down_weight))
     returned = exchange(sent)
     base, spread = pl.pallas_call(
         functools.partial(middle_kernel, n_dev=n_dev, local=local),

time: 61.8 us -> 61.4 us (level)
  no operation moved by 1% of the time
where the time goes in v6:
time: 61.4 us; the launch traced here: 61.1 us
  blocking collectives  29 us (47%)
  Pallas kernels  13.4 us (22%)
  waiting for transfers between devices  13 us (21%)
  starting transfers between devices  5.71 us (9%)
    all_to_all x1, blocking collectives, exchange(): lax.all_to_all(value, ('side', 'dev'), split_axis=0, concat_axis=0, tiled...  29 us
    all_to_all x1, waiting for transfers between devices, exchange(): lax.all_to_all(value, ('side', 'dev'), split_axis=0, concat_axis=0, tiled...  13 us
    all_to_all x1, starting transfers between devices, exchange(): lax.all_to_all(value, ('side', 'dev'), split_axis=0, concat_axis=0, tiled...  5.71 us
    pallas_call x1, Pallas kernels, on_device(): pl.pallas_call(functools.partial(front_kernel, page=page, local=local), o...  4.9 us
    pallas_call x1, Pallas kernels, on_device(): pl.pallas_call(functools.partial(middle_kernel, n_dev=n_dev, local=local)...  4.66 us
    pallas_call x1, Pallas kernels, on_device(): pl.pallas_call(expert_kernel, out_shape=jax.ShapeDtypeStruct((slots, colu...  2.93 us
  transfers between devices with their start and end apart: 1, of which 1 were waited for; matrix products, arithmetic and copies ran while one was open for 0% of the time, Pallas kernels for 8%

profile of v6, /device:TPU:1, one launch (start us, length us, event | category | flops | bytes accessed | tf_op | source)
XLA Modules:
  0.0 61.1 jit_solution(4806500229569736718)
XLA Ops:
  0.0 0.0 copy-start
  0.0 4.9 %shard_map.199 = (bf16[1024,512]{1,0:T(8,128)(2,1)S(1)}, bf16[32,1024]{1,0:T(8,128)(2,1)S(1)}, bf16[32,2048]{1,0:T(8,128)(2,1)S(1)}, bf16[2,2048,256]{2,1,0:T(8,...) custom-call(s32[1,32]{1,0:T(1,128)} %bitcast.26, s32[8,32]{1,0:T(8,128)} %bitcast.23, ...), custom_call_target="tpu_custom_call" | custom-call | tf_op jit(solution)/shard_map/pallas_call | solution.py:456
  4.9 29.0 %all_to_all.22 = bf16[128,8,512]{2,1,0:T(8,128)(2,1)S(1)} all-to-all(bf16[128,8,512]{2,1,0:T(8,128)(2,1)S(1)} %bitcast.15), channel_id=1, replica_groups=mesh['side'=2,'dev'=64] {'side','dev'}, dimensions={0} | all-to-all | bytes 2097152 | tf_op jit(solution)/shard_map/all_to_all | solution.py:401
  33.9 0.0 copy-done
  33.9 2.9 %shard_map.200.refs_11_ = bf16[1024,512]{1,0:T(8,128)(2,1)} custom-call(bf16[1024,512]{1,0:T(8,128)(2,1)S(1)} %bitcast.13, f32[1,2048]{1,0:T(1,128)S(1)} %bitcast.17, bf16[2,2048,256]{2,1,0:T(8,128)(2,1)S(1)} %get-tuple-element.16.gate, bf16[2,2048,256]{2,1,0:T(8,128)(2,1)S(1)} %get-tuple-element.17.up, bf16[1,256,2048]{2,1,0:T(8,128)(2,1)S(1)} %get-tuple-element.18.down, ...), custom_call_target="tpu_custom_call" | custom-call | tf_op jit(solution)/shard_map/pallas_call | solution.py:481
  36.8 5.7 %all-to-all-start.1 = ((bf16[128,8,512]{2,1,0:T(8,128)(2,1)}), bf16[128,8,512]{2,1,0:T(8,128)(2,1)S(1)}, u32[]{:S(2)}, u32[]{:S(2)}) async-start(bf16[128,8,512]{2,1,0:T(8,128)(2,1)} %bitcast.11), calls=%async_computation.1 | async-start | bytes 2097152 | tf_op jit(solution)/shard_map/all_to_all | solution.py:401
  42.5 4.7 %shard_map.201 = (f32[32,1024]{1,0:T(8,128)S(1)}, bf16[128,1024]{1,0:T(8,128)(2,1)S(1)}) custom-call(bf16[32,2048]{1,0:T(8,128)(2,1)S(1)} %get-tuple-element.13.refs_0_, bf16[32,1024]{1,0:T(8,128)(2,1)S(1)} %get-tuple-element.14.refs_1_, s32[10,32]{1,0:T(8,128)} %bitcast.20, f32[10,32]{1,0:T(8,128)} %bitcast.21, bf16[16,128]{1,0:T(8,128)(2,1)} %bitcast.22, ...), custom_call_target="tpu_custom_call" | custom-call | flops 234881024 | bytes 8388608 | tf_op jit(solution)/shard_map/pallas_call | solution.py:497
  47.2 13.0 %all-to-all-done.1 = bf16[128,8,512]{2,1,0:T(8,128)(2,1)S(1)} async-done(((bf16[128,8,512]{2,1,0:T(8,128)(2,1)}), bf16[128,8,512]{2,1,0:T(8,128)(2,1)S(1)}, u32[]{:S(2)}, u32[]{:S(2)}) %all-to-all-start.1) | async-done | bytes 1048608 | tf_op jit(solution)/shard_map/all_to_all | solution.py:401
  60.2 0.9 %shard_map.202 = bf16[32,1024]{1,0:T(8,128)(2,1)} custom-call(bf16[128,1024]{1,0:T(8,128)(2,1)S(1)} %get-tuple-element.19.spread_ref, f32[32,1024]{1,0:T(8,128)S(1)} %get-tuple-element.20.base_ref, bf16[1024,512]{1,0:T(8,128)(2,1)S(1)} %bitcast.14), custom_call_target="tpu_custom_call" | custom-call | tf_op jit(solution)/shard_map/pallas_call | solution.py:543
Async XLA Ops:
  0.0 33.9 %copy-start = (f32[2048]{0:T(1024)S(1)}, f32[2048]{0:T(1024)}, u32[]{:S(2)}) copy-start(f32[2048]{0:T(1024)} %param.32) | copy-start | bytes 24580
  36.8 23.4 %all-to-all-start.1 = ((bf16[128,8,512]{2,1,0:T(8,128)(2,1)}), bf16[128,8,512]{2,1,0:T(8,128)(2,1)S(1)}, u32[]{:S(2)}, u32[]{:S(2)}) async-start(bf16[128,8,512]{2,1,0:T(8,128)(2,1)} %bitcast.11), calls=%async_computation.1 | async-start | bytes 2097152 | tf_op jit(solution)/shard_map/all_to_all | solution.py:401

commit v7 on v6

--- a/solution.py
+++ b/solution.py
@@ -53,11 +53,11 @@
 
 
 def front_kernel(*refs, page, local):
-    sources, expert_sources, refs = refs[:12], refs[12:15], refs[15:]
+    sources, refs = refs[:12], refs[12:]
     packed_ref, hidden_ref, attended = refs[:3]
-    expert_targets, refs = refs[3:6], refs[6:]
+    refs = refs[3:]
     targets, refs = refs[:12], refs[12:]
-    query, prob, valid, own_weight, chosen, sem, expert_sem = refs
+    query, prob, valid, own_weight, chosen, sem = refs
     residual_hbm, pool_hbm, weight_hbm = sources[-3:]
     (
         lengths_ref,
@@ -148,13 +148,6 @@
 
     for copy in copies[7:11]:
         copy.wait()
-    expert_copies = start_all(
-        [
-            (source.at[pl.ds(side * mine, target.shape[0])], target)
-            for source, target in zip(expert_sources, expert_targets)
-        ],
-        expert_sem,
-    )
 
     @pl.when(always)
     def _():
@@ -186,7 +179,7 @@
             gate = jax.nn.sigmoid(gates_ref[:, h * head : (h + 1) * head].astype(f32))
             attended[:, h * head : (h + 1) * head] = (value * gate).astype(bf16)
 
-    copies[11].wait()
+    copies[-1].wait()
 
     @pl.when(always)
     def _():
@@ -197,9 +190,6 @@
             [hidden[:, p * columns : (p + 1) * columns] for p in range(parts)], axis=0
         )
         packed_ref[...] = dot(chosen[...], stacked).astype(bf16)
-
-    for copy in expert_copies:
-        copy.wait()
 
 
 def middle_kernel(*refs, n_dev, local):
@@ -303,21 +293,15 @@
     gate,
     up,
     down,
-    down_hbm,
     sent_hbm,
-    last_down,
     taken,
-    inner,
     result,
     sent,
     sem,
 ):
-    mine, width, inner_width = gate.shape
-    side = lax.axis_index("side")
-    last = pltpu.make_async_copy(
-        down_hbm.at[side * mine + mine - 1], last_down, sem.at[sem.shape[0] - 1]
-    )
-    last.start()
+    local, width, inner_width = gate.shape
+    mine = local // 2
+    first = lax.axis_index("side") * mine
     slots, columns = received.shape
     half = width // 2
     parts = half // columns
@@ -327,29 +311,23 @@
     inward = group_order(groups, block, True)
     outward = group_order(groups, block, False)
 
-    @pl.when(side >= 0)
-    def _():
-        for s in range(2):
-            for b in range(n_dev // block):
-                at = (s * n_dev + b * block) * groups
-                ordered = dot(inward, received[at : at + groups * block, :]).astype(bf16)
-                for p in range(parts):
-                    for r in range(2):
-                        for j in range(mine):
-                            at = ((p * 2 + r) * mine + j) * block
-                            row = r * n_dev + b * block
-                            column = s * half + p * columns
-                            taken[j, row : row + block, column : column + columns] = ordered[
-                                at : at + block
-                            ]
-        for j in range(mine):
-            normed = rms_scale(taken[j].astype(f32), post_gain[...]).astype(bf16)
-            inner[j] = (jax.nn.silu(dot(normed, gate[j])) * dot(normed, up[j])).astype(bf16)
-        for j in range(mine - 1):
-            result[j] = dot(inner[j], down[j]).astype(bf16)
-
-    last.wait()
-    result[mine - 1] = dot(inner[mine - 1], last_down[...]).astype(bf16)
+    for s in range(2):
+        for b in range(n_dev // block):
+            at = (s * n_dev + b * block) * groups
+            ordered = dot(inward, received[at : at + groups * block, :]).astype(bf16)
+            for p in range(parts):
+                for r in range(2):
+                    for j in range(mine):
+                        at = ((p * 2 + r) * mine + j) * block
+                        row = r * n_dev + b * block
+                        column = s * half + p * columns
+                        taken[j, row : row + block, column : column + columns] = ordered[
+                            at : at + block
+                        ]
+    for j in range(mine):
+        normed = rms_scale(taken[j].astype(f32), post_gain[...]).astype(bf16)
+        inner = jax.nn.silu(dot(normed, gate[first + j])) * dot(normed, up[first + j])
+        result[j] = dot(inner.astype(bf16), down[first + j]).astype(bf16)
 
     copies = []
     for t in range(2):
@@ -395,6 +373,10 @@
 
 def in_hbm(value):
     return pltpu.with_memory_space_constraint(value, pltpu.HBM)
+
+
+def in_vmem(value):
+    return pltpu.with_memory_space_constraint(value, pltpu.VMEM)
 
 
 def exchange(value):
@@ -453,18 +435,15 @@
     held = [pltpu.VMEM(source.shape, source.dtype) for source in sources]
     held[9] = pltpu.VMEM((rows, half), bf16)
     held[11] = pltpu.VMEM((width, half), bf16)
-    packed, hidden, attended, gate, up, down = pl.pallas_call(
+    packed, hidden, attended = pl.pallas_call(
         functools.partial(front_kernel, page=page, local=local),
         out_shape=(
             jax.ShapeDtypeStruct((slots, columns), bf16),
             jax.ShapeDtypeStruct((rows, half), bf16),
             jax.ShapeDtypeStruct((rows, width), bf16),
-            jax.ShapeDtypeStruct((mine, width, inner_width), bf16),
-            jax.ShapeDtypeStruct((mine, width, inner_width), bf16),
-            jax.ShapeDtypeStruct((mine - 1, inner_width, width), bf16),
         ),
-        in_specs=[HBM] * (len(sources) + 3),
-        out_specs=(VMEM,) * 6,
+        in_specs=[HBM] * len(sources),
+        out_specs=(VMEM,) * 3,
         scratch_shapes=held
         + [
             pltpu.VMEM((heads * rows, head), bf16),
@@ -473,26 +452,23 @@
             pltpu.VMEM((heads * rows, 1), f32),
             pltpu.VMEM((slots, half // columns * rows), bf16),
             pltpu.SemaphoreType.DMA((12,)),
-            pltpu.SemaphoreType.DMA((3,)),
         ],
         compiler_params=pltpu.CompilerParams(vmem_limit_bytes=24 * MIB),
-    )(*map(in_hbm, sources + (gate_weight, up_weight, down_weight)))
+    )(*map(in_hbm, sources))
     received = exchange(packed)
     sent = pl.pallas_call(
         expert_kernel,
         out_shape=jax.ShapeDtypeStruct((slots, columns), bf16),
-        in_specs=[VMEM] * 5 + [HBM],
+        in_specs=[VMEM] * 5,
         out_specs=HBM,
         scratch_shapes=[
-            pltpu.VMEM((inner_width, width), bf16),
             pltpu.VMEM((mine, 2 * n_dev, width), bf16),
-            pltpu.VMEM((mine, 2 * n_dev, inner_width), bf16),
             pltpu.VMEM((mine, 2 * n_dev, width), bf16),
             pltpu.VMEM((slots, columns), bf16),
-            pltpu.SemaphoreType.DMA((2 * n_dev // 32 + 1,)),
+            pltpu.SemaphoreType.DMA((2 * n_dev // 32,)),
         ],
         compiler_params=pltpu.CompilerParams(vmem_limit_bytes=24 * MIB),
-    )(received, post_gain[None, :], gate, up, down, in_hbm(down_weight))
+    )(received, post_gain[None, :], *map(in_vmem, (gate_weight, up_weight, down_weight)))
     returned = exchange(sent)
     base, spread = pl.pallas_call(
         functools.partial(middle_kernel, n_dev=n_dev, local=local),

time: 61.4 us -> 61 us (level)
  no operation moved by 1% of the time
where the time goes in v7:
time: 61 us; the launch traced here: 60.8 us
  blocking collectives  29 us (48%)
  Pallas kernels  13.1 us (21%)
  waiting for transfers between devices  13 us (21%)
  starting transfers between devices  5.71 us (9%)
    all_to_all x1, blocking collectives, exchange(): lax.all_to_all(value, ('side', 'dev'), split_axis=0, concat_axis=0, tiled...  29 us
    all_to_all x1, waiting for transfers between devices, exchange(): lax.all_to_all(value, ('side', 'dev'), split_axis=0, concat_axis=0, tiled...  13 us
    all_to_all x1, starting transfers between devices, exchange(): lax.all_to_all(value, ('side', 'dev'), split_axis=0, concat_axis=0, tiled...  5.71 us
    pallas_call x1, Pallas kernels, on_device(): pl.pallas_call(functools.partial(middle_kernel, n_dev=n_dev, local=local)...  4.66 us
    pallas_call x1, Pallas kernels, on_device(): pl.pallas_call(functools.partial(front_kernel, page=page, local=local), o...  4.57 us
    pallas_call x1, Pallas kernels, on_device(): pl.pallas_call(expert_kernel, out_shape=jax.ShapeDtypeStruct((slots, colu...  2.92 us
  transfers between devices with their start and end apart: 1, of which 1 were waited for; matrix products, arithmetic and copies ran while one was open for 0% of the time, Pallas kernels for 8%

profile of v7, /device:TPU:1, one launch (start us, length us, event | category | flops | bytes accessed | tf_op | source)
XLA Modules:
  0.0 60.8 jit_solution(10908659681287968496)
XLA Ops:
  0.0 0.0 copy-start
  0.0 0.0 copy-start.1
  0.0 0.0 copy-start.2
  0.0 0.0 copy-start.3
  0.0 4.6 %shard_map.199 = (bf16[1024,512]{1,0:T(8,128)(2,1)S(1)}, bf16[32,1024]{1,0:T(8,128)(2,1)S(1)}, bf16[32,2048]{1,0:T(8,128)(2,1)S(1)}) custom-call(s32[1,32]{1,0:T(1,128)} %bitcast.26, s32[8,32]{1,0:T(8,128)} %bitcast.22, s32[10,32]{1,0:T(8,128)} %bitcast.19, bf16[32,2048]{1,0:T(8,128)(2,1)} %refs_3_.1, f32[1,256]{1,0:T(1,128)} %bitcast.24, ...), custom_call_target="tpu_custom_call" | custom-call | tf_op jit(solution)/shard_map/pallas_call | solution.py:438
  4.6 29.0 %all_to_all.22 = bf16[128,8,512]{2,1,0:T(8,128)(2,1)S(1)} all-to-all(bf16[128,8,512]{2,1,0:T(8,128)(2,1)S(1)} %bitcast.15), channel_id=1, replica_groups=mesh['side'=2,'dev'=64] {'side','dev'}, dimensions={0} | all-to-all | bytes 2097152 | tf_op jit(solution)/shard_map/all_to_all | solution.py:383
  33.6 0.0 copy-done
  33.6 0.0 copy-done.1
  33.6 0.0 copy-done.2
  33.6 0.0 copy-done.3
  33.6 2.9 %shard_map.200.refs_11_ = bf16[1024,512]{1,0:T(8,128)(2,1)} custom-call(bf16[1024,512]{1,0:T(8,128)(2,1)S(1)} %bitcast.13, f32[1,2048]{1,0:T(1,128)S(1)} %bitcast.17, bf16[4,2048,256]{2,1,0:T(8,128)(2,1)S(1)} %copy-done, bf16[4,2048,256]{2,1,0:T(8,128)(2,1)S(1)} %copy-done.1, bf16[4,256,2048]{2,1,0:T(8,128)(2,1)S(1)} %copy-done.2), custom_call_target="tpu_custom_call" | custom-call | tf_op jit(solution)/shard_map/pallas_call | solution.py:459
  36.5 5.7 %all-to-all-start.1 = ((bf16[128,8,512]{2,1,0:T(8,128)(2,1)}), bf16[128,8,512]{2,1,0:T(8,128)(2,1)S(1)}, u32[]{:S(2)}, u32[]{:S(2)}) async-start(bf16[128,8,512]{2,1,0:T(8,128)(2,1)} %bitcast.11), calls=%async_computation.1 | async-start | bytes 2097152 | tf_op jit(solution)/shard_map/all_to_all | solution.py:383
  42.2 4.7 %shard_map.201 = (f32[32,1024]{1,0:T(8,128)S(1)}, bf16[128,1024]{1,0:T(8,128)(2,1)S(1)}) custom-call(bf16[32,2048]{1,0:T(8,128)(2,1)S(1)} %get-tuple-element.10.refs_0_, bf16[32,1024]{1,0:T(8,128)(2,1)S(1)} %get-tuple-element.11.refs_1_, s32[10,32]{1,0:T(8,128)} %bitcast.20, f32[10,32]{1,0:T(8,128)} %bitcast.21, bf16[16,128]{1,0:T(8,128)(2,1)} %bitcast.23, ...), custom_call_target="tpu_custom_call" | custom-call | flops 234881024 | bytes 8388608 | tf_op jit(solution)/shard_map/pallas_call | solution.py:473
  46.9 13.0 %all-to-all-done.1 = bf16[128,8,512]{2,1,0:T(8,128)(2,1)S(1)} async-done(((bf16[128,8,512]{2,1,0:T(8,128)(2,1)}), bf16[128,8,512]{2,1,0:T(8,128)(2,1)S(1)}, u32[]{:S(2)}, u32[]{:S(2)}) %all-to-all-start.1) | async-done | bytes 1048608 | tf_op jit(solution)/shard_map/all_to_all | solution.py:383
  59.9 0.9 %shard_map.202 = bf16[32,1024]{1,0:T(8,128)(2,1)} custom-call(bf16[128,1024]{1,0:T(8,128)(2,1)S(1)} %get-tuple-element.13.spread_ref, f32[32,1024]{1,0:T(8,128)S(1)} %get-tuple-element.14.base_ref, bf16[1024,512]{1,0:T(8,128)(2,1)S(1)} %bitcast.14), custom_call_target="tpu_custom_call" | custom-call | tf_op jit(solution)/shard_map/pallas_call | solution.py:519
Async XLA Ops:
  0.0 33.6 %copy-start = (bf16[4,2048,256]{2,1,0:T(8,128)(2,1)S(1)}, bf16[4,2048,256]{2,1,0:T(8,128)(2,1)}, u32[]{:S(2)}) copy-start(bf16[4,2048,256]{2,1,0:T(8,128)(2,1)} %gate.1) | copy-start | bytes 12582916
  0.0 33.6 %copy-start.1 = (bf16[4,2048,256]{2,1,0:T(8,128)(2,1)S(1)}, bf16[4,2048,256]{2,1,0:T(8,128)(2,1)}, u32[]{:S(2)}) copy-start(bf16[4,2048,256]{2,1,0:T(8,128)(2,1)} %up.1) | copy-start | bytes 12582916
  0.0 33.6 %copy-start.2 = (bf16[4,256,2048]{2,1,0:T(8,128)(2,1)S(1)}, bf16[4,256,2048]{2,1,0:T(8,128)(2,1)}, u32[]{:S(2)}) copy-start(bf16[4,256,2048]{2,1,0:T(8,128)(2,1)} %down.1) | copy-start | bytes 12582916
  0.0 33.6 %copy-start.3 = (f32[2048]{0:T(1024)S(1)}, f32[2048]{0:T(1024)}, u32[]{:S(2)}) copy-start(f32[2048]{0:T(1024)} %param.32) | copy-start | bytes 24580
  36.5 23.4 %all-to-all-start.1 = ((bf16[128,8,512]{2,1,0:T(8,128)(2,1)}), bf16[128,8,512]{2,1,0:T(8,128)(2,1)S(1)}, u32[]{:S(2)}, u32[]{:S(2)}) async-start(bf16[128,8,512]{2,1,0:T(8,128)(2,1)} %bitcast.11), calls=%async_computation.1 | async-start | bytes 2097152 | tf_op jit(solution)/shard_map/all_to_all | solution.py:383

commit v8 on v7

--- a/solution.py
+++ b/solution.py
@@ -57,7 +57,7 @@
     packed_ref, hidden_ref, attended = refs[:3]
     refs = refs[3:]
     targets, refs = refs[:12], refs[12:]
-    query, prob, valid, own_weight, chosen, sem = refs
+    query, prob, valid, own_weight, chosen, total, sem = refs
     residual_hbm, pool_hbm, weight_hbm = sources[-3:]
     (
         lengths_ref,
@@ -89,7 +89,10 @@
     pairs = list(zip(sources, targets))
     copies = start_all(
         pairs[:7]
-        + [pairs[10]]
+        + [
+            (pool_hbm.at[:, pl.ds(i * head, head)], pool.at[:, pl.ds(i * head, head)])
+            for i in range(2)
+        ]
         + pairs[7:9]
         + [
             (residual_hbm.at[:, columns_at], residual_ref),
@@ -146,12 +149,11 @@
             own.append(jnp.sum(normed.astype(f32) * key_normed, axis=-1, keepdims=True))
         own_weight[...] = jnp.exp(jnp.concatenate(own, axis=0) * scale)
 
-    for copy in copies[7:11]:
-        copy.wait()
+    copies[7].wait()
 
     @pl.when(always)
     def _():
-        total = jnp.zeros((heads * rows, context), f32)
+        summed = jnp.zeros((heads * rows, context), f32)
         for c in range(chunks):
             at = slice(c * context, (c + 1) * context)
             scores = lax.dot_general(
@@ -164,14 +166,20 @@
             weights = (jnp.exp(scores).reshape(heads, rows, context) * mask[None]).reshape(
                 heads * rows, context
             )
-            total = total + weights
+            summed = summed + weights
             prob[:, at] = weights.astype(bf16)
-
+        total[...] = summed
+
+    for copy in copies[8:12]:
+        copy.wait()
+
+    @pl.when(always)
+    def _():
         middle = heads * rows // 2
         mixed = jnp.concatenate(
             [dot(prob[:middle], pool[:, head:]), dot(prob[middle:], pool[:, head:])], axis=0
         )
-        inverse = 1.0 / (jnp.sum(total, axis=1, keepdims=True) + own_weight[...])
+        inverse = 1.0 / (jnp.sum(total[...], axis=1, keepdims=True) + own_weight[...])
         new_values = values_ref[...].astype(f32)
         for h in range(heads):
             part = slice(h * rows, (h + 1) * rows)
@@ -451,7 +459,8 @@
             pltpu.VMEM((rows * tokens // 256, 256), f32),
             pltpu.VMEM((heads * rows, 1), f32),
             pltpu.VMEM((slots, half // columns * rows), bf16),
-            pltpu.SemaphoreType.DMA((12,)),
+            pltpu.VMEM((heads * rows, 256), f32),
+            pltpu.SemaphoreType.DMA((13,)),
         ],
         compiler_params=pltpu.CompilerParams(vmem_limit_bytes=24 * MIB),
     )(*map(in_hbm, sources))

time: 61 us -> 61 us (level)
  no operation moved by 1% of the time
where the time goes in v8:
time: 61 us; the launch traced here: 60.8 us
  blocking collectives  29 us (48%)
  Pallas kernels  13.1 us (21%)
  waiting for transfers between devices  13 us (21%)
  starting transfers between devices  5.7 us (9%)
    all_to_all x1, blocking collectives, exchange(): lax.all_to_all(value, ('side', 'dev'), split_axis=0, concat_axis=0, tiled...  29 us
    all_to_all x1, waiting for transfers between devices, exchange(): lax.all_to_all(value, ('side', 'dev'), split_axis=0, concat_axis=0, tiled...  13 us
    all_to_all x1, starting transfers between devices, exchange(): lax.all_to_all(value, ('side', 'dev'), split_axis=0, concat_axis=0, tiled...  5.7 us
    pallas_call x1, Pallas kernels, on_device(): pl.pallas_call(functools.partial(middle_kernel, n_dev=n_dev, local=local)...  4.66 us
    pallas_call x1, Pallas kernels, on_device(): pl.pallas_call(functools.partial(front_kernel, page=page, local=local), o...  4.58 us
    pallas_call x1, Pallas kernels, on_device(): pl.pallas_call(expert_kernel, out_shape=jax.ShapeDtypeStruct((slots, colu...  2.92 us
  transfers between devices with their start and end apart: 1, of which 1 were waited for; matrix products, arithmetic and copies ran while one was open for 0% of the time, Pallas kernels for 8%

profile of v8, /device:TPU:1, one launch (start us, length us, event | category | flops | bytes accessed | tf_op | source)
XLA Modules:
  0.0 60.8 jit_solution(17262323006186570191)
XLA Ops:
  0.0 0.0 copy-start
  0.0 0.0 copy-start.1
  0.0 0.0 copy-start.2
  0.0 0.0 copy-start.3
  0.0 4.6 %shard_map.199 = (bf16[1024,512]{1,0:T(8,128)(2,1)S(1)}, bf16[32,1024]{1,0:T(8,128)(2,1)S(1)}, bf16[32,2048]{1,0:T(8,128)(2,1)S(1)}) custom-call(s32[1,32]{1,0:T(1,128)} %bitcast.26, s32[8,32]{1,0:T(8,128)} %bitcast.22, s32[10,32]{1,0:T(8,128)} %bitcast.19, bf16[32,2048]{1,0:T(8,128)(2,1)} %refs_3_.1, f32[1,256]{1,0:T(1,128)} %bitcast.24, ...), custom_call_target="tpu_custom_call" | custom-call | tf_op jit(solution)/shard_map/pallas_call | solution.py:446
  4.6 29.0 %all_to_all.22 = bf16[128,8,512]{2,1,0:T(8,128)(2,1)S(1)} all-to-all(bf16[128,8,512]{2,1,0:T(8,128)(2,1)S(1)} %bitcast.15), channel_id=1, replica_groups=mesh['side'=2,'dev'=64] {'side','dev'}, dimensions={0} | all-to-all | bytes 2097152 | tf_op jit(solution)/shard_map/all_to_all | solution.py:391
  33.6 0.0 copy-done
  33.6 0.0 copy-done.1
  33.6 0.0 copy-done.2
  33.6 0.0 copy-done.3
  33.6 2.9 %shard_map.200.refs_11_ = bf16[1024,512]{1,0:T(8,128)(2,1)} custom-call(bf16[1024,512]{1,0:T(8,128)(2,1)S(1)} %bitcast.13, f32[1,2048]{1,0:T(1,128)S(1)} %bitcast.17, bf16[4,2048,256]{2,1,0:T(8,128)(2,1)S(1)} %copy-done, bf16[4,2048,256]{2,1,0:T(8,128)(2,1)S(1)} %copy-done.1, bf16[4,256,2048]{2,1,0:T(8,128)(2,1)S(1)} %copy-done.2), custom_call_target="tpu_custom_call" | custom-call | tf_op jit(solution)/shard_map/pallas_call | solution.py:468
  36.5 5.7 %all-to-all-start.1 = ((bf16[128,8,512]{2,1,0:T(8,128)(2,1)}), bf16[128,8,512]{2,1,0:T(8,128)(2,1)S(1)}, u32[]{:S(2)}, u32[]{:S(2)}) async-start(bf16[128,8,512]{2,1,0:T(8,128)(2,1)} %bitcast.11), calls=%async_computation.1 | async-start | bytes 2097152 | tf_op jit(solution)/shard_map/all_to_all | solution.py:391
  42.2 4.7 %shard_map.201 = (f32[32,1024]{1,0:T(8,128)S(1)}, bf16[128,1024]{1,0:T(8,128)(2,1)S(1)}) custom-call(bf16[32,2048]{1,0:T(8,128)(2,1)S(1)} %get-tuple-element.10.refs_0_, bf16[32,1024]{1,0:T(8,128)(2,1)S(1)} %get-tuple-element.11.refs_1_, s32[10,32]{1,0:T(8,128)} %bitcast.20, f32[10,32]{1,0:T(8,128)} %bitcast.21, bf16[16,128]{1,0:T(8,128)(2,1)} %bitcast.23, ...), custom_call_target="tpu_custom_call" | custom-call | flops 234881024 | bytes 8388608 | tf_op jit(solution)/shard_map/pallas_call | solution.py:482
  46.9 13.0 %all-to-all-done.1 = bf16[128,8,512]{2,1,0:T(8,128)(2,1)S(1)} async-done(((bf16[128,8,512]{2,1,0:T(8,128)(2,1)}), bf16[128,8,512]{2,1,0:T(8,128)(2,1)S(1)}, u32[]{:S(2)}, u32[]{:S(2)}) %all-to-all-start.1) | async-done | bytes 1048608 | tf_op jit(solution)/shard_map/all_to_all | solution.py:391
  59.9 1.0 %shard_map.202 = bf16[32,1024]{1,0:T(8,128)(2,1)} custom-call(bf16[128,1024]{1,0:T(8,128)(2,1)S(1)} %get-tuple-element.13.spread_ref, f32[32,1024]{1,0:T(8,128)S(1)} %get-tuple-element.14.base_ref, bf16[1024,512]{1,0:T(8,128)(2,1)S(1)} %bitcast.14), custom_call_target="tpu_custom_call" | custom-call | tf_op jit(solution)/shard_map/pallas_call | solution.py:528
Async XLA Ops:
  0.0 33.6 %copy-start = (bf16[4,2048,256]{2,1,0:T(8,128)(2,1)S(1)}, bf16[4,2048,256]{2,1,0:T(8,128)(2,1)}, u32[]{:S(2)}) copy-start(bf16[4,2048,256]{2,1,0:T(8,128)(2,1)} %gate.1) | copy-start | bytes 12582916
  0.0 33.6 %copy-start.1 = (bf16[4,2048,256]{2,1,0:T(8,128)(2,1)S(1)}, bf16[4,2048,256]{2,1,0:T(8,128)(2,1)}, u32[]{:S(2)}) copy-start(bf16[4,2048,256]{2,1,0:T(8,128)(2,1)} %up.1) | copy-start | bytes 12582916
  0.0 33.6 %copy-start.2 = (bf16[4,256,2048]{2,1,0:T(8,128)(2,1)S(1)}, bf16[4,256,2048]{2,1,0:T(8,128)(2,1)}, u32[]{:S(2)}) copy-start(bf16[4,256,2048]{2,1,0:T(8,128)(2,1)} %down.1) | copy-start | bytes 12582916
  0.0 33.6 %copy-start.3 = (f32[2048]{0:T(1024)S(1)}, f32[2048]{0:T(1024)}, u32[]{:S(2)}) copy-start(f32[2048]{0:T(1024)} %param.32) | copy-start | bytes 24580
  36.5 23.4 %all-to-all-start.1 = ((bf16[128,8,512]{2,1,0:T(8,128)(2,1)}), bf16[128,8,512]{2,1,0:T(8,128)(2,1)S(1)}, u32[]{:S(2)}, u32[]{:S(2)}) async-start(bf16[128,8,512]{2,1,0:T(8,128)(2,1)} %bitcast.11), calls=%async_computation.1 | async-start | bytes 2097152 | tf_op jit(solution)/shard_map/all_to_all | solution.py:391
